TPU v7x, 512 devices: a whole 4x8x8 slice. The times are simulated.
512 devices in a mesh: outer: 4 (over x), dp: 128 (over z, y, core).
Axes of the slice: x: 4, y: 8, z: 8, core: 2. Of those that a mesh axis runs over, the one named last changes fastest.
Arguments:
- feats: bfloat16 [65536, 3072], P(('outer', 'dp')), may hold values from -24 to 24
- ln_gain: float32 [2048], replicated, may hold values from 0.5 to 1.5
- ln_bias: float32 [2048], replicated, may hold values from -3 to 3
- head_weight: bfloat16 [2048, 512], P('dp'), may hold values from -0.125 to 0.125
- captions: bfloat16 [262144, 512], P(('outer', 'dp'))
- image_cluster: int32 [65536], P(('outer', 'dp')), may hold values from 0 to 511, as said below
- image_target: int32 [65536], P(('outer', 'dp')), may hold values from 0 to 127, as said below
- cluster_owner: int32 [4, 512], P('outer'), may hold values from 0 to 127, as said below
- cluster_size: int32 [4, 512], P('outer'), may hold values from 1 to 128, as said below
- cap_index: int32 [4, 512, 128], P('outer'), may hold values from 0 to 511, as said below
- cotangent: float32 [65536], P(('outer', 'dp')), may hold values from -8 to 8
Outputs:
- feat_grad: bfloat16 [65536, 3072], P(('outer', 'dp'))
- weight_grad: float32 [2048, 512], P('dp')
- gain_grad: float32 [2048], replicated
- bias_grad: float32 [2048], replicated
Inputs may be any that keep to these rules, and one draw needn't show every extreme that they name: `cluster_owner`: each dp index of a replica owns exactly 4 of its clusters. `cluster_size`: every replica has a cluster of 128 captions. `cap_index`: the first cluster_size entries of a cluster's row are distinct; the entries after them are not read. `image_cluster`: the images of one device belong to clusters of at most 2 images per owner; in each replica one owner receives exactly 2 images from every device. `image_target`: less than the size of the image's cluster.
All inputs are finite; a program needn't handle non-finite values.
Results may differ from a plain program's by a relative error of at most 0.012.
The roundings to bfloat16 on the way count: a program that leaves them out, or rounds other values in their place, can miss the bound.
Values may be sent and summed in bfloat16 or wider, within the bound.
No kernel may reach another device: no remote copies, remote signals or barrier semaphores. Data moves between devices by JAX's collectives and lax.ppermute only.
A program may use at most 64 MiB of HBM per device.

v0:
```python
import jax
import jax.numpy as jnp
from jax import lax
from jax.sharding import PartitionSpec as P

logit_scale = 100.0


def owner_work(embedded, labels, captions, size_table, index_table):
    sources, slots, width = embedded.shape
    row_count = sources * slots
    flattened = embedded.reshape(row_count, width)
    label_rows = labels.reshape(row_count, 2)
    cluster_ids = label_rows[:, 0]
    filled = cluster_ids >= 0
    safe_ids = jnp.where(filled, cluster_ids, 0)
    matches = safe_ids[:, None] == jnp.arange(size_table.shape[0], dtype=jnp.int32)[None, :]
    lengths = jnp.sum(jnp.where(matches, size_table[None, :], 0), axis=1)
    selected = index_table[safe_ids]
    every_score = logit_scale * lax.dot_general(
        flattened, captions, (((1,), (1,)), ((), ())), preferred_element_type=jnp.float32
    )
    scores = jnp.take_along_axis(every_score, selected, axis=1)
    columns = jnp.arange(selected.shape[1], dtype=jnp.int32)[None, :]
    valid = (columns < lengths[:, None]) & filled[:, None]
    highest = jnp.max(jnp.where(valid, scores, -jnp.inf), axis=1, keepdims=True)
    highest = jnp.where(filled[:, None], highest, 0.0)
    weights = jnp.where(valid, jnp.exp(scores - highest), 0.0)
    totals = jnp.where(filled[:, None], jnp.sum(weights, axis=1, keepdims=True), 1.0)
    probs = weights / totals
    positive = (columns == label_rows[:, 1:2]).astype(jnp.float32)
    coefficients = (logit_scale * (probs - positive)).astype(jnp.bfloat16)
    placed = (
        jnp.zeros((row_count, captions.shape[0]), jnp.bfloat16)
        .at[jnp.arange(row_count)[:, None], selected]
        .set(coefficients)
    )
    gradient = jnp.dot(placed, captions, preferred_element_type=jnp.float32).astype(jnp.bfloat16)
    return gradient.reshape(sources, slots, width)


def send_back(gradient):
    return lax.all_to_all(gradient, "dp", split_axis=0, concat_axis=0, tiled=True)


def body(
    feats,
    ln_gain,
    ln_bias,
    head_weight,
    captions,
    image_cluster,
    image_target,
    cluster_owner,
    cluster_size,
    cap_index,
    cotangent,
):
    count, width = feats.shape
    window_width = ln_gain.shape[0]
    widened = feats.astype(jnp.float32)
    means = jnp.mean(widened, axis=1, keepdims=True)
    centred = widened - means
    inv_std = lax.rsqrt(jnp.mean(centred * centred, axis=1, keepdims=True) + 1e-05)
    normed_head = centred[:, :window_width] * inv_std
    normed_tail = centred[:, window_width:] * inv_std
    window_bf = (normed_head * ln_gain + ln_bias).astype(jnp.bfloat16)
    full_weight = lax.all_gather(head_weight, "dp", axis=0, tiled=True)
    projected = jnp.dot(window_bf, full_weight, preferred_element_type=jnp.float32)
    norm_len = jnp.sqrt(jnp.sum(projected * projected, axis=1, keepdims=True) + 1e-06)
    unit = projected / norm_len
    unit_bf = unit.astype(jnp.bfloat16)
    embed_width = unit_bf.shape[1]
    dp_count = lax.axis_size("dp")
    capacity = max(2, (2 * count + dp_count - 1) // dp_count)
    owner_table = cluster_owner[0]
    size_table = cluster_size[0]
    index_table = cap_index[0]
    matches = image_cluster[:, None] == jnp.arange(owner_table.shape[0], dtype=jnp.int32)[None, :]
    owners = jnp.sum(jnp.where(matches, owner_table[None, :], 0), axis=1)
    to_owner = (owners[:, None] == jnp.arange(dp_count, dtype=jnp.int32)[None, :]).astype(jnp.int32)
    earlier = jnp.cumsum(to_owner, axis=0) - to_owner
    ranks = jnp.sum(earlier * to_owner, axis=1)
    slot_ids = owners * capacity + ranks
    send_rows = (
        jnp.zeros((dp_count * capacity, embed_width), jnp.bfloat16).at[slot_ids].set(unit_bf)
    )
    send_rows = send_rows.reshape(dp_count, capacity, embed_width)
    label_pairs = jnp.stack([image_cluster, image_target], axis=1)
    send_labels = jnp.full((dp_count * capacity, 2), -1, jnp.int32).at[slot_ids].set(label_pairs)
    send_labels = send_labels.reshape(dp_count, capacity, 2)
    received = (
        lax.all_to_all(send_rows, "dp", split_axis=0, concat_axis=0, tiled=True),
        lax.all_to_all(send_labels, "dp", split_axis=0, concat_axis=0, tiled=True),
    )
    returned = send_back(owner_work(received[0], received[1], captions, size_table, index_table))
    unit_grad0 = returned.reshape(dp_count * capacity, embed_width)[slot_ids].astype(jnp.float32)
    unit_grad = cotangent[:, None] * unit_grad0
    proj_grad = (unit_grad - unit * jnp.sum(unit * unit_grad, axis=1, keepdims=True)) / norm_len
    proj_bf = proj_grad.astype(jnp.bfloat16)
    term = lax.dot_general(
        window_bf, proj_bf, (((0,), (0,)), ((), ())), preferred_element_type=jnp.float32
    )
    row_share = lax.psum_scatter(term, "dp", scatter_dimension=0, tiled=True)
    weight_grad = lax.psum(row_share, "outer")
    window_grad = lax.dot_general(
        proj_bf, full_weight, (((1,), (1,)), ((), ())), preferred_element_type=jnp.float32
    )
    gain_local = jnp.sum(window_grad * normed_head, axis=0)
    bias_local = jnp.sum(window_grad, axis=0)
    gain_grad, bias_grad = lax.psum((gain_local, bias_local), ("outer", "dp"))
    scaled_grad = window_grad * ln_gain
    first_mean = jnp.sum(scaled_grad, axis=1, keepdims=True) / width
    second_mean = jnp.sum(scaled_grad * normed_head, axis=1, keepdims=True) / width
    grad_head = inv_std * (scaled_grad - first_mean - normed_head * second_mean)
    grad_tail = inv_std * (0.0 - first_mean - normed_tail * second_mean)
    feat_grad = jnp.concatenate(
        [grad_head.astype(jnp.bfloat16), grad_tail.astype(jnp.bfloat16)], axis=1
    )
    return (feat_grad, weight_grad, gain_grad, bias_grad)


def solution(mesh):
    in_specs = (
        P(("outer", "dp"), None),
        P(),
        P(),
        P("dp", None),
        P(("outer", "dp"), None),
        P(("outer", "dp")),
        P(("outer", "dp")),
        P("outer", None),
        P("outer", None),
        P("outer", None, None),
        P(("outer", "dp")),
    )
    out_specs = (P(("outer", "dp"), None), P("dp", None), P(), P())
    return jax.shard_map(body, mesh=mesh, in_specs=in_specs, out_specs=out_specs, check_vma=False)
```

profile of v0, /device:TPU:1, one launch (start us, length us, event | category | flops | bytes accessed | tf_op | source)
XLA Modules:
  0.0 850.0 jit_solution(12763450232729559890)
XLA Ops:
  7.2 0.7 all-gather.2.cloned.1.call-update
  7.9 0.7 pad_add_fusion.1
  8.6 0.1 copy.22
  8.7 0.9 select_reduce_fusion.1
  9.7 0.2 reduce_window_sum.11
  9.9 0.2 select_reduce_fusion.3
  10.1 0.9 scatter_custom_fusion
  11.0 1.5 copy.23
  12.5 18.4 %all-to-all-start = ((s32[128,2,2]{1,2,0:T(2,128)}), s32[128,2,2]{1,2,0:T(2,128)S(1)}, u32[]{:S(2)}, u32[]{:S(2)}) async-start(s32[128,2,2]{1,2,0:T(2,128)} %copy.23), calls=%async_computation | async-start | bytes 262144 | tf_op jit(solution)/shard_map/all_to_all | solution.py:94
  30.9 1.3 convert_reduce_fusion
  32.3 0.4 multiply_reduce_fusion
  32.7 11.0 %all-to-all-done = s32[128,2,2]{1,2,0:T(2,128)S(1)} async-done(((s32[128,2,2]{1,2,0:T(2,128)}), s32[128,2,2]{1,2,0:T(2,128)S(1)}, u32[]{:S(2)}, u32[]{:S(2)}) %all-to-all-start) | async-done | bytes 2080 | tf_op jit(solution)/shard_map/all_to_all | solution.py:94
  43.7 0.1 reshape.116
  43.9 0.6 compare_select_fusion.2
  44.4 0.7 gather_fusion
  45.2 0.6 fusion.16
  45.9 0.1 and_reduce_fusion
  46.1 0.8 select_reduce_fusion
  46.8 53.3 %all-gather.2.cloned.1.call-done = bf16[2048,512]{1,0:T(8,128)(2,1)} async-done(((bf16[16,512]{1,0:T(8,128)(2,1)}), bf16[2048,512]{1,0:T(8,128)(2,1)}) %all-gather.2.cloned.1.call-update) | async-done | bytes 2097168 | tf_op jit(solution)/shard_map/all_gather | solution.py:68
  100.1 2.2 multiply_reduce_fusion.6
  102.3 1.2 scatter_custom_fusion.1
  103.5 0.8 reshape.117
  104.3 9.5 %all-to-all-start.1 = ((bf16[128,2,512]{2,1,0:T(2,128)(2,1)}), bf16[128,2,512]{2,1,0:T(2,128)(2,1)S(1)}, u32[]{:S(2)}, u32[]{:S(2)}) async-start(bf16[128,2,512]{2,1,0:T(2,128)(2,1)} %reshape.117), calls=%async_computation.1 | async-start | bytes 524288 | tf_op jit(solution)/shard_map/all_to_all | solution.py:93
  113.8 0.7 select_bitcast_fusion
  114.5 14.6 %all-to-all-done.1 = bf16[128,2,512]{2,1,0:T(2,128)(2,1)S(1)} async-done(((bf16[128,2,512]{2,1,0:T(2,128)(2,1)}), bf16[128,2,512]{2,1,0:T(2,128)(2,1)S(1)}, u32[]{:S(2)}, u32[]{:S(2)}) %all-to-all-start.1) | async-done | bytes 262176 | tf_op jit(solution)/shard_map/all_to_all | solution.py:93
  129.1 0.1 reshape.118
  129.2 0.3 convolution_multiply_fusion
  129.6 258.4 %gather_fusion.2 = f32[32768]{0:T(1024)S(1)} fusion(f32[256,512]{1,0:T(8,128)S(1)} %convolution_multiply_fusion, s32[32768]{0:T(1024)S(1)} %get-tuple-element.14), kind=kCustom, calls=%fused_computation.2 | custom fusion | bytes 524288 | tf_op jit(solution)/shard_map/jit(take_along_axis)/gather | solution.py:23
  388.0 0.2 select_reduce_fusion.2
  388.3 0.2 fusion.10
  388.6 0.2 fusion.14
  388.8 224.7 %scatter_custom_fusion.2 = bf16[131072]{0:T(1024)(128)(2,1)S(1)} fusion(s32[32768]{0:T(1024)} %select_bitcast_fusion, bf16[32768]{0:T(1024)(128)(2,1)S(1)} %fusion.14, bf16[]{:T(256)} %constant.18.clone.1), kind=kCustom, calls=%fused_computation.38 | custom fusion | bytes 262656
  613.5 0.2 reshape.124
  613.7 0.3 convolution_convert_fusion
  614.0 0.8 reshape.119
  614.8 5.5 all-to-all-start.2
  620.4 15.3 %all-to-all-done.2 = bf16[128,2,512]{2,1,0:T(2,128)(2,1)S(1)} async-done(((bf16[128,2,512]{2,1,0:T(2,128)(2,1)}), bf16[128,2,512]{2,1,0:T(2,128)(2,1)S(1)}, u32[]{:S(2)}, u32[]{:S(2)}) %all-to-all-start.2) | async-done | bytes 262176 | tf_op jit(solution)/shard_map/all_to_all | solution.py:43
  635.8 0.8 gather_fusion.1
  636.7 0.2 multiply_reduce_fusion.5
  636.9 2.8 fusion.17
  639.7 3.2 multiply_reduce_fusion.1
  642.9 95.6 %all-reduce = (f32[2048]{0:T(1024)}, f32[2048]{0:T(1024)}) all-reduce(f32[2048]{0:T(1024)S(1)} %get-tuple-element.4, f32[2048]{0:T(1024)} %get-tuple-element.7), channel_id=1, replica_groups=mesh['outer'=4,'dp'=128] {'outer','dp'}, use_global_device_ids=true, to_apply=%region_18.19 | all-reduce | flops 4096 | bytes 32768 | tf_op jit(solution)/shard_map/psum | solution.py:111
  738.5 0.7 broadcast_multiply_fusion.1
  739.2 0.8 fusion.3
  740.0 0.9 multiply_convert_fusion
  741.0 0.9 pad_maximum_fusion
  741.9 86.8 %reduce-scatter.2.cloned.1.call-done = f32[16,512]{1,0:T(8,128)} async-done(((f32[2048,512]{1,0:T(8,128)}), f32[16,512]{1,0:T(8,128)}) %reduce-scatter.2.cloned.1.call-update) | async-done | bytes 32784 | tf_op jit(solution)/shard_map/reduce_scatter | solution.py:104
  828.7 14.4 %psum.21 = f32[16,512]{1,0:T(8,128)} all-reduce(f32[16,512]{1,0:T(8,128)} %reduce-scatter.2.cloned.1.call-done), channel_id=1, replica_groups=mesh['outer'=4,'dp'=128] {'outer'}, use_global_device_ids=true, to_apply=%region_16.17 | all-reduce | flops 8192 | bytes 65536 | tf_op jit(solution)/shard_map/psum | solution.py:105
  (59 shorter events, 0.6 us)
Async XLA Ops:
  7.2 122.0 %copy-start = (bf16[512,512]{1,0:T(8,128)(2,1)S(1)}, bf16[512,512]{1,0:T(8,128)(2,1)}, u32[]{:S(2)}) copy-start(bf16[512,512]{1,0:T(8,128)(2,1)} %param.15) | copy-start | bytes 1572868
  7.2 25.1 %copy-start.2 = (bf16[128,3072]{1,0:T(8,128)(2,1)S(1)}, bf16[128,3072]{1,0:T(8,128)(2,1)}, u32[]{:S(2)}) copy-start(bf16[128,3072]{1,0:T(8,128)(2,1)} %param.11) | copy-start | bytes 2359300
  7.2 92.9 %all-gather.2.cloned.1.call-start = ((), (), s32[]{:S(2)}) async-start(), calls=%async_computation.4 | async-start | bytes 2113536 | tf_op jit(solution)/shard_map/all_gather | solution.py:68
  10.0 92.2 %copy-start.19 = (s32[128]{0:T(128)}, s32[128]{0:T(128)S(1)}, u32[]{:S(2)}) copy-start(s32[128]{0:T(128)S(1)} %fusion.15) | copy-start | bytes 1540
  10.1 34.4 %copy-start.1 = (s32[1,512,128]{2,1,0:T(8,128)S(1)}, s32[1,512,128]{2,1,0:T(8,128)}, u32[]{:S(2)}) copy-start(s32[1,512,128]{2,1,0:T(8,128)} %param.20) | copy-start | bytes 786436
  12.5 31.2 %all-to-all-start = ((s32[128,2,2]{1,2,0:T(2,128)}), s32[128,2,2]{1,2,0:T(2,128)S(1)}, u32[]{:S(2)}, u32[]{:S(2)}) async-start(s32[128,2,2]{1,2,0:T(2,128)} %copy.23), calls=%async_computation | async-start | bytes 262144 | tf_op jit(solution)/shard_map/all_to_all | solution.py:94
  32.3 13.5 %copy-start.18 = (s32[2]{0:T(128)S(1)}, s32[2]{0:T(128)}, u32[]{:S(2)}) copy-start(s32[2]{0:T(128)} %constant.65) | copy-start | bytes 28
  32.3 13.6 %copy-start.17 = (s32[2]{0:T(128)S(1)}, s32[2]{0:T(128)}, u32[]{:S(2)}) copy-start(s32[2]{0:T(128)} %constant.68) | copy-start | bytes 28
  32.3 13.8 %copy-start.16 = (s32[1,512]{1,0:T(1,128)S(1)}, s32[1,512]{1,0:T(1,128)}, u32[]{:S(2)}) copy-start(s32[1,512]{1,0:T(1,128)} %param.19) | copy-start | bytes 6148
  32.3 67.8 %copy-start.3 = (f32[2048]{0:T(1024)S(1)}, f32[2048]{0:T(1024)}, u32[]{:S(2)}) copy-start(f32[2048]{0:T(1024)} %param.12) | copy-start | bytes 24580
  32.3 67.8 %copy-start.4 = (f32[2048]{0:T(1024)S(1)}, f32[2048]{0:T(1024)}, u32[]{:S(2)}) copy-start(f32[2048]{0:T(1024)} %param.13) | copy-start | bytes 24580
  32.7 69.6 %copy-start.8 = (f32[128]{0:T(128)}, f32[128]{0:T(128)S(1)}, u32[]{:S(2)}) copy-start(f32[128]{0:T(128)S(1)} %add_rsqrt_fusion) | copy-start | bytes 1540
  43.9 1.9 copy-start.5
  102.3 26.8 %copy-start.11 = (f32[128]{0:T(128)}, f32[128]{0:T(128)S(1)}, u32[]{:S(2)}) copy-start(f32[128]{0:T(128)S(1)} %add_sqrt_fusion) | copy-start | bytes 1540
  104.3 24.8 %all-to-all-start.1 = ((bf16[128,2,512]{2,1,0:T(2,128)(2,1)}), bf16[128,2,512]{2,1,0:T(2,128)(2,1)S(1)}, u32[]{:S(2)}, u32[]{:S(2)}) async-start(bf16[128,2,512]{2,1,0:T(2,128)(2,1)} %reshape.117), calls=%async_computation.1 | async-start | bytes 524288 | tf_op jit(solution)/shard_map/all_to_all | solution.py:93
  129.5 258.5 %copy-start.7 = (s32[256]{0:T(256)S(1)}, s32[256]{0:T(256)}, u32[]{:S(2)}) copy-start(s32[256]{0:T(256)} %select_reduce_fusion) | copy-start | bytes 3076
  129.6 258.5 %copy-start.10 = (pred[256]{0:T(512)(128)(4,1)S(1)}, pred[256]{0:T(512)(128)(4,1)}, u32[]{:S(2)}) copy-start(pred[256]{0:T(512)(128)(4,1)} %fusion.16) | copy-start | bytes 772
  129.6 258.7 %copy-start.6 = (s32[256,2]{0,1:T(2,128)S(1)}, s32[256,2]{0,1:T(2,128)}, u32[]{:S(2)}) copy-start(s32[256,2]{0,1:T(2,128)} %copy-done.5) | copy-start | bytes 6148
  129.6 259.0 %copy-start.13 = (s32[256,1]{0,1:T(1,128)S(1)}, s32[256,1]{0,1:T(1,128)}, u32[]{:S(2)}) copy-start(s32[256,1]{0,1:T(1,128)} %get-tuple-element.16) | copy-start | bytes 3076
  388.0 232.4 %copy-start.20 = (s32[128]{0:T(128)S(1)}, s32[128]{0:T(128)}, u32[]{:S(2)}) copy-start(s32[128]{0:T(128)} %copy-done.19) | copy-start | bytes 1540
  613.5 23.2 %copy-start.12 = (f32[128]{0:T(128)S(1)}, f32[128]{0:T(128)}, u32[]{:S(2)}) copy-start(f32[128]{0:T(128)} %copy-done.11) | copy-start | bytes 1540
  613.5 23.2 %copy-start.14 = (f32[128]{0:T(128)S(1)}, f32[128]{0:T(128)}, u32[]{:S(2)}) copy-start(f32[128]{0:T(128)} %param.21) | copy-start | bytes 1540
  613.7 23.2 %copy-start.9 = (f32[128]{0:T(128)S(1)}, f32[128]{0:T(128)}, u32[]{:S(2)}) copy-start(f32[128]{0:T(128)} %copy-done.8) | copy-start | bytes 1540
  614.8 20.9 %all-to-all-start.2 = ((bf16[128,2,512]{2,1,0:T(2,128)(2,1)}), bf16[128,2,512]{2,1,0:T(2,128)(2,1)S(1)}, u32[]{:S(2)}, u32[]{:S(2)}) async-start(bf16[128,2,512]{2,1,0:T(2,128)(2,1)} %reshape.119), calls=%async_computation.2 | async-start | bytes 524288 | tf_op jit(solution)/shard_map/all_to_all | solution.py:43
  620.3 208.4 %reduce-scatter.2.cloned.1.call-start = ((), (), s32[]{:S(2)}) async-start(), calls=%async_computation.5 | async-start | bytes 4227072 | tf_op jit(solution)/shard_map/reduce_scatter | solution.py:104
  636.9 2.8 copy-start.15
Sparse Core Ops, SparseCore 0:
  11.2 88.8 all-gather.1
  639.8 188.8 reduce-scatter.1
where the time goes:
time: 858 us; the launch traced here: 850 us
  local copies, waits for them, and re-layouts  489 us (57%)
  waiting for transfers between devices  182 us (21%)
  blocking collectives  110 us (13%)
  starting transfers between devices  33.6 us (4%)
  between operations  14.5 us (2%)
  other arithmetic  12 us (1%)
  matrix products  8.75 us (1%)
    gather x1, local copies, waits for them, and re-layouts, owner_work(): scores = jnp.take_along_axis(every_score, selected, axis=1)  258 us
    unnamed x43, local copies, waits for them, and re-layouts  225 us
    psum x1, blocking collectives, body(): gain_grad, bias_grad = lax.psum((gain_local, bias_local), ('outer', 'dp'))  95.6 us
    reduce_scatter x1, waiting for transfers between devices, body(): row_share = lax.psum_scatter(term, 'dp', scatter_dimension=0, tiled=True)  86.8 us
    all_gather x1, waiting for transfers between devices, body(): full_weight = lax.all_gather(head_weight, 'dp', axis=0, tiled=True)  53.3 us
    all_to_all x1, starting transfers between devices, body(): lax.all_to_all(send_labels, 'dp', split_axis=0, concat_axis=0, tiled=True)  18.4 us
  transfers between devices with their start and end apart: 5, of which 5 were waited for; matrix products, arithmetic and copies ran while one was open for 2% of the time, Pallas kernels for 0%

commit v1 on v0

v1 whole, which is shorter than its diff:
```python
import jax
import jax.numpy as jnp
from jax import lax
from jax.sharding import Mesh, PartitionSpec as P

logit_scale = 100.0
bf16 = jnp.bfloat16
f32 = jnp.float32
DP = ("z", "y", "core")
ALL = ("outer", "z", "y", "core")


def split_sum(value):
    high = lax.reduce_precision(value, 8, 7)
    return jnp.concatenate([high.astype(bf16), (value - high).astype(bf16)], axis=0)


def swap(value, axis, flip):
    size = lax.axis_size(axis)
    return lax.ppermute(value, axis, [(i, i ^ flip) for i in range(size)])


def owner_tables(captions, owner_table, size_table, index_table, me):
    count = owner_table.shape[0]
    kmax = index_table.shape[1]
    held = 4
    mine = (owner_table == me).astype(jnp.int32)
    ids = jnp.arange(count, dtype=jnp.int32)
    before = jnp.sum(jnp.where(ids[None, :] < ids[:, None], mine[None, :], 0), axis=1)
    chosen = (mine[None, :] > 0) & (before[None, :] == jnp.arange(held, dtype=jnp.int32)[:, None])
    picked = jnp.sum(jnp.where(chosen, ids[None, :], 0), axis=1)
    lengths = jnp.sum(jnp.where(chosen, size_table[None, :], 0), axis=1)
    rows = index_table.at[picked].get(mode="promise_in_bounds")
    used = (jnp.arange(kmax, dtype=jnp.int32)[None, :] < lengths[:, None]).reshape(1, held * kmax)
    place = rows.reshape(held * kmax, 1) == jnp.arange(captions.shape[0], dtype=jnp.int32)[None, :]
    ordered = jnp.dot(place.astype(bf16), captions, preferred_element_type=f32).astype(bf16)
    return ordered, used


def owner_work(rows, ordered, used, kmax):
    width = ordered.shape[1]
    embedded = rows[:, :width]
    local = rows[:, width : width + 1].astype(f32)
    target = rows[:, width + 1 : width + 2].astype(f32)
    columns = jnp.arange(ordered.shape[0], dtype=jnp.int32)[None, :]
    cluster_of = (columns // kmax).astype(f32)
    scores = logit_scale * lax.dot_general(
        embedded, ordered, (((1,), (1,)), ((), ())), preferred_element_type=f32
    )
    valid = used & (cluster_of == local)
    highest = jnp.max(jnp.where(valid, scores, -jnp.inf), axis=1, keepdims=True)
    weights = jnp.where(valid, jnp.exp(scores - highest), 0.0)
    probs = weights / jnp.sum(weights, axis=1, keepdims=True)
    positive = (columns.astype(f32) == local * kmax + target).astype(f32)
    coefficients = (logit_scale * (probs - positive)).astype(bf16)
    return jnp.dot(coefficients, ordered, preferred_element_type=f32).astype(bf16)


def body(
    feats,
    ln_gain,
    ln_bias,
    head_weight,
    captions,
    image_cluster,
    image_target,
    cluster_owner,
    cluster_size,
    cap_index,
    cotangent,
):
    count, width = feats.shape
    window_width = ln_gain.shape[0]
    embed_width = head_weight.shape[1]
    shard = head_weight.shape[0]
    nz, ny, nc = lax.axis_size("z"), lax.axis_size("y"), lax.axis_size("core")
    dp_count = nz * ny * nc
    half = window_width // nc
    core = lax.axis_index("core")
    me = lax.axis_index(DP)
    capacity = 2
    kmax = cap_index.shape[2]
    owner_table = cluster_owner[0]

    weight_z = lax.all_gather(head_weight, "z", axis=0, tiled=True)
    weight_own = lax.all_gather(weight_z, "y", axis=0, tiled=True)
    weight_other = swap(weight_own, "core", 1)

    widened = feats.astype(f32)
    means = jnp.mean(widened, axis=1, keepdims=True)
    centred = widened - means
    inv_std = lax.rsqrt(jnp.mean(centred * centred, axis=1, keepdims=True) + 1e-05)
    normed_head = centred[:, :window_width] * inv_std
    normed_tail = centred[:, window_width:] * inv_std
    window_bf = (normed_head * ln_gain + ln_bias).astype(bf16)
    by_feature = (
        window_bf.T.reshape(nz, ny, nc, shard, count).transpose(2, 1, 0, 3, 4).reshape(nc, half, count)
    )
    window_own = lax.dynamic_index_in_dim(by_feature, core, 0, keepdims=False)
    window_other = lax.dynamic_index_in_dim(by_feature, 1 - core, 0, keepdims=False)

    ids = jnp.arange(owner_table.shape[0], dtype=jnp.int32)[None, :]
    owners = jnp.sum(jnp.where(image_cluster[:, None] == ids, owner_table[None, :], 0), axis=1)
    local = jnp.sum(
        ((owner_table[None, :] == owners[:, None]) & (ids < image_cluster[:, None])).astype(jnp.int32), axis=1
    )
    images = jnp.arange(count, dtype=jnp.int32)
    ranks = jnp.sum(
        ((owners[:, None] == owners[None, :]) & (images[None, :] < images[:, None])).astype(jnp.int32), axis=1
    )
    slots = owners * capacity + ranks
    place = (jnp.arange(dp_count * capacity, dtype=jnp.int32)[:, None] == slots[None, :]).astype(bf16)
    labels = jnp.stack([local, image_target], axis=1).astype(bf16)
    labels = jnp.concatenate([labels, jnp.zeros((count, 126), bf16)], axis=1)
    ordered, used = owner_tables(captions, owner_table, cluster_size[0], cap_index[0], me)

    def by_rows(left, right):
        return lax.dot_general(left, right, (((0,), (0,)), ((), ())), preferred_element_type=f32)

    projected = by_rows(window_own, weight_own) + by_rows(window_other, weight_other)
    norm_len = jnp.sqrt(jnp.sum(projected * projected, axis=1, keepdims=True) + 1e-06)
    unit = projected / norm_len
    payload = jnp.concatenate([unit.astype(bf16), labels], axis=1)
    send_rows = jnp.dot(place, payload, preferred_element_type=f32).astype(bf16)
    received = lax.all_to_all(
        send_rows.reshape(dp_count, capacity, -1), DP, split_axis=0, concat_axis=0, tiled=True
    )
    gradient = owner_work(received.reshape(dp_count * capacity, -1), ordered, used, kmax)
    returned = lax.all_to_all(
        gradient.reshape(dp_count, capacity, embed_width), DP, split_axis=0, concat_axis=0, tiled=True
    )
    unit_grad0 = by_rows(place, returned.reshape(dp_count * capacity, embed_width))
    unit_grad = cotangent[:, None] * unit_grad0
    proj_grad = (unit_grad - unit * jnp.sum(unit * unit_grad, axis=1, keepdims=True)) / norm_len
    proj_bf = proj_grad.astype(bf16)

    term_other = jnp.dot(window_other, proj_bf, preferred_element_type=f32).astype(bf16)
    term = jnp.dot(window_own, proj_bf, preferred_element_type=f32) + swap(term_other, "core", 1).astype(f32)

    first = jnp.where(core == 0, weight_own, weight_other)
    second = jnp.where(core == 0, weight_other, weight_own)
    full_weight = (
        jnp.stack([first, second])
        .reshape(nc, ny, nz, shard, embed_width)
        .transpose(2, 1, 0, 3, 4)
        .reshape(window_width, embed_width)
    )
    window_grad = lax.dot_general(
        proj_bf, full_weight, (((1,), (1,)), ((), ())), preferred_element_type=f32
    )
    gain_local = jnp.sum(window_grad * normed_head, axis=0)
    bias_local = jnp.sum(window_grad, axis=0)
    sums = jnp.concatenate([gain_local, bias_local]).reshape(-1, embed_width)
    depth = sums.shape[0]
    sums = sums + swap(sums, "core", 1)

    for axis, parts in (("y", ny), ("z", nz)):
        both = split_sum(sums)
        pieces = jnp.concatenate(
            [
                term.astype(bf16).reshape(parts, -1, embed_width),
                jnp.broadcast_to(both[None], (parts,) + both.shape),
            ],
            axis=1,
        )
        pieces = lax.all_to_all(pieces, axis, split_axis=0, concat_axis=0, tiled=True)
        total = jnp.sum(pieces.astype(f32), axis=0)
        term = total[: -2 * depth]
        sums = total[-2 * depth : -depth] + total[-depth:]

    both = jnp.concatenate([term, sums], axis=0)
    both = (both + swap(both, "outer", 2)) + (swap(both, "outer", 1) + swap(both, "outer", 3))
    weight_grad = both[:shard]
    gain_grad = both[shard : shard + depth // 2].reshape(window_width)
    bias_grad = both[shard + depth // 2 :].reshape(window_width)

    scaled_grad = window_grad * ln_gain
    first_mean = jnp.sum(scaled_grad, axis=1, keepdims=True) / width
    second_mean = jnp.sum(scaled_grad * normed_head, axis=1, keepdims=True) / width
    grad_head = inv_std * (scaled_grad - first_mean - normed_head * second_mean)
    grad_tail = inv_std * (0.0 - first_mean - normed_tail * second_mean)
    feat_grad = jnp.concatenate([grad_head.astype(bf16), grad_tail.astype(bf16)], axis=1)
    return (feat_grad, weight_grad, gain_grad, bias_grad)


def solution(mesh):
    outer, dp = mesh.devices.shape
    fine = Mesh(mesh.devices.reshape(outer, 8, dp // 16, 2), ALL)
    in_specs = (
        P(ALL, None),
        P(),
        P(),
        P(DP, None),
        P(ALL, None),
        P(ALL),
        P(ALL),
        P("outer", None),
        P("outer", None),
        P("outer", None, None),
        P(ALL),
    )
    out_specs = (P(ALL, None), P(DP, None), P(), P())
    return jax.shard_map(body, mesh=fine, in_specs=in_specs, out_specs=out_specs, check_vma=False)
```

time: 858 us -> 233 us (0.27)
  local copies, waits for them, and re-layouts: 489 us -> 6.31 us
  blocking collectives: 110 us -> 27.7 us
  waiting for transfers between devices: 182 us -> 112 us
  starting transfers between devices: 33.6 us -> 44.8 us
    gather x3 -> x1, local copies, waits for them, and re-layouts: 260 us -> 1.51 us  [owner_tables(): rows = index_table.at[picked].get(mode='promise_in_bounds')]
    unnamed x43 -> x33, local copies, waits for them, and re-layouts: 225 us -> 1.3 us
    psum x2 -> x0, blocking collectives: 110 us -> none  [the longest x1 95.6 us: body(): gain_grad, bias_grad = lax.psum((gain_local, bias_local), ('outer', 'dp'))]
    reduce_scatter x1 -> x0, waiting for transfers between devices: 86.8 us -> none  [body(): row_share = lax.psum_scatter(term, 'dp', scatter_dimension=0, tiled=True)]
    all_to_all x3 -> x4, waiting for transfers between devices: 40.9 us -> 71.7 us  [the longest x2 42.2 us: body(): lax.all_to_all(pieces, axis, split_axis=0, concat_axis=0, tiled=True)]
    all_gather x0 -> x1, blocking collectives: none -> 27.7 us  [body(): weight_z = lax.all_gather(head_weight, 'z', axis=0, tiled=True)]
    ppermute x0 -> x6, starting transfers between devices: none -> 21 us  [swap(): return lax.ppermute(value, axis, [(i, i ^ flip) for i in range(size)])]
    all_gather x1, waiting for transfers between devices: 53.3 us -> 37.2 us  [body(): weight_own = lax.all_gather(weight_z, 'y', axis=0, tiled=True)]
  transfers between devices with their start and end apart: 5 -> 11, of which waited for: 5 -> 7; matrix products, arithmetic and copies ran while one was open for 2% -> 8% of each run, Pallas kernels for 0% -> 0%
where the time goes in v1:
time: 233 us; the launch traced here: 232 us
  waiting for transfers between devices  112 us (48%)
  starting transfers between devices  44.8 us (19%)
  blocking collectives  27.7 us (12%)
  between operations  14.6 us (6%)
  other arithmetic  14.4 us (6%)
  matrix products  12.6 us (5%)
  local copies, waits for them, and re-layouts  6.31 us (3%)
    all_to_all x2, waiting for transfers between devices, body(): lax.all_to_all(pieces, axis, split_axis=0, concat_axis=0, tiled=True)  42.2 us
    all_gather x1, waiting for transfers between devices, body(): weight_own = lax.all_gather(weight_z, 'y', axis=0, tiled=True)  37.2 us
    all_gather x1, blocking collectives, body(): weight_z = lax.all_gather(head_weight, 'z', axis=0, tiled=True)  27.7 us
    ppermute x6, starting transfers between devices, swap(): return lax.ppermute(value, axis, [(i, i ^ flip) for i in range(size)])  21 us
    all_to_all x1, waiting for transfers between devices, body(): lax.all_to_all(gradient.reshape(dp_count, capacity, embed_width), DP, spl...  15.4 us
    all_to_all x1, waiting for transfers between devices, body(): lax.all_to_all(send_rows.reshape(dp_count, capacity, -1), DP, split_axis=...  14.1 us
    all_to_all x1, starting transfers between devices, body(): lax.all_to_all(send_rows.reshape(dp_count, capacity, -1), DP, split_axis=...  11.3 us
    all_to_all x2, starting transfers between devices, body(): lax.all_to_all(pieces, axis, split_axis=0, concat_axis=0, tiled=True)  6.98 us
  transfers between devices with their start and end apart: 11, of which 7 were waited for; matrix products, arithmetic and copies ran while one was open for 8% of the time, Pallas kernels for 0%

profile of v1, /device:TPU:1, one launch (start us, length us, event | category | flops | bytes accessed | tf_op | source)
XLA Modules:
  0.0 232.1 jit_solution(6740253843401060369)
XLA Ops:
  7.2 27.7 %all_gather.6 = bf16[128,512]{1,0:T(8,128)(2,1)} all-gather(bf16[16,512]{1,0:T(8,128)(2,1)} %param.14), channel_id=1, replica_groups=mesh['outer'=4,'z'=8,'y'=8,'core'=2] {'z'}, dimensions={0}, use_global_device_ids=true | all-gather | bytes 147456 | tf_op jit(solution)/shard_map/all_gather | solution.py:85
  35.0 1.3 convert_reduce_fusion.1
  36.4 0.9 select_reduce_fusion.2
  37.3 0.9 convert_reduce_fusion.3
  38.2 0.4 multiply_reduce_fusion
  38.8 37.2 %all-gather.2.cloned.1.call-done = bf16[1024,512]{1,0:T(8,128)(2,1)} async-done(((bf16[128,512]{1,0:T(8,128)(2,1)}), bf16[1024,512]{1,0:T(8,128)(2,1)}) %all-gather.2.cloned.1.call-update) | async-done | bytes 1048592 | tf_op jit(solution)/shard_map/all_gather | solution.py:86
  76.0 7.3 %collective-permute-start = (bf16[1024,512]{1,0:T(8,128)(2,1)}, bf16[1024,512]{1,0:T(8,128)(2,1)}, u32[]{:S(2)}, u32[]{:S(2)}) collective-permute-start(bf16[1024,512]{1,0:T(8,128)(2,1)} %all-gather.2.cloned.1.call-done), channel_id=1, source_target_pairs={{0,1},{1,0},{2,3},{3,2},{4,5},{5,4},{6,7},{7,6},{8,9},{9,8},{10,11... | collective-permute-start | bytes 3145736 | tf_op jit(solution)/shard_map/ppermute | solution.py:20
  83.4 0.3 copy.27
  84.2 1.5 gather_fusion
  86.0 1.6 fusion.12
  87.6 1.6 multiply_reduce_fusion.5
  89.4 0.3 convolution_convert_fusion.2
  89.7 0.9 reshape.175
  90.5 11.3 %all-to-all-start = ((bf16[128,2,640]{2,1,0:T(2,128)(2,1)}), bf16[128,2,640]{2,1,0:T(2,128)(2,1)S(1)}, u32[]{:S(2)}, u32[]{:S(2)}) async-start(bf16[128,2,640]{2,1,0:T(2,128)(2,1)} %reshape.175), calls=%async_computation | async-start | bytes 655360 | tf_op jit(solution)/shard_map/all_to_all | solution.py:125
  101.9 0.6 iota_convert_fusion
  102.5 0.6 fusion.49
  103.1 1.3 convolution_convert_fusion.1
  104.3 14.1 %all-to-all-done = bf16[128,2,640]{2,1,0:T(2,128)(2,1)S(1)} async-done(((bf16[128,2,640]{2,1,0:T(2,128)(2,1)}), bf16[128,2,640]{2,1,0:T(2,128)(2,1)S(1)}, u32[]{:S(2)}, u32[]{:S(2)}) %all-to-all-start) | async-done | bytes 327712 | tf_op jit(solution)/shard_map/all_to_all | solution.py:125
  118.8 1.5 select_reduce_fusion.1
  120.3 1.0 fusion.6
  121.3 1.2 convolution_convert_fusion.3
  122.5 0.8 reshape.177
  123.3 5.5 %all-to-all-start.1 = ((bf16[128,2,512]{2,1,0:T(2,128)(2,1)}), bf16[128,2,512]{2,1,0:T(2,128)(2,1)S(1)}, u32[]{:S(2)}, u32[]{:S(2)}) async-start(bf16[128,2,512]{2,1,0:T(2,128)(2,1)} %reshape.177), calls=%async_computation.1 | async-start | bytes 524288 | tf_op jit(solution)/shard_map/all_to_all | solution.py:129
  128.8 15.4 %all-to-all-done.1 = bf16[128,2,512]{2,1,0:T(2,128)(2,1)S(1)} async-done(((bf16[128,2,512]{2,1,0:T(2,128)(2,1)}), bf16[128,2,512]{2,1,0:T(2,128)(2,1)S(1)}, u32[]{:S(2)}, u32[]{:S(2)}) %all-to-all-start.1) | async-done | bytes 262176 | tf_op jit(solution)/shard_map/all_to_all | solution.py:129
  144.3 0.3 multiply_reduce_fusion.4
  144.7 1.4 convolution_convert_fusion
  146.1 2.3 collective-permute-start.1
  148.4 1.4 broadcast_select_fusion.1
  150.2 1.8 multiply_reduce_fusion.1
  152.1 2.1 collective-permute-start.2
  154.2 1.0 collective-permute-done.2
  155.2 1.6 add_convert_fusion
  156.9 1.1 pad_maximum_fusion
  158.0 3.6 %all-to-all-start.2 = ((bf16[8,144,512]{2,1,0:T(8,128)(2,1)}), bf16[8,144,512]{2,1,0:T(8,128)(2,1)S(1)}, u32[]{:S(2)}, u32[]{:S(2)}) async-start(bf16[8,144,512]{2,1,0:T(8,128)(2,1)} %pad_maximum_fusion), calls=%async_computation.2 | async-start | bytes 2359296 | tf_op jit(solution)/shard_map/all_to_all | solution.py:166
  161.6 0.9 fusion.4
  162.5 31.1 %all-to-all-done.2 = bf16[8,144,512]{2,1,0:T(8,128)(2,1)S(1)} async-done(((bf16[8,144,512]{2,1,0:T(8,128)(2,1)}), bf16[8,144,512]{2,1,0:T(8,128)(2,1)S(1)}, u32[]{:S(2)}, u32[]{:S(2)}) %all-to-all-start.2) | async-done | bytes 1179680 | tf_op jit(solution)/shard_map/all_to_all | solution.py:166
  193.8 0.7 pad_maximum_fusion.2
  194.5 3.4 %all-to-all-start.3 = ((bf16[8,32,512]{2,1,0:T(8,128)(2,1)}), bf16[8,32,512]{2,1,0:T(8,128)(2,1)S(1)}, u32[]{:S(2)}, u32[]{:S(2)}) async-start(bf16[8,32,512]{2,1,0:T(8,128)(2,1)} %pad_maximum_fusion.2), calls=%async_computation.3 | async-start | bytes 524288 | tf_op jit(solution)/shard_map/all_to_all | solution.py:166
  198.0 1.1 multiply_convert_fusion
  199.0 11.1 %all-to-all-done.3 = bf16[8,32,512]{2,1,0:T(8,128)(2,1)S(1)} async-done(((bf16[8,32,512]{2,1,0:T(8,128)(2,1)}), bf16[8,32,512]{2,1,0:T(8,128)(2,1)S(1)}, u32[]{:S(2)}, u32[]{:S(2)}) %all-to-all-start.3) | async-done | bytes 262176 | tf_op jit(solution)/shard_map/all_to_all | solution.py:166
  210.2 3.1 %collective-permute-start.4 = (f32[24,512]{1,0:T(8,128)S(1)}, f32[24,512]{1,0:T(8,128)S(1)}, u32[]{:S(2)}, u32[]{:S(2)}) collective-permute-start(f32[24,512]{1,0:T(8,128)S(1)} %pad_maximum_fusion.3), channel_id=1, source_target_pairs={{0,128},{128,0},{256,384},{384,256},{1,129},{129,1},{257,385},{385... | collective-permute-start | bytes 147464 | tf_op jit(solution)/shard_map/ppermute | solution.py:20
  213.3 3.7 %collective-permute-start.5 = (f32[24,512]{1,0:T(8,128)S(1)}, f32[24,512]{1,0:T(8,128)S(1)}, u32[]{:S(2)}, u32[]{:S(2)}) collective-permute-start(f32[24,512]{1,0:T(8,128)S(1)} %pad_maximum_fusion.3), channel_id=1, source_target_pairs={{0,384},{128,256},{256,128},{384,0},{1,385},{129,257},{257,129},{3... | collective-permute-start | bytes 147464 | tf_op jit(solution)/shard_map/ppermute | solution.py:20
  217.0 2.5 %collective-permute-start.3 = (f32[24,512]{1,0:T(8,128)S(1)}, f32[24,512]{1,0:T(8,128)S(1)}, u32[]{:S(2)}, u32[]{:S(2)}) collective-permute-start(f32[24,512]{1,0:T(8,128)S(1)} %pad_maximum_fusion.3), channel_id=1, source_target_pairs={{0,256},{128,384},{256,0},{384,128},{1,257},{129,385},{257,1},{385... | collective-permute-start | bytes 147464 | tf_op jit(solution)/shard_map/ppermute | solution.py:20
  219.6 2.1 pad_maximum_fusion.1
  221.6 1.7 collective-permute-done.3
  223.4 0.6 slice.70
  224.0 0.6 copy.32
  224.6 0.6 copy.33
  (80 shorter events, 2.7 us)
Async XLA Ops:
  7.2 95.9 %copy-start = (bf16[512,512]{1,0:T(8,128)(2,1)S(1)}, bf16[512,512]{1,0:T(8,128)(2,1)}, u32[]{:S(2)}) copy-start(bf16[512,512]{1,0:T(8,128)(2,1)} %param.15) | copy-start | bytes 1572868
  7.2 31.0 %copy-start.3 = (bf16[128,3072]{1,0:T(8,128)(2,1)S(1)}, bf16[128,3072]{1,0:T(8,128)(2,1)}, u32[]{:S(2)}) copy-start(bf16[128,3072]{1,0:T(8,128)(2,1)} %param.11) | copy-start | bytes 2359300
  7.2 68.8 %all-gather.2.cloned.1.call-start = ((), (), s32[]{:S(2)}) async-start(), calls=%async_computation.4 | async-start | bytes 1179648 | tf_op jit(solution)/shard_map/all_gather | solution.py:86
  35.0 3.5 %copy-start.10 = (s32[128]{0:T(128)S(1)}, s32[128]{0:T(128)}, u32[]{:S(2)}) copy-start(s32[128]{0:T(128)} %param.17) | copy-start | bytes 1540
  35.0 3.5 %copy-start.5 = (s32[1,512]{1,0:T(1,128)S(1)}, s32[1,512]{1,0:T(1,128)}, u32[]{:S(2)}) copy-start(s32[1,512]{1,0:T(1,128)} %param.18) | copy-start | bytes 6148
  35.0 3.6 %copy-start.4 = (f32[2048]{0:T(1024)S(1)}, f32[2048]{0:T(1024)}, u32[]{:S(2)}) copy-start(f32[2048]{0:T(1024)} %param.12) | copy-start | bytes 24580
  35.0 3.6 %copy-start.6 = (f32[2048]{0:T(1024)S(1)}, f32[2048]{0:T(1024)}, u32[]{:S(2)}) copy-start(f32[2048]{0:T(1024)} %param.13) | copy-start | bytes 24580
  38.6 45.5 %copy-start.9 = (s32[1,512]{1,0:T(1,128)S(1)}, s32[1,512]{1,0:T(1,128)}, u32[]{:S(2)}) copy-start(s32[1,512]{1,0:T(1,128)} %param.19) | copy-start | bytes 6148
  76.0 11.6 %collective-permute-start = (bf16[1024,512]{1,0:T(8,128)(2,1)}, bf16[1024,512]{1,0:T(8,128)(2,1)}, u32[]{:S(2)}, u32[]{:S(2)}) collective-permute-start(bf16[1024,512]{1,0:T(8,128)(2,1)} %all-gather.2.cloned.1.call-done), channel_id=1, source_target_pairs={{0,1},{1,0},{2,3},{3,2},{4,5},{5,4},{6,7},{7,6},{8,9},{9,8},{10,11... | collective-permute-start | bytes 3145736 | tf_op jit(solution)/shard_map/ppermute | solution.py:20
  86.0 3.4 %copy-start.12 = (s32[128]{0:T(128)}, s32[128]{0:T(128)S(1)}, u32[]{:S(2)}) copy-start(s32[128]{0:T(128)S(1)} %multiply_add_fusion) | copy-start | bytes 1540
  89.3 1.3 copy-start.7
  90.5 27.9 %all-to-all-start = ((bf16[128,2,640]{2,1,0:T(2,128)(2,1)}), bf16[128,2,640]{2,1,0:T(2,128)(2,1)S(1)}, u32[]{:S(2)}, u32[]{:S(2)}) async-start(bf16[128,2,640]{2,1,0:T(2,128)(2,1)} %reshape.175), calls=%async_computation | async-start | bytes 655360 | tf_op jit(solution)/shard_map/all_to_all | solution.py:125
  118.6 2.7 %copy-start.14 = (bf16[512,512]{1,0:T(8,128)(2,1)S(1)}, bf16[512,512]{1,0:T(8,128)(2,1)}, u32[]{:S(2)}) copy-start(bf16[512,512]{1,0:T(8,128)(2,1)} %convolution_convert_fusion.1) | copy-start | bytes 1572868
  122.4 21.8 %copy-start.8 = (f32[128]{0:T(128)S(1)}, f32[128]{0:T(128)}, u32[]{:S(2)}) copy-start(f32[128]{0:T(128)} %copy-done.7) | copy-start | bytes 1540
  122.5 21.8 %copy-start.11 = (f32[128]{0:T(128)S(1)}, f32[128]{0:T(128)}, u32[]{:S(2)}) copy-start(f32[128]{0:T(128)} %param.21) | copy-start | bytes 1540
  122.5 21.8 %copy-start.13 = (s32[128]{0:T(128)S(1)}, s32[128]{0:T(128)}, u32[]{:S(2)}) copy-start(s32[128]{0:T(128)} %copy-done.12) | copy-start | bytes 1540
  123.3 20.8 %all-to-all-start.1 = ((bf16[128,2,512]{2,1,0:T(2,128)(2,1)}), bf16[128,2,512]{2,1,0:T(2,128)(2,1)S(1)}, u32[]{:S(2)}, u32[]{:S(2)}) async-start(bf16[128,2,512]{2,1,0:T(2,128)(2,1)} %reshape.177), calls=%async_computation.1 | async-start | bytes 524288 | tf_op jit(solution)/shard_map/all_to_all | solution.py:129
  144.3 4.1 %copy-start.1 = (bf16[1024,512]{1,0:T(8,128)(2,1)S(1)}, bf16[1024,512]{1,0:T(8,128)(2,1)}, u32[]{:S(2)}) copy-start(bf16[1024,512]{1,0:T(8,128)(2,1)} %all-gather.2.cloned.1.call-done) | copy-start | bytes 3145732
  146.1 9.1 %collective-permute-start.1 = (bf16[1024,512]{1,0:T(8,128)(2,1)}, bf16[1024,512]{1,0:T(8,128)(2,1)}, u32[]{:S(2)}, u32[]{:S(2)}) collective-permute-start(bf16[1024,512]{1,0:T(8,128)(2,1)} %convolution_convert_fusion), channel_id=1, source_target_pairs={{0,1},{1,0},{2,3},{3,2},{4,5},{5,4},{6,7},{7,6},{8,9},{9,8},{10,11... | collective-permute-start | bytes 3145736 | tf_op jit(solution)/shard_map/ppermute | solution.py:20
  152.1 3.1 %collective-permute-start.2 = (f32[8,512]{1,0:T(8,128)S(1)}, f32[8,512]{1,0:T(8,128)S(1)}, u32[]{:S(2)}, u32[]{:S(2)}) collective-permute-start(f32[8,512]{1,0:T(8,128)S(1)} %pad_maximum_fusion.4), channel_id=1, source_target_pairs={{0,1},{1,0},{2,3},{3,2},{4,5},{5,4},{6,7},{7,6},{8,9},{9,8},{10,11... | collective-permute-start | bytes 49160 | tf_op jit(solution)/shard_map/ppermute | solution.py:20
  158.0 35.6 %all-to-all-start.2 = ((bf16[8,144,512]{2,1,0:T(8,128)(2,1)}), bf16[8,144,512]{2,1,0:T(8,128)(2,1)S(1)}, u32[]{:S(2)}, u32[]{:S(2)}) async-start(bf16[8,144,512]{2,1,0:T(8,128)(2,1)} %pad_maximum_fusion), calls=%async_computation.2 | async-start | bytes 2359296 | tf_op jit(solution)/shard_map/all_to_all | solution.py:166
  193.7 4.2 %copy-start.2 = (f32[128,2048]{1,0:T(8,128)S(1)}, f32[128,2048]{1,0:T(8,128)}, u32[]{:S(2)}) copy-start(f32[128,2048]{1,0:T(8,128)} %get-tuple-element.32) | copy-start | bytes 3145732
  194.5 15.6 %all-to-all-start.3 = ((bf16[8,32,512]{2,1,0:T(8,128)(2,1)}), bf16[8,32,512]{2,1,0:T(8,128)(2,1)S(1)}, u32[]{:S(2)}, u32[]{:S(2)}) async-start(bf16[8,32,512]{2,1,0:T(8,128)(2,1)} %pad_maximum_fusion.2), calls=%async_computation.3 | async-start | bytes 524288 | tf_op jit(solution)/shard_map/all_to_all | solution.py:166
  210.2 11.4 %collective-permute-start.4 = (f32[24,512]{1,0:T(8,128)S(1)}, f32[24,512]{1,0:T(8,128)S(1)}, u32[]{:S(2)}, u32[]{:S(2)}) collective-permute-start(f32[24,512]{1,0:T(8,128)S(1)} %pad_maximum_fusion.3), channel_id=1, source_target_pairs={{0,128},{128,0},{256,384},{384,256},{1,129},{129,1},{257,385},{385... | collective-permute-start | bytes 147464 | tf_op jit(solution)/shard_map/ppermute | solution.py:20
  213.3 8.3 %collective-permute-start.5 = (f32[24,512]{1,0:T(8,128)S(1)}, f32[24,512]{1,0:T(8,128)S(1)}, u32[]{:S(2)}, u32[]{:S(2)}) collective-permute-start(f32[24,512]{1,0:T(8,128)S(1)} %pad_maximum_fusion.3), channel_id=1, source_target_pairs={{0,384},{128,256},{256,128},{384,0},{1,385},{129,257},{257,129},{3... | collective-permute-start | bytes 147464 | tf_op jit(solution)/shard_map/ppermute | solution.py:20
  217.0 6.3 %collective-permute-start.3 = (f32[24,512]{1,0:T(8,128)S(1)}, f32[24,512]{1,0:T(8,128)S(1)}, u32[]{:S(2)}, u32[]{:S(2)}) collective-permute-start(f32[24,512]{1,0:T(8,128)S(1)} %pad_maximum_fusion.3), channel_id=1, source_target_pairs={{0,256},{128,384},{256,0},{384,128},{1,257},{129,385},{257,1},{385... | collective-permute-start | bytes 147464 | tf_op jit(solution)/shard_map/ppermute | solution.py:20
Sparse Core Ops, SparseCore 0:
  35.1 40.8 all-gather.1

commit v2 on v1

--- a/solution.py
+++ b/solution.py
@@ -10,14 +10,27 @@
 ALL = ("outer", "z", "y", "core")
 
 
-def split_sum(value):
-    high = lax.reduce_precision(value, 8, 7)
-    return jnp.concatenate([high.astype(bf16), (value - high).astype(bf16)], axis=0)
-
-
 def swap(value, axis, flip):
     size = lax.axis_size(axis)
     return lax.ppermute(value, axis, [(i, i ^ flip) for i in range(size)])
+
+
+def split_sum(value, axis):
+    high = lax.reduce_precision(value, 8, 7)
+    return jnp.concatenate([high.astype(bf16), (value - high).astype(bf16)], axis=axis)
+
+
+def exchange(pieces, axis):
+    return lax.all_to_all(pieces, axis, split_axis=0, concat_axis=0, tiled=True)
+
+
+def gather(value, axis):
+    size = lax.axis_size(axis)
+    return exchange(jnp.broadcast_to(value[None], (size,) + value.shape), axis)
+
+
+def side_by_side(blocks):
+    return jnp.concatenate([blocks[i] for i in range(blocks.shape[0])], axis=1)
 
 
 def owner_tables(captions, owner_table, size_table, index_table, me):
@@ -82,9 +95,12 @@
     kmax = cap_index.shape[2]
     owner_table = cluster_owner[0]
 
-    weight_z = lax.all_gather(head_weight, "z", axis=0, tiled=True)
-    weight_own = lax.all_gather(weight_z, "y", axis=0, tiled=True)
-    weight_other = swap(weight_own, "core", 1)
+    outer = lax.axis_index("outer")
+    n_outer = lax.axis_size("outer")
+    block = embed_width // n_outer
+    columns = lax.dynamic_slice_in_dim(head_weight, outer * block, block, 1)
+    columns = gather(columns, ("z", "y")).reshape(half, block)
+    weight_own = side_by_side(gather(columns, "outer"))
 
     widened = feats.astype(f32)
     means = jnp.mean(widened, axis=1, keepdims=True)
@@ -93,11 +109,14 @@
     normed_head = centred[:, :window_width] * inv_std
     normed_tail = centred[:, window_width:] * inv_std
     window_bf = (normed_head * ln_gain + ln_bias).astype(bf16)
-    by_feature = (
-        window_bf.T.reshape(nz, ny, nc, shard, count).transpose(2, 1, 0, 3, 4).reshape(nc, half, count)
-    )
-    window_own = lax.dynamic_index_in_dim(by_feature, core, 0, keepdims=False)
-    window_other = lax.dynamic_index_in_dim(by_feature, 1 - core, 0, keepdims=False)
+    by_feature = window_bf.T.reshape(nz * ny, nc, shard, count)
+    window_own = lax.dynamic_index_in_dim(by_feature, core, 1, keepdims=False).reshape(half, count)
+    window_other = lax.dynamic_index_in_dim(by_feature, 1 - core, 1, keepdims=False).reshape(half, count)
+    window_sent = swap(window_other, "core", 1)
+    window_pair = jnp.concatenate(
+        [jnp.where(core == 0, window_own, window_sent), jnp.where(core == 0, window_sent, window_own)], axis=1
+    )
+    window_all = side_by_side(lax.all_gather(window_pair, "outer", axis=0))
 
     ids = jnp.arange(owner_table.shape[0], dtype=jnp.int32)[None, :]
     owners = jnp.sum(jnp.where(image_cluster[:, None] == ids, owner_table[None, :], 0), axis=1)
@@ -117,7 +136,16 @@
     def by_rows(left, right):
         return lax.dot_general(left, right, (((0,), (0,)), ((), ())), preferred_element_type=f32)
 
-    projected = by_rows(window_own, weight_own) + by_rows(window_other, weight_other)
+    partial = by_rows(window_pair, weight_own).reshape(nc, count, embed_width)
+    partial_own = lax.dynamic_index_in_dim(partial, core, 0, keepdims=False)
+    partial_other = lax.dynamic_index_in_dim(partial, 1 - core, 0, keepdims=False)
+    partial_sent = swap(partial_other, "core", 1)
+    projected = partial_own + partial_sent
+    weight_own, projected = lax.optimization_barrier((weight_own, projected))
+    weight_other = swap(weight_own, "core", 1)
+    first = jnp.where(core == 0, weight_own, weight_other).reshape(nz * ny, 1, shard, embed_width)
+    second = jnp.where(core == 0, weight_other, weight_own).reshape(nz * ny, 1, shard, embed_width)
+    full_weight = jnp.concatenate([first, second], axis=1).reshape(window_width, embed_width)
     norm_len = jnp.sqrt(jnp.sum(projected * projected, axis=1, keepdims=True) + 1e-06)
     unit = projected / norm_len
     payload = jnp.concatenate([unit.astype(bf16), labels], axis=1)
@@ -126,6 +154,7 @@
         send_rows.reshape(dp_count, capacity, -1), DP, split_axis=0, concat_axis=0, tiled=True
     )
     gradient = owner_work(received.reshape(dp_count * capacity, -1), ordered, used, kmax)
+    window_all, gradient = lax.optimization_barrier((window_all, gradient))
     returned = lax.all_to_all(
         gradient.reshape(dp_count, capacity, embed_width), DP, split_axis=0, concat_axis=0, tiled=True
     )
@@ -134,45 +163,35 @@
     proj_grad = (unit_grad - unit * jnp.sum(unit * unit_grad, axis=1, keepdims=True)) / norm_len
     proj_bf = proj_grad.astype(bf16)
 
-    term_other = jnp.dot(window_other, proj_bf, preferred_element_type=f32).astype(bf16)
-    term = jnp.dot(window_own, proj_bf, preferred_element_type=f32) + swap(term_other, "core", 1).astype(f32)
-
-    first = jnp.where(core == 0, weight_own, weight_other)
-    second = jnp.where(core == 0, weight_other, weight_own)
-    full_weight = (
-        jnp.stack([first, second])
-        .reshape(nc, ny, nz, shard, embed_width)
-        .transpose(2, 1, 0, 3, 4)
-        .reshape(window_width, embed_width)
-    )
     window_grad = lax.dot_general(
         proj_bf, full_weight, (((1,), (1,)), ((), ())), preferred_element_type=f32
     )
     gain_local = jnp.sum(window_grad * normed_head, axis=0)
     bias_local = jnp.sum(window_grad, axis=0)
-    sums = jnp.concatenate([gain_local, bias_local]).reshape(-1, embed_width)
-    depth = sums.shape[0]
-    sums = sums + swap(sums, "core", 1)
-
-    for axis, parts in (("y", ny), ("z", nz)):
-        both = split_sum(sums)
-        pieces = jnp.concatenate(
-            [
-                term.astype(bf16).reshape(parts, -1, embed_width),
-                jnp.broadcast_to(both[None], (parts,) + both.shape),
-            ],
-            axis=1,
-        )
-        pieces = lax.all_to_all(pieces, axis, split_axis=0, concat_axis=0, tiled=True)
-        total = jnp.sum(pieces.astype(f32), axis=0)
-        term = total[: -2 * depth]
-        sums = total[-2 * depth : -depth] + total[-depth:]
-
-    both = jnp.concatenate([term, sums], axis=0)
-    both = (both + swap(both, "outer", 2)) + (swap(both, "outer", 1) + swap(both, "outer", 3))
-    weight_grad = both[:shard]
-    gain_grad = both[shard : shard + depth // 2].reshape(window_width)
-    bias_grad = both[shard + depth // 2 :].reshape(window_width)
+
+    group = n_outer * nc
+    sums = jnp.concatenate([gain_local, bias_local]).reshape(group, -1, block)
+    depth = sums.shape[1]
+    blocks = jnp.concatenate([proj_bf[:, i * block : (i + 1) * block] for i in range(n_outer)], axis=0)
+    blocks = blocks.reshape(n_outer, 1, count, block)
+    blocks = jnp.broadcast_to(blocks, (n_outer, nc, count, block)).reshape(group, count, block)
+    pieces = exchange(jnp.concatenate([blocks, split_sum(sums, 1)], axis=1), ("outer", "core"))
+    proj_all = pieces[:, :count].reshape(-1, block)
+    sums = jnp.sum(pieces[:, count:].astype(f32), axis=0)
+    sums = sums[:depth] + sums[depth:]
+
+    term = jnp.dot(window_all, proj_all, preferred_element_type=f32).astype(bf16)
+    sums = split_sum(sums, 0)
+    sums = jnp.broadcast_to(sums[None], (nz * ny,) + sums.shape)
+    pieces = exchange(jnp.concatenate([term.reshape(nz * ny, shard, block), sums], axis=1), ("z", "y"))
+    pieces = jnp.sum(pieces.astype(f32), axis=0)
+    sums = pieces[shard : shard + depth] + pieces[shard + depth :]
+
+    last = gather(jnp.concatenate([pieces[:shard], sums], axis=0), ("outer", "core"))
+    last = last.reshape(n_outer, nc, shard + depth, block)
+    weight_grad = side_by_side(lax.dynamic_index_in_dim(last[:, :, :shard], core, 1, keepdims=False))
+    sums = last[:, :, shard:].reshape(2, window_width)
+    gain_grad, bias_grad = sums[0], sums[1]
 
     scaled_grad = window_grad * ln_gain
     first_mean = jnp.sum(scaled_grad, axis=1, keepdims=True) / width

time: 233 us -> 186 us (0.80)
  waiting for transfers between devices: 112 us -> 60.5 us
  blocking collectives: 27.7 us -> 0 us
  starting transfers between devices: 44.8 us -> 62.5 us
  local copies, waits for them, and re-layouts: 6.31 us -> 18.6 us
  other arithmetic: 14.4 us -> 19.1 us
  matrix products: 12.6 us -> 9.58 us
    all_gather x1, waiting for transfers between devices: 37.2 us -> 0.01 us  [body(): window_all = side_by_side(lax.all_gather(window_pair, 'outer', axis=0))]
    all_to_all x2 -> x5, starting transfers between devices: 6.98 us -> 36.3 us  [exchange(): return lax.all_to_all(pieces, axis, split_axis=0, concat_axis=0, tiled=True)]
    all_gather x1 -> x0, blocking collectives: 27.7 us -> none  [body(): weight_z = lax.all_gather(head_weight, 'z', axis=0, tiled=True)]
    ppermute x6 -> x3, starting transfers between devices: 21 us -> 12.4 us  [swap(): return lax.ppermute(value, axis, [(i, i ^ flip) for i in range(size)])]
    all_to_all x2 -> x5, waiting for transfers between devices: 42.2 us -> 36.3 us  [exchange(): return lax.all_to_all(pieces, axis, split_axis=0, concat_axis=0, tiled=True)]
    concatenate x6 -> x10, other arithmetic: 1.85 us -> 6.27 us  [the longest x3 2.38 us: side_by_side(): return jnp.concatenate([blocks[i] for i in range(blocks.shape[0])], axis=1)]
    all_to_all x1, starting transfers between devices: 11.3 us -> 7.41 us  [body(): lax.all_to_all(send_rows.reshape(dp_count, capacity, -1), DP, split_axis=...]
    all_to_all x1, waiting for transfers between devices: 15.4 us -> 12.1 us  [body(): lax.all_to_all(gradient.reshape(dp_count, capacity, embed_width), DP, spl...]
  transfers between devices with their start and end apart: 11 -> 11, of which waited for: 7 -> 7; matrix products, arithmetic and copies ran while one was open for 8% -> 18% of each run, Pallas kernels for 0% -> 0%
where the time goes in v2:
time: 186 us; the launch traced here: 185 us
  starting transfers between devices  62.5 us (34%)
  waiting for transfers between devices  60.5 us (33%)
  other arithmetic  19.1 us (10%)
  local copies, waits for them, and re-layouts  18.6 us (10%)
  between operations  14.5 us (8%)
  matrix products  9.58 us (5%)
    all_to_all x5, starting transfers between devices, exchange(): return lax.all_to_all(pieces, axis, split_axis=0, concat_axis=0, tiled=True)  36.3 us
    all_to_all x5, waiting for transfers between devices, exchange(): return lax.all_to_all(pieces, axis, split_axis=0, concat_axis=0, tiled=True)  36.3 us
    ppermute x3, starting transfers between devices, swap(): return lax.ppermute(value, axis, [(i, i ^ flip) for i in range(size)])  12.4 us
    all_to_all x1, waiting for transfers between devices, body(): lax.all_to_all(gradient.reshape(dp_count, capacity, embed_width), DP, spl...  12.1 us
    all_to_all x1, waiting for transfers between devices, body(): lax.all_to_all(send_rows.reshape(dp_count, capacity, -1), DP, split_axis=...  12 us
    all_to_all x1, starting transfers between devices, body(): lax.all_to_all(send_rows.reshape(dp_count, capacity, -1), DP, split_axis=...  7.41 us
    all_to_all x1, starting transfers between devices, body(): lax.all_to_all(gradient.reshape(dp_count, capacity, embed_width), DP, spl...  6.49 us
  transfers between devices with their start and end apart: 11, of which 7 were waited for; matrix products, arithmetic and copies ran while one was open for 18% of the time, Pallas kernels for 0%

profile of v2, /device:TPU:1, one launch (start us, length us, event | category | flops | bytes accessed | tf_op | source)
XLA Modules:
  0.0 184.9 jit_solution(8967550010441391228)
XLA Ops:
  7.2 0.8 constant_dynamic-slice_fusion
  8.0 0.7 broadcast_in_dim.133
  8.7 17.1 %all-to-all-start = ((bf16[64,16,128]{2,1,0:T(8,128)(2,1)}), bf16[64,16,128]{2,1,0:T(8,128)(2,1)S(1)}, u32[]{:S(2)}, u32[]{:S(2)}) async-start(bf16[64,16,128]{2,1,0:T(8,128)(2,1)} %broadcast_in_dim.133), calls=%async_computation | async-start | bytes 524288 | tf_op jit(solution)/shard_map/all_to_all | solution.py:24
  25.9 1.3 convert_reduce_fusion
  28.1 0.8 constant_dynamic-slice_fusion.2
  29.0 2.9 %collective-permute-start = (bf16[1024,128]{1,0:T(8,128)(2,1)}, bf16[1024,128]{1,0:T(8,128)(2,1)}, u32[]{:S(2)}, u32[]{:S(2)}) collective-permute-start(bf16[1024,128]{1,0:T(8,128)(2,1)} %bitcast.4), channel_id=1, source_target_pairs={{0,1},{1,0},{2,3},{3,2},{4,5},{5,4},{6,7},{7,6},{8,9},{9,8},{10,11... | collective-permute-start | bytes 786440 | tf_op jit(solution)/shard_map/ppermute | solution.py:15
  32.4 6.1 %all-to-all-done = bf16[64,16,128]{2,1,0:T(8,128)(2,1)S(1)} async-done(((bf16[64,16,128]{2,1,0:T(8,128)(2,1)}), bf16[64,16,128]{2,1,0:T(8,128)(2,1)S(1)}, u32[]{:S(2)}, u32[]{:S(2)}) %all-to-all-start) | async-done | bytes 262176 | tf_op jit(solution)/shard_map/all_to_all | solution.py:24
  38.5 1.1 broadcast_in_dim.135
  39.7 4.1 %all-to-all-start.1 = ((bf16[4,1024,128]{2,1,0:T(8,128)(2,1)}), bf16[4,1024,128]{2,1,0:T(8,128)(2,1)S(1)}, u32[]{:S(2)}, u32[]{:S(2)}) async-start(bf16[4,1024,128]{2,1,0:T(8,128)(2,1)} %broadcast_in_dim.135), calls=%async_computation.1 | async-start | bytes 2097152 | tf_op jit(solution)/shard_map/all_to_all | solution.py:24
  44.2 1.0 bitcast_select_fusion.1
  46.0 0.8 pad_maximum_fusion.4
  46.9 8.3 %all-to-all-done.1 = bf16[4,1024,128]{2,1,0:T(8,128)(2,1)S(1)} async-done(((bf16[4,1024,128]{2,1,0:T(8,128)(2,1)}), bf16[4,1024,128]{2,1,0:T(8,128)(2,1)S(1)}, u32[]{:S(2)}, u32[]{:S(2)}) %all-to-all-start.1) | async-done | bytes 1048608 | tf_op jit(solution)/shard_map/all_to_all | solution.py:24
  55.3 0.7 copy-done.7
  56.6 0.8 copy-done.8
  57.4 6.7 %collective-permute-start.1 = (f32[128,512]{1,0:T(8,128)S(1)}, f32[128,512]{1,0:T(8,128)}, u32[]{:S(2)}, u32[]{:S(2)}) collective-permute-start(f32[128,512]{1,0:T(8,128)S(1)} %dynamic-slice_bitcast_fusion), channel_id=1, source_target_pairs={{0,1},{1,0},{2,3},{3,2},{4,5},{5,4},{6,7},{7,6},{8,9},{9,8},{10,11... | collective-permute-start | bytes 786440 | tf_op jit(solution)/shard_map/ppermute | solution.py:15
  64.3 1.5 gather_fusion
  65.9 1.1 bitcast_add_fusion
  67.2 1.0 convolution_convert_fusion.1
  68.2 1.8 reshape.203
  70.0 7.4 %all-to-all-start.2 = ((bf16[128,2,640]{2,1,0:T(2,128)(2,1)}), bf16[128,2,640]{2,1,0:T(2,128)(2,1)}, u32[]{:S(2)}, u32[]{:S(2)}) async-start(bf16[128,2,640]{2,1,0:T(2,128)(2,1)} %reshape.203), calls=%async_computation.2 | async-start | bytes 655360 | tf_op jit(solution)/shard_map/all_to_all | solution.py:153
  77.5 1.3 convolution_convert_fusion
  78.8 2.8 %collective-permute-start.2 = (bf16[1024,512]{1,0:T(8,128)(2,1)S(1)}, bf16[1024,512]{1,0:T(8,128)(2,1)}, u32[]{:S(2)}, u32[]{:S(2)}) collective-permute-start(bf16[1024,512]{1,0:T(8,128)(2,1)S(1)} %pad_maximum_fusion.2), channel_id=1, source_target_pairs={{0,1},{1,0},{2,3},{3,2},{4,5},{5,4},{6,7},{7,6},{8,9},{9,8},{10,11... | collective-permute-start | bytes 3145736 | tf_op jit(solution)/shard_map/ppermute | solution.py:15
  81.7 12.0 %all-to-all-done.2 = bf16[128,2,640]{2,1,0:T(2,128)(2,1)} async-done(((bf16[128,2,640]{2,1,0:T(2,128)(2,1)}), bf16[128,2,640]{2,1,0:T(2,128)(2,1)}, u32[]{:S(2)}, u32[]{:S(2)}) %all-to-all-start.2) | async-done | bytes 327712 | tf_op jit(solution)/shard_map/all_to_all | solution.py:153
  93.7 1.8 reshape.204
  95.5 1.1 fusion.25
  96.7 1.6 select_reduce_fusion.1
  98.6 1.2 convolution_convert_fusion.3
  99.8 1.7 fusion.44
  101.4 1.6 pad_maximum_fusion
  103.1 1.7 reshape.205
  104.8 6.5 %all-to-all-start.3 = ((bf16[128,2,512]{2,1,0:T(2,128)(2,1)}), bf16[128,2,512]{2,1,0:T(2,128)(2,1)}, u32[]{:S(2)}, u32[]{:S(2)}) async-start(bf16[128,2,512]{2,1,0:T(2,128)(2,1)} %reshape.205), calls=%async_computation.3 | async-start | bytes 524288 | tf_op jit(solution)/shard_map/all_to_all | solution.py:158
  111.3 1.4 broadcast_select_fusion.1
  112.7 1.5 pad_maximum_fusion.1
  114.2 12.1 %all-to-all-done.3 = bf16[128,2,512]{2,1,0:T(2,128)(2,1)} async-done(((bf16[128,2,512]{2,1,0:T(2,128)(2,1)}), bf16[128,2,512]{2,1,0:T(2,128)(2,1)}, u32[]{:S(2)}, u32[]{:S(2)}) %all-to-all-start.3) | async-done | bytes 262176 | tf_op jit(solution)/shard_map/all_to_all | solution.py:158
  126.3 1.1 reshape.206
  127.9 1.1 copy-done.1
  129.0 1.5 multiply_reduce_fusion.1
  131.3 3.7 %all-to-all-start.4 = ((bf16[8,136,128]{2,1,0:T(8,128)(2,1)}), bf16[8,136,128]{2,1,0:T(8,128)(2,1)S(1)}, u32[]{:S(2)}, u32[]{:S(2)}) async-start(bf16[8,136,128]{2,1,0:T(8,128)(2,1)} %pad_maximum_fusion.6), calls=%async_computation.4 | async-start | bytes 557056 | tf_op jit(solution)/shard_map/all_to_all | solution.py:24
  135.0 6.7 %all-to-all-done.4 = bf16[8,136,128]{2,1,0:T(8,128)(2,1)S(1)} async-done(((bf16[8,136,128]{2,1,0:T(8,128)(2,1)}), bf16[8,136,128]{2,1,0:T(8,128)(2,1)S(1)}, u32[]{:S(2)}, u32[]{:S(2)}) %all-to-all-start.4) | async-done | bytes 278560 | tf_op jit(solution)/shard_map/all_to_all | solution.py:24
  141.7 2.3 %convolution_convert_fusion.2 = bf16[1024,128]{1,0:T(8,128)(2,1)S(1)} fusion(bf16[1024,1024]{1,0:T(8,128)(2,1)} %pad_maximum_fusion, bf16[1024,128]{1,0:T(8,128)(2,1)S(1)} %bitcast.71), kind=kOutput, calls=%fused_computation.9 | convolution fusion | flops 268566528 | bytes 2621440 | tf_op jit(solution)/shard_map/dot_general | solution.py:183
  144.1 0.8 pad_maximum_fusion.5
  144.9 4.6 %all-to-all-start.5 = ((bf16[64,24,128]{2,1,0:T(8,128)(2,1)}), bf16[64,24,128]{2,1,0:T(8,128)(2,1)S(1)}, u32[]{:S(2)}, u32[]{:S(2)}) async-start(bf16[64,24,128]{2,1,0:T(8,128)(2,1)} %pad_maximum_fusion.5), calls=%async_computation.5 | async-start | bytes 786432 | tf_op jit(solution)/shard_map/all_to_all | solution.py:24
  150.2 0.9 fusion.4
  151.0 1.1 multiply_convert_fusion
  152.1 12.3 %all-to-all-done.5 = bf16[64,24,128]{2,1,0:T(8,128)(2,1)S(1)} async-done(((bf16[64,24,128]{2,1,0:T(8,128)(2,1)}), bf16[64,24,128]{2,1,0:T(8,128)(2,1)S(1)}, u32[]{:S(2)}, u32[]{:S(2)}) %all-to-all-start.5) | async-done | bytes 393248 | tf_op jit(solution)/shard_map/all_to_all | solution.py:24
  165.1 6.7 %all-to-all-start.6 = ((f32[8,20,128]{2,1,0:T(8,128)}), f32[8,20,128]{2,1,0:T(8,128)S(1)}, u32[]{:S(2)}, u32[]{:S(2)}) async-start(f32[8,20,128]{2,1,0:T(8,128)} %broadcast_in_dim.143), calls=%async_computation.6 | async-start | bytes 196608 | tf_op jit(solution)/shard_map/all_to_all | solution.py:24
  171.8 2.1 %pad_maximum_fusion.3 = bf16[128,3072]{1,0:T(8,128)(2,1)} fusion(bf16[128,1024]{1,0:T(8,128)(2,1)} %fusion.4, bf16[128,2048]{1,0:T(8,128)(2,1)} %multiply_convert_fusion), kind=kLoop, calls=%fused_computation.24 | loop fusion | flops 1572864 | bytes 1572864 | tf_op jit(solution)/shard_map/concatenate | solution.py:201
  173.8 2.9 %all-to-all-done.6 = f32[8,20,128]{2,1,0:T(8,128)S(1)} async-done(((f32[8,20,128]{2,1,0:T(8,128)}), f32[8,20,128]{2,1,0:T(8,128)S(1)}, u32[]{:S(2)}, u32[]{:S(2)}) %all-to-all-start.6) | async-done | bytes 81952 | tf_op jit(solution)/shard_map/all_to_all | solution.py:24
  (90 shorter events, 8.2 us)
Async XLA Ops:
  7.2 70.4 %copy-start = (bf16[512,512]{1,0:T(8,128)(2,1)S(1)}, bf16[512,512]{1,0:T(8,128)(2,1)}, u32[]{:S(2)}) copy-start(bf16[512,512]{1,0:T(8,128)(2,1)} %param.15) | copy-start | bytes 1572868
  7.2 20.0 %copy-start.2 = (bf16[128,3072]{1,0:T(8,128)(2,1)S(1)}, bf16[128,3072]{1,0:T(8,128)(2,1)}, u32[]{:S(2)}) copy-start(bf16[128,3072]{1,0:T(8,128)(2,1)} %param.11) | copy-start | bytes 2359300
  7.2 20.5 %copy-start.9 = (f32[2048]{0:T(1024)S(1)}, f32[2048]{0:T(1024)}, u32[]{:S(2)}) copy-start(f32[2048]{0:T(1024)} %param.12) | copy-start | bytes 24580
  7.2 20.5 %copy-start.11 = (f32[2048]{0:T(1024)S(1)}, f32[2048]{0:T(1024)}, u32[]{:S(2)}) copy-start(f32[2048]{0:T(1024)} %param.13) | copy-start | bytes 24580
  8.7 29.8 %all-to-all-start = ((bf16[64,16,128]{2,1,0:T(8,128)(2,1)}), bf16[64,16,128]{2,1,0:T(8,128)(2,1)S(1)}, u32[]{:S(2)}, u32[]{:S(2)}) async-start(bf16[64,16,128]{2,1,0:T(8,128)(2,1)} %broadcast_in_dim.133), calls=%async_computation | async-start | bytes 524288 | tf_op jit(solution)/shard_map/all_to_all | solution.py:24
  27.6 4.3 %copy-start.10 = (s32[1,512]{1,0:T(1,128)S(1)}, s32[1,512]{1,0:T(1,128)}, u32[]{:S(2)}) copy-start(s32[1,512]{1,0:T(1,128)} %param.18) | copy-start | bytes 6148
  27.6 4.4 %copy-start.12 = (s32[128]{0:T(128)S(1)}, s32[128]{0:T(128)}, u32[]{:S(2)}) copy-start(s32[128]{0:T(128)} %param.16) | copy-start | bytes 1540
  27.6 4.6 %copy-start.13 = (s32[1,512]{1,0:T(1,128)S(1)}, s32[1,512]{1,0:T(1,128)}, u32[]{:S(2)}) copy-start(s32[1,512]{1,0:T(1,128)} %param.19) | copy-start | bytes 6148
  27.6 4.8 %copy-start.14 = (s32[128]{0:T(128)S(1)}, s32[128]{0:T(128)}, u32[]{:S(2)}) copy-start(s32[128]{0:T(128)} %param.17) | copy-start | bytes 1540
  29.0 15.2 %collective-permute-start = (bf16[1024,128]{1,0:T(8,128)(2,1)}, bf16[1024,128]{1,0:T(8,128)(2,1)}, u32[]{:S(2)}, u32[]{:S(2)}) collective-permute-start(bf16[1024,128]{1,0:T(8,128)(2,1)} %bitcast.4), channel_id=1, source_target_pairs={{0,1},{1,0},{2,3},{3,2},{4,5},{5,4},{6,7},{7,6},{8,9},{9,8},{10,11... | collective-permute-start | bytes 786440 | tf_op jit(solution)/shard_map/ppermute | solution.py:15
  39.7 4.5 %copy-start.3 = (bf16[64,1,16,128]{3,2,1,0:T(8,128)(2,1)S(1)}, bf16[64,1,16,128]{3,2,1,0:T(8,128)(2,1)}, u32[]{:S(2)}) copy-start(bf16[64,1,16,128]{3,2,1,0:T(8,128)(2,1)} %get-tuple-element.36) | copy-start | bytes 786436
  39.7 15.5 %all-to-all-start.1 = ((bf16[4,1024,128]{2,1,0:T(8,128)(2,1)}), bf16[4,1024,128]{2,1,0:T(8,128)(2,1)S(1)}, u32[]{:S(2)}, u32[]{:S(2)}) async-start(bf16[4,1024,128]{2,1,0:T(8,128)(2,1)} %broadcast_in_dim.135), calls=%async_computation.1 | async-start | bytes 2097152 | tf_op jit(solution)/shard_map/all_to_all | solution.py:24
  43.8 56.0 %all-gather.3.cloned.1.call-start = ((), (), s32[]{:S(2)}) async-start(), calls=%async_computation.7 | async-start | bytes 2621440 | tf_op jit(solution)/shard_map/all_gather | solution.py:119
  45.2 0.7 copy-start.4
  45.2 0.8 copy-start.6
  46.9 8.5 %copy-start.5 = (bf16[1024,128]{1,0:T(8,128)(2,1)S(1)}, bf16[1024,128]{1,0:T(8,128)(2,1)}, u32[]{:S(2)}) copy-start(bf16[1024,128]{1,0:T(8,128)(2,1)} %copy-done.4) | copy-start | bytes 786436
  55.1 1.0 copy-start.7
  56.5 0.8 copy-start.8
  57.4 8.6 %collective-permute-start.1 = (f32[128,512]{1,0:T(8,128)S(1)}, f32[128,512]{1,0:T(8,128)}, u32[]{:S(2)}, u32[]{:S(2)}) collective-permute-start(f32[128,512]{1,0:T(8,128)S(1)} %dynamic-slice_bitcast_fusion), channel_id=1, source_target_pairs={{0,1},{1,0},{2,3},{3,2},{4,5},{5,4},{6,7},{7,6},{8,9},{9,8},{10,11... | collective-permute-start | bytes 786440 | tf_op jit(solution)/shard_map/ppermute | solution.py:15
  70.0 23.7 %all-to-all-start.2 = ((bf16[128,2,640]{2,1,0:T(2,128)(2,1)}), bf16[128,2,640]{2,1,0:T(2,128)(2,1)}, u32[]{:S(2)}, u32[]{:S(2)}) async-start(bf16[128,2,640]{2,1,0:T(2,128)(2,1)} %reshape.203), calls=%async_computation.2 | async-start | bytes 655360 | tf_op jit(solution)/shard_map/all_to_all | solution.py:153
  78.8 32.5 %collective-permute-start.2 = (bf16[1024,512]{1,0:T(8,128)(2,1)S(1)}, bf16[1024,512]{1,0:T(8,128)(2,1)}, u32[]{:S(2)}, u32[]{:S(2)}) collective-permute-start(bf16[1024,512]{1,0:T(8,128)(2,1)S(1)} %pad_maximum_fusion.2), channel_id=1, source_target_pairs={{0,1},{1,0},{2,3},{3,2},{4,5},{5,4},{6,7},{7,6},{8,9},{9,8},{10,11... | collective-permute-start | bytes 3145736 | tf_op jit(solution)/shard_map/ppermute | solution.py:15
  95.5 3.0 %copy-start.16 = (bf16[512,512]{1,0:T(8,128)(2,1)S(1)}, bf16[512,512]{1,0:T(8,128)(2,1)}, u32[]{:S(2)}) copy-start(bf16[512,512]{1,0:T(8,128)(2,1)} %convolution_convert_fusion) | copy-start | bytes 1572868
  104.8 21.5 %all-to-all-start.3 = ((bf16[128,2,512]{2,1,0:T(2,128)(2,1)}), bf16[128,2,512]{2,1,0:T(2,128)(2,1)}, u32[]{:S(2)}, u32[]{:S(2)}) async-start(bf16[128,2,512]{2,1,0:T(2,128)(2,1)} %reshape.205), calls=%async_computation.3 | async-start | bytes 524288 | tf_op jit(solution)/shard_map/all_to_all | solution.py:158
  112.7 14.7 %copy-start.15 = (f32[128]{0:T(128)S(1)}, f32[128]{0:T(128)}, u32[]{:S(2)}) copy-start(f32[128]{0:T(128)} %param.21) | copy-start | bytes 1540
  127.4 1.6 copy-start.1
  131.3 10.4 %all-to-all-start.4 = ((bf16[8,136,128]{2,1,0:T(8,128)(2,1)}), bf16[8,136,128]{2,1,0:T(8,128)(2,1)S(1)}, u32[]{:S(2)}, u32[]{:S(2)}) async-start(bf16[8,136,128]{2,1,0:T(8,128)(2,1)} %pad_maximum_fusion.6), calls=%async_computation.4 | async-start | bytes 557056 | tf_op jit(solution)/shard_map/all_to_all | solution.py:24
  144.9 19.5 %all-to-all-start.5 = ((bf16[64,24,128]{2,1,0:T(8,128)(2,1)}), bf16[64,24,128]{2,1,0:T(8,128)(2,1)S(1)}, u32[]{:S(2)}, u32[]{:S(2)}) async-start(bf16[64,24,128]{2,1,0:T(8,128)(2,1)} %pad_maximum_fusion.5), calls=%async_computation.5 | async-start | bytes 786432 | tf_op jit(solution)/shard_map/all_to_all | solution.py:24
  165.1 11.7 %all-to-all-start.6 = ((f32[8,20,128]{2,1,0:T(8,128)}), f32[8,20,128]{2,1,0:T(8,128)S(1)}, u32[]{:S(2)}, u32[]{:S(2)}) async-start(f32[8,20,128]{2,1,0:T(8,128)} %broadcast_in_dim.143), calls=%async_computation.6 | async-start | bytes 196608 | tf_op jit(solution)/shard_map/all_to_all | solution.py:24
Sparse Core Ops, SparseCore 0:
  47.0 31.6 all-gather.2

commit v3 on v2

--- a/solution.py
+++ b/solution.py
@@ -1,6 +1,10 @@
+import functools
+
 import jax
 import jax.numpy as jnp
 from jax import lax
+from jax.experimental import pallas as pl
+from jax.experimental.pallas import tpu as pltpu
 from jax.sharding import Mesh, PartitionSpec as P
 
 logit_scale = 100.0
@@ -50,23 +54,87 @@
     return ordered, used
 
 
-def owner_work(rows, ordered, used, kmax):
-    width = ordered.shape[1]
-    embedded = rows[:, :width]
-    local = rows[:, width : width + 1].astype(f32)
-    target = rows[:, width + 1 : width + 2].astype(f32)
-    columns = jnp.arange(ordered.shape[0], dtype=jnp.int32)[None, :]
-    cluster_of = (columns // kmax).astype(f32)
+def call(kernel, out_shape, *operands):
+    return pl.pallas_call(
+        kernel,
+        out_shape=out_shape,
+        compiler_params=pltpu.CompilerParams(vmem_limit_bytes=24 * 2**20),
+    )(*operands)
+
+
+def owner_kernel(kmax, parts, rows_ref, ordered_ref, used_ref, out_ref):
+    count, (held, width) = rows_ref.shape[0], ordered_ref.shape
+    block = width // parts
+    ordered = ordered_ref[...]
+    labels = rows_ref[:, width:].astype(f32).astype(jnp.int32)
+    local, target = labels[:, 0:1], labels[:, 1:2]
+    columns = lax.broadcasted_iota(jnp.int32, (count, held), 1)
+    first = local * kmax
+    valid = (used_ref[...] > 0) & (columns >= first) & (columns < first + kmax)
     scores = logit_scale * lax.dot_general(
-        embedded, ordered, (((1,), (1,)), ((), ())), preferred_element_type=f32
-    )
-    valid = used & (cluster_of == local)
+        rows_ref[:, :width], ordered, (((1,), (1,)), ((), ())), preferred_element_type=f32
+    )
     highest = jnp.max(jnp.where(valid, scores, -jnp.inf), axis=1, keepdims=True)
     weights = jnp.where(valid, jnp.exp(scores - highest), 0.0)
     probs = weights / jnp.sum(weights, axis=1, keepdims=True)
-    positive = (columns.astype(f32) == local * kmax + target).astype(f32)
+    positive = jnp.where(columns == first + target, 1.0, 0.0)
     coefficients = (logit_scale * (probs - positive)).astype(bf16)
-    return jnp.dot(coefficients, ordered, preferred_element_type=f32).astype(bf16)
+    gradient = jnp.dot(coefficients, ordered, preferred_element_type=f32).astype(bf16)
+    size = 16 * parts
+    row = lax.broadcasted_iota(jnp.int32, (size, size), 0)
+    column = lax.broadcasted_iota(jnp.int32, (size, size), 1)
+    order = jnp.where(column == lax.rem(row, parts) * 16 + lax.div(row, parts), 1.0, 0.0).astype(bf16)
+    for at in range(0, count, 16):
+        some = jnp.concatenate([gradient[at : at + 16, i * block : (i + 1) * block] for i in range(parts)], axis=0)
+        out_ref[at * parts : (at + 16) * parts, :] = jnp.dot(order, some, preferred_element_type=f32).astype(bf16)
+
+
+def gradient_kernel(
+    parts, depth, back_ref, slots_ref, unit_ref, norm_ref, cot_ref, weight_ref, normed_ref, pieces_ref, grad_ref
+):
+    group, rows, block = pieces_ref.shape
+    count = unit_ref.shape[0]
+    back, unit, slots = back_ref[...], unit_ref[...], slots_ref[...]
+    columns = lax.broadcasted_iota(jnp.int32, (count, back.shape[0]), 1)
+    blocks = []
+    for i in range(parts):
+        here = jnp.where(columns == slots * parts + i, 1.0, 0.0).astype(bf16)
+        blocks.append(jnp.dot(here, back, preferred_element_type=f32))
+    unit_grad = cot_ref[...] * jnp.concatenate(blocks, axis=1)
+    along = jnp.sum(unit * unit_grad, axis=1, keepdims=True)
+    proj = ((unit_grad - unit * along) / norm_ref[...]).astype(bf16)
+    window_grad = lax.dot_general(
+        proj, weight_ref[...], (((1,), (1,)), ((), ())), preferred_element_type=f32
+    )
+    grad_ref[...] = window_grad
+    gain = jnp.sum(window_grad * normed_ref[...], axis=0, keepdims=True)
+    bias = jnp.sum(window_grad, axis=0, keepdims=True)
+    place = lax.broadcasted_iota(jnp.int32, (rows - count, block), 0)
+    for g in range(group):
+        tail = jnp.zeros((rows - count, block), f32)
+        values, at = (gain, g) if g < group // 2 else (bias, g - group // 2)
+        for r in range(depth):
+            line = values[:, (at * depth + r) * block : (at * depth + r + 1) * block]
+            high = line.astype(bf16).astype(f32)
+            tail = jnp.where(place == r, high, jnp.where(place == depth + r, line - high, tail))
+        i = g * parts // group
+        pieces_ref[g, :count, :] = proj[:, i * block : (i + 1) * block]
+        pieces_ref[g, count:, :] = tail.astype(bf16)
+
+
+def term_kernel(windows_ref, pieces_ref, out_ref):
+    groups, height, width = windows_ref.shape
+    count = width // 2
+    step = height // 4
+    proj = [
+        jnp.concatenate([pieces_ref[2 * g, :count, :], pieces_ref[2 * g + 1, :count, :]], axis=0)
+        for g in range(groups)
+    ]
+    for at in range(0, height, step):
+        total = jnp.dot(windows_ref[0, at : at + step, :], proj[0], preferred_element_type=f32)
+        for g in range(1, groups):
+            total += jnp.dot(windows_ref[g, at : at + step, :], proj[g], preferred_element_type=f32)
+        out_ref[at : at + step, :] = total.astype(bf16)
 
 
 def body(
@@ -100,7 +168,12 @@
     block = embed_width // n_outer
     columns = lax.dynamic_slice_in_dim(head_weight, outer * block, block, 1)
     columns = gather(columns, ("z", "y")).reshape(half, block)
-    weight_own = side_by_side(gather(columns, "outer"))
+    blocks = [columns] + [swap(columns, "outer", i) for i in range(1, n_outer)]
+    for bit in (1, 2):
+        odd = (outer & bit) > 0
+        blocks = [jnp.where(odd, blocks[i ^ bit], blocks[i]) for i in range(n_outer)]
+    weight_own = jnp.concatenate(blocks, axis=1)
+
 
     widened = feats.astype(f32)
     means = jnp.mean(widened, axis=1, keepdims=True)
@@ -116,7 +189,7 @@
     window_pair = jnp.concatenate(
         [jnp.where(core == 0, window_own, window_sent), jnp.where(core == 0, window_sent, window_own)], axis=1
     )
-    window_all = side_by_side(lax.all_gather(window_pair, "outer", axis=0))
+    window_all = lax.all_gather(window_pair, "outer", axis=0)
 
     ids = jnp.arange(owner_table.shape[0], dtype=jnp.int32)[None, :]
     owners = jnp.sum(jnp.where(image_cluster[:, None] == ids, owner_table[None, :], 0), axis=1)
@@ -132,6 +205,7 @@
     labels = jnp.stack([local, image_target], axis=1).astype(bf16)
     labels = jnp.concatenate([labels, jnp.zeros((count, 126), bf16)], axis=1)
     ordered, used = owner_tables(captions, owner_table, cluster_size[0], cap_index[0], me)
+    weight_own, ordered, used, place, labels = lax.optimization_barrier((weight_own, ordered, used, place, labels))
 
     def by_rows(left, right):
         return lax.dot_general(left, right, (((0,), (0,)), ((), ())), preferred_element_type=f32)
@@ -153,34 +227,37 @@
     received = lax.all_to_all(
         send_rows.reshape(dp_count, capacity, -1), DP, split_axis=0, concat_axis=0, tiled=True
     )
-    gradient = owner_work(received.reshape(dp_count * capacity, -1), ordered, used, kmax)
+    gradient = call(
+        functools.partial(owner_kernel, kmax, n_outer),
+        jax.ShapeDtypeStruct((dp_count * capacity * n_outer, block), bf16),
+        received.reshape(dp_count * capacity, -1),
+        ordered,
+        used.astype(f32),
+    )
     window_all, gradient = lax.optimization_barrier((window_all, gradient))
-    returned = lax.all_to_all(
-        gradient.reshape(dp_count, capacity, embed_width), DP, split_axis=0, concat_axis=0, tiled=True
-    )
-    unit_grad0 = by_rows(place, returned.reshape(dp_count * capacity, embed_width))
-    unit_grad = cotangent[:, None] * unit_grad0
-    proj_grad = (unit_grad - unit * jnp.sum(unit * unit_grad, axis=1, keepdims=True)) / norm_len
-    proj_bf = proj_grad.astype(bf16)
-
-    window_grad = lax.dot_general(
-        proj_bf, full_weight, (((1,), (1,)), ((), ())), preferred_element_type=f32
-    )
-    gain_local = jnp.sum(window_grad * normed_head, axis=0)
-    bias_local = jnp.sum(window_grad, axis=0)
+    returned = exchange(gradient.reshape(dp_count, capacity * n_outer, block), DP).reshape(-1, block)
 
     group = n_outer * nc
-    sums = jnp.concatenate([gain_local, bias_local]).reshape(group, -1, block)
-    depth = sums.shape[1]
-    blocks = jnp.concatenate([proj_bf[:, i * block : (i + 1) * block] for i in range(n_outer)], axis=0)
-    blocks = blocks.reshape(n_outer, 1, count, block)
-    blocks = jnp.broadcast_to(blocks, (n_outer, nc, count, block)).reshape(group, count, block)
-    pieces = exchange(jnp.concatenate([blocks, split_sum(sums, 1)], axis=1), ("outer", "core"))
-    proj_all = pieces[:, :count].reshape(-1, block)
-    sums = jnp.sum(pieces[:, count:].astype(f32), axis=0)
+    depth = 2 * window_width // (group * block)
+    pieces, window_grad = call(
+        functools.partial(gradient_kernel, n_outer, depth),
+        (
+            jax.ShapeDtypeStruct((group, count + 16, block), bf16),
+            jax.ShapeDtypeStruct((count, window_width), f32),
+        ),
+        returned,
+        slots[:, None],
+        unit,
+        norm_len,
+        cotangent[:, None],
+        full_weight,
+        normed_head,
+    )
+    pieces = exchange(pieces, ("outer", "core"))
+    sums = jnp.sum(pieces[:, count : count + 2 * depth].astype(f32), axis=0)
     sums = sums[:depth] + sums[depth:]
 
-    term = jnp.dot(window_all, proj_all, preferred_element_type=f32).astype(bf16)
+    term = call(term_kernel, jax.ShapeDtypeStruct((half, block), bf16), window_all, pieces)
     sums = split_sum(sums, 0)
     sums = jnp.broadcast_to(sums[None], (nz * ny,) + sums.shape)
     pieces = exchange(jnp.concatenate([term.reshape(nz * ny, shard, block), sums], axis=1), ("z", "y"))

time: 186 us -> 185 us (level)
  starting transfers between devices: 62.5 us -> 72.7 us
  local copies, waits for them, and re-layouts: 18.6 us -> 10.5 us
  matrix products: 9.58 us -> 2.4 us
  Pallas kernels: 0 us -> 5.1 us
  other arithmetic: 19.1 us -> 14.6 us
  waiting for transfers between devices: 60.5 us -> 64.2 us
    ppermute x3 -> x6, starting transfers between devices: 12.4 us -> 27.3 us  [swap(): return lax.ppermute(value, axis, [(i, i ^ flip) for i in range(size)])]
    all_to_all x1 -> x0, waiting for transfers between devices: 12.1 us -> none  [body(): lax.all_to_all(gradient.reshape(dp_count, capacity, embed_width), DP, spl...]
    ppermute x3 -> x6, waiting for transfers between devices: 0.01 us -> 7.75 us  [swap(): return lax.ppermute(value, axis, [(i, i ^ flip) for i in range(size)])]
    dot_general x4 -> x0, matrix products: 6.55 us -> none  [the longest x1 2.29 us: body(): jnp.dot(window_all, proj_all, preferred_element_type=f32).astype(bf16)]
    all_to_all x1 -> x0, starting transfers between devices: 6.49 us -> none  [body(): lax.all_to_all(gradient.reshape(dp_count, capacity, embed_width), DP, spl...]
    pallas_call x0 -> x3, Pallas kernels: none -> 5.1 us  [call(): pl.pallas_call(kernel, out_shape=out_shape, compiler_params=pltpu.Compile...]
    all_to_all x1, waiting for transfers between devices: 12 us -> 16.7 us  [body(): lax.all_to_all(send_rows.reshape(dp_count, capacity, -1), DP, split_axis=...]
    all_to_all x5, starting transfers between devices: 36.3 us -> 40.1 us  [exchange(): return lax.all_to_all(pieces, axis, split_axis=0, concat_axis=0, tiled=True)]
  transfers between devices with their start and end apart: 11 -> 13, of which waited for: 7 -> 10; matrix products, arithmetic and copies ran while one was open for 18% -> 10% of each run, Pallas kernels for 0% -> 1%
where the time goes in v3:
time: 185 us; the launch traced here: 184 us
  starting transfers between devices  72.7 us (39%)
  waiting for transfers between devices  64.2 us (35%)
  other arithmetic  14.6 us (8%)
  between operations  14.5 us (8%)
  local copies, waits for them, and re-layouts  10.5 us (6%)
  Pallas kernels  5.1 us (3%)
  matrix products  2.4 us (1%)
    all_to_all x5, starting transfers between devices, exchange(): return lax.all_to_all(pieces, axis, split_axis=0, concat_axis=0, tiled=True)  40.1 us
    all_to_all x5, waiting for transfers between devices, exchange(): return lax.all_to_all(pieces, axis, split_axis=0, concat_axis=0, tiled=True)  39.8 us
    ppermute x6, starting transfers between devices, swap(): return lax.ppermute(value, axis, [(i, i ^ flip) for i in range(size)])  27.3 us
    all_to_all x1, waiting for transfers between devices, body(): lax.all_to_all(send_rows.reshape(dp_count, capacity, -1), DP, split_axis=...  16.7 us
    ppermute x6, waiting for transfers between devices, swap(): return lax.ppermute(value, axis, [(i, i ^ flip) for i in range(size)])  7.75 us
    all_to_all x1, starting transfers between devices, body(): lax.all_to_all(send_rows.reshape(dp_count, capacity, -1), DP, split_axis=...  5.3 us
    pallas_call x3, Pallas kernels, call(): pl.pallas_call(kernel, out_shape=out_shape, compiler_params=pltpu.Compile...  5.1 us
    unnamed x25, local copies, waits for them, and re-layouts  4.39 us
  transfers between devices with their start and end apart: 13, of which 10 were waited for; matrix products, arithmetic and copies ran while one was open for 10% of the time, Pallas kernels for 1%

profile of v3, /device:TPU:1, one launch (start us, length us, event | category | flops | bytes accessed | tf_op | source)
XLA Modules:
  0.0 184.0 jit_solution(14847631672146193175)
XLA Ops:
  7.2 0.8 constant_dynamic-slice_fusion
  8.0 0.7 broadcast_in_dim.56
  8.7 17.1 %all-to-all-start = ((bf16[64,16,128]{2,1,0:T(8,128)(2,1)}), bf16[64,16,128]{2,1,0:T(8,128)(2,1)S(1)}, u32[]{:S(2)}, u32[]{:S(2)}) async-start(bf16[64,16,128]{2,1,0:T(8,128)(2,1)} %broadcast_in_dim.56), calls=%async_computation | async-start | bytes 524288 | tf_op jit(solution)/shard_map/all_to_all | solution.py:28
  25.9 1.3 convert_reduce_fusion
  27.3 0.4 multiply_reduce_fusion
  27.7 1.2 copy-done.3
  29.1 0.3 copy.33
  29.4 2.9 %collective-permute-start = (bf16[1024,128]{1,0:T(8,128)(2,1)S(1)}, bf16[1024,128]{1,0:T(8,128)(2,1)S(1)}, u32[]{:S(2)}, u32[]{:S(2)}) collective-permute-start(bf16[1024,128]{1,0:T(8,128)(2,1)S(1)} %bitcast.75), channel_id=1, source_target_pairs={{0,1},{1,0},{2,3},{3,2},{4,5},{5,4},{6,7},{7,6},{8,9},{9,8},{10,11... | collective-permute-start | bytes 786440 | tf_op jit(solution)/shard_map/ppermute | solution.py:19
  33.5 0.9 pad_maximum_fusion.3
  34.4 4.2 %all-to-all-done = bf16[64,16,128]{2,1,0:T(8,128)(2,1)S(1)} async-done(((bf16[64,16,128]{2,1,0:T(8,128)(2,1)}), bf16[64,16,128]{2,1,0:T(8,128)(2,1)S(1)}, u32[]{:S(2)}, u32[]{:S(2)}) %all-to-all-start) | async-done | bytes 262176 | tf_op jit(solution)/shard_map/all_to_all | solution.py:28
  38.5 4.4 %collective-permute-start.1 = (bf16[1024,128]{1,0:T(8,128)(2,1)S(1)}, bf16[1024,128]{1,0:T(8,128)(2,1)S(1)}, u32[]{:S(2)}, u32[]{:S(2)}) collective-permute-start(bf16[1024,128]{1,0:T(8,128)(2,1)S(1)} %bitcast.68), channel_id=1, source_target_pairs={{0,384},{128,256},{256,128},{384,0},{1,385},{129,257},{257,129},{3... | collective-permute-start | bytes 786440 | tf_op jit(solution)/shard_map/ppermute | solution.py:19
  42.9 2.4 %collective-permute-start.2 = (bf16[1024,128]{1,0:T(8,128)(2,1)S(1)}, bf16[1024,128]{1,0:T(8,128)(2,1)S(1)}, u32[]{:S(2)}, u32[]{:S(2)}) collective-permute-start(bf16[1024,128]{1,0:T(8,128)(2,1)S(1)} %bitcast.69), channel_id=1, source_target_pairs={{0,256},{128,384},{256,0},{384,128},{1,257},{129,385},{257,1},{385... | collective-permute-start | bytes 786440 | tf_op jit(solution)/shard_map/ppermute | solution.py:19
  45.4 2.2 %collective-permute-start.3 = (bf16[1024,128]{1,0:T(8,128)(2,1)S(1)}, bf16[1024,128]{1,0:T(8,128)(2,1)}, u32[]{:S(2)}, u32[]{:S(2)}) collective-permute-start(bf16[1024,128]{1,0:T(8,128)(2,1)S(1)} %bitcast.70), channel_id=1, source_target_pairs={{0,128},{128,0},{256,384},{384,256},{1,129},{129,1},{257,385},{385... | collective-permute-start | bytes 786440 | tf_op jit(solution)/shard_map/ppermute | solution.py:19
  47.7 1.5 gather_fusion
  49.2 0.5 convolution_convert_fusion.ordered_ref
  49.7 1.9 %collective-permute-done.2 = bf16[1024,128]{1,0:T(8,128)(2,1)S(1)} collective-permute-done((bf16[1024,128]{1,0:T(8,128)(2,1)S(1)}, bf16[1024,128]{1,0:T(8,128)(2,1)S(1)}, u32[]{:S(2)}, u32[]{:S(2)}) %collective-permute-start.2) | collective-permute-done | bytes 262176 | tf_op jit(solution)/shard_map/ppermute | solution.py:19
  51.7 4.6 %collective-permute-done.3 = bf16[1024,128]{1,0:T(8,128)(2,1)} collective-permute-done((bf16[1024,128]{1,0:T(8,128)(2,1)S(1)}, bf16[1024,128]{1,0:T(8,128)(2,1)}, u32[]{:S(2)}, u32[]{:S(2)}) %collective-permute-start.3) | collective-permute-done | bytes 262176 | tf_op jit(solution)/shard_map/ppermute | solution.py:19
  56.3 1.0 broadcast_select_fusion.9
  57.3 1.1 pad_maximum_fusion.1
  58.4 1.7 fusion.18
  60.2 13.2 %collective-permute-start.4 = (f32[128,512]{1,0:T(8,128)S(1)}, f32[128,512]{1,0:T(8,128)S(1)}, u32[]{:S(2)}, u32[]{:S(2)}) collective-permute-start(f32[128,512]{1,0:T(8,128)S(1)} %dynamic-slice_bitcast_fusion), channel_id=1, source_target_pairs={{0,1},{1,0},{2,3},{3,2},{4,5},{5,4},{6,7},{7,6},{8,9},{9,8},{10,11... | collective-permute-start | bytes 786440 | tf_op jit(solution)/shard_map/ppermute | solution.py:19
  73.3 1.1 collective-permute-done.4
  74.5 2.3 %collective-permute-start.5 = (bf16[1024,512]{1,0:T(8,128)(2,1)}, bf16[1024,512]{1,0:T(8,128)(2,1)}, u32[]{:S(2)}, u32[]{:S(2)}) collective-permute-start(bf16[1024,512]{1,0:T(8,128)(2,1)} %pad_maximum_fusion.1), channel_id=1, source_target_pairs={{0,1},{1,0},{2,3},{3,2},{4,5},{5,4},{6,7},{7,6},{8,9},{9,8},{10,11... | collective-permute-start | bytes 3145736 | tf_op jit(solution)/shard_map/ppermute | solution.py:19
  77.3 0.9 reshape.181
  78.1 5.3 %all-to-all-start.1 = ((bf16[128,2,640]{2,1,0:T(2,128)(2,1)}), bf16[128,2,640]{2,1,0:T(2,128)(2,1)S(1)}, u32[]{:S(2)}, u32[]{:S(2)}) async-start(bf16[128,2,640]{2,1,0:T(2,128)(2,1)} %reshape.181), calls=%async_computation.1 | async-start | bytes 655360 | tf_op jit(solution)/shard_map/all_to_all | solution.py:227
  83.5 16.7 %all-to-all-done.1 = bf16[128,2,640]{2,1,0:T(2,128)(2,1)S(1)} async-done(((bf16[128,2,640]{2,1,0:T(2,128)(2,1)}), bf16[128,2,640]{2,1,0:T(2,128)(2,1)S(1)}, u32[]{:S(2)}, u32[]{:S(2)}) %all-to-all-start.1) | async-done | bytes 327712 | tf_op jit(solution)/shard_map/all_to_all | solution.py:227
  100.3 2.3 %shard_map.138 = bf16[1024,128]{1,0:T(8,128)(2,1)} custom-call(bf16[256,640]{1,0:T(8,128)(2,1)S(1)} %reshape.182.rows_ref, bf16[512,512]{1,0:T(8,128)(2,1)S(1)} %convolution_convert_fusion.ordered_ref, f32[1,512]{1,0:T(1,128)S(1)} %convert_element_type.61.used_ref), custom_call_target="tpu_custom_call" | custom-call | tf_op jit(solution)/shard_map/pallas_call | solution.py:58
  102.6 5.5 %all-to-all-start.2 = ((bf16[128,8,128]{2,1,0:T(8,128)(2,1)}), bf16[128,8,128]{2,1,0:T(8,128)(2,1)S(1)}, u32[]{:S(2)}, u32[]{:S(2)}) async-start(bf16[128,8,128]{2,1,0:T(8,128)(2,1)} %bitcast.18), calls=%async_computation.2 | async-start | bytes 524288 | tf_op jit(solution)/shard_map/all_to_all | solution.py:28
  108.4 1.7 broadcast_select_fusion.1
  110.1 1.5 pad_maximum_fusion
  111.6 11.8 %all-to-all-done.2 = bf16[128,8,128]{2,1,0:T(8,128)(2,1)S(1)} async-done(((bf16[128,8,128]{2,1,0:T(8,128)(2,1)}), bf16[128,8,128]{2,1,0:T(8,128)(2,1)S(1)}, u32[]{:S(2)}, u32[]{:S(2)}) %all-to-all-start.2) | async-done | bytes 262176 | tf_op jit(solution)/shard_map/all_to_all | solution.py:28
  123.4 1.6 copy-done.1
  125.0 2.1 %shard_map.139 = (bf16[8,144,128]{2,1,0:T(8,128)(2,1)}, f32[128,2048]{1,0:T(8,128)S(1)}) custom-call(bf16[1024,128]{1,0:T(8,128)(2,1)S(1)} %bitcast.64, s32[128,1]{1,0:T(8,128)S(1)} %copy.35.slots_ref, f32[128,512]{1,0:T(8,128)S(1)} %get-tuple-element.31.unit_ref, f32[128,1]{1,0:T(8,128)S(1)} %copy.36.norm_ref, f32[128,1]{1,0:T(8,128)S(1)} %copy.37.cot_ref, ...), custom_call_target="tpu_custom_call" | custom-call | tf_op jit(solution)/shard_map/pallas_call | solution.py:58
  127.1 5.2 %all-to-all-start.3 = ((bf16[8,144,128]{2,1,0:T(8,128)(2,1)}), bf16[8,144,128]{2,1,0:T(8,128)(2,1)S(1)}, u32[]{:S(2)}, u32[]{:S(2)}) async-start(bf16[8,144,128]{2,1,0:T(8,128)(2,1)} %get-tuple-element.25), calls=%async_computation.3 | async-start | bytes 589824 | tf_op jit(solution)/shard_map/all_to_all | solution.py:28
  132.6 6.6 %all-to-all-done.3.pieces_ref = bf16[8,144,128]{2,1,0:T(8,128)(2,1)S(1)} async-done(((bf16[8,144,128]{2,1,0:T(8,128)(2,1)}), bf16[8,144,128]{2,1,0:T(8,128)(2,1)S(1)}, u32[]{:S(2)}, u32[]{:S(2)}) %all-to-all-start.3) | async-done | bytes 294944 | tf_op jit(solution)/shard_map/all_to_all | solution.py:28
  139.2 1.6 copy-done.2
  140.8 0.7 shard_map.140
  141.5 0.8 pad_maximum_fusion.4
  142.3 5.5 %all-to-all-start.4 = ((bf16[64,24,128]{2,1,0:T(8,128)(2,1)}), bf16[64,24,128]{2,1,0:T(8,128)(2,1)}, u32[]{:S(2)}, u32[]{:S(2)}) async-start(bf16[64,24,128]{2,1,0:T(8,128)(2,1)} %pad_maximum_fusion.4), calls=%async_computation.4 | async-start | bytes 786432 | tf_op jit(solution)/shard_map/all_to_all | solution.py:28
  147.8 1.2 fusion.4
  149.2 13.1 %all-to-all-done.4 = bf16[64,24,128]{2,1,0:T(8,128)(2,1)} async-done(((bf16[64,24,128]{2,1,0:T(8,128)(2,1)}), bf16[64,24,128]{2,1,0:T(8,128)(2,1)}, u32[]{:S(2)}, u32[]{:S(2)}) %all-to-all-start.4) | async-done | bytes 393248 | tf_op jit(solution)/shard_map/all_to_all | solution.py:28
  162.4 1.1 convert_reduce_fusion.1
  163.5 0.6 broadcast_in_dim.113
  164.1 6.8 %all-to-all-start.5 = ((f32[8,20,128]{2,1,0:T(8,128)}), f32[8,20,128]{2,1,0:T(8,128)S(1)}, u32[]{:S(2)}, u32[]{:S(2)}) async-start(f32[8,20,128]{2,1,0:T(8,128)} %broadcast_in_dim.113), calls=%async_computation.5 | async-start | bytes 196608 | tf_op jit(solution)/shard_map/all_to_all | solution.py:28
  170.9 0.9 pad_maximum_fusion.2
  171.9 4.1 %all-to-all-done.5 = f32[8,20,128]{2,1,0:T(8,128)S(1)} async-done(((f32[8,20,128]{2,1,0:T(8,128)}), f32[8,20,128]{2,1,0:T(8,128)S(1)}, u32[]{:S(2)}, u32[]{:S(2)}) %all-to-all-start.5) | async-done | bytes 81952 | tf_op jit(solution)/shard_map/all_to_all | solution.py:28
  175.9 0.6 fusion.20
  176.5 0.6 pad_maximum_fusion.5
  (72 shorter events, 3.2 us)
Async XLA Ops:
  7.2 42.1 %copy-start = (bf16[512,512]{1,0:T(8,128)(2,1)S(1)}, bf16[512,512]{1,0:T(8,128)(2,1)}, u32[]{:S(2)}) copy-start(bf16[512,512]{1,0:T(8,128)(2,1)} %param.15) | copy-start | bytes 1572868
  7.2 20.1 %copy-start.4 = (bf16[128,3072]{1,0:T(8,128)(2,1)S(1)}, bf16[128,3072]{1,0:T(8,128)(2,1)}, u32[]{:S(2)}) copy-start(bf16[128,3072]{1,0:T(8,128)(2,1)} %param.11) | copy-start | bytes 2359300
  7.2 21.6 %copy-start.5 = (f32[2048]{0:T(1024)S(1)}, f32[2048]{0:T(1024)}, u32[]{:S(2)}) copy-start(f32[2048]{0:T(1024)} %param.12) | copy-start | bytes 24580
  7.2 21.6 %copy-start.7 = (f32[2048]{0:T(1024)S(1)}, f32[2048]{0:T(1024)}, u32[]{:S(2)}) copy-start(f32[2048]{0:T(1024)} %param.13) | copy-start | bytes 24580
  8.7 29.8 %all-to-all-start = ((bf16[64,16,128]{2,1,0:T(8,128)(2,1)}), bf16[64,16,128]{2,1,0:T(8,128)(2,1)S(1)}, u32[]{:S(2)}, u32[]{:S(2)}) async-start(bf16[64,16,128]{2,1,0:T(8,128)(2,1)} %broadcast_in_dim.56), calls=%async_computation | async-start | bytes 524288 | tf_op jit(solution)/shard_map/all_to_all | solution.py:28
  25.9 76.7 %all-gather.3.cloned.1.call-start = ((), (), s32[]{:S(2)}) async-start(), calls=%async_computation.6 | async-start | bytes 2621440 | tf_op jit(solution)/shard_map/all_gather | solution.py:192
  27.6 1.2 copy-start.3
  28.8 3.4 %copy-start.6 = (s32[1,512]{1,0:T(1,128)S(1)}, s32[1,512]{1,0:T(1,128)}, u32[]{:S(2)}) copy-start(s32[1,512]{1,0:T(1,128)} %param.18) | copy-start | bytes 6148
  28.8 3.5 %copy-start.8 = (s32[128]{0:T(128)S(1)}, s32[128]{0:T(128)}, u32[]{:S(2)}) copy-start(s32[128]{0:T(128)} %param.16) | copy-start | bytes 1540
  28.8 4.2 %copy-start.11 = (s32[128]{0:T(128)S(1)}, s32[128]{0:T(128)}, u32[]{:S(2)}) copy-start(s32[128]{0:T(128)} %param.17) | copy-start | bytes 1540
  28.8 4.3 %copy-start.9 = (s32[1,512]{1,0:T(1,128)S(1)}, s32[1,512]{1,0:T(1,128)}, u32[]{:S(2)}) copy-start(s32[1,512]{1,0:T(1,128)} %param.19) | copy-start | bytes 6148
  29.4 4.0 %collective-permute-start = (bf16[1024,128]{1,0:T(8,128)(2,1)S(1)}, bf16[1024,128]{1,0:T(8,128)(2,1)S(1)}, u32[]{:S(2)}, u32[]{:S(2)}) collective-permute-start(bf16[1024,128]{1,0:T(8,128)(2,1)S(1)} %bitcast.75), channel_id=1, source_target_pairs={{0,1},{1,0},{2,3},{3,2},{4,5},{5,4},{6,7},{7,6},{8,9},{9,8},{10,11... | collective-permute-start | bytes 786440 | tf_op jit(solution)/shard_map/ppermute | solution.py:19
  38.5 11.2 %collective-permute-start.1 = (bf16[1024,128]{1,0:T(8,128)(2,1)S(1)}, bf16[1024,128]{1,0:T(8,128)(2,1)S(1)}, u32[]{:S(2)}, u32[]{:S(2)}) collective-permute-start(bf16[1024,128]{1,0:T(8,128)(2,1)S(1)} %bitcast.68), channel_id=1, source_target_pairs={{0,384},{128,256},{256,128},{384,0},{1,385},{129,257},{257,129},{3... | collective-permute-start | bytes 786440 | tf_op jit(solution)/shard_map/ppermute | solution.py:19
  42.9 8.7 %collective-permute-start.2 = (bf16[1024,128]{1,0:T(8,128)(2,1)S(1)}, bf16[1024,128]{1,0:T(8,128)(2,1)S(1)}, u32[]{:S(2)}, u32[]{:S(2)}) collective-permute-start(bf16[1024,128]{1,0:T(8,128)(2,1)S(1)} %bitcast.69), channel_id=1, source_target_pairs={{0,256},{128,384},{256,0},{384,128},{1,257},{129,385},{257,1},{385... | collective-permute-start | bytes 786440 | tf_op jit(solution)/shard_map/ppermute | solution.py:19
  45.4 10.9 %collective-permute-start.3 = (bf16[1024,128]{1,0:T(8,128)(2,1)S(1)}, bf16[1024,128]{1,0:T(8,128)(2,1)}, u32[]{:S(2)}, u32[]{:S(2)}) collective-permute-start(bf16[1024,128]{1,0:T(8,128)(2,1)S(1)} %bitcast.70), channel_id=1, source_target_pairs={{0,128},{128,0},{256,384},{384,256},{1,129},{129,1},{257,385},{385... | collective-permute-start | bytes 786440 | tf_op jit(solution)/shard_map/ppermute | solution.py:19
  60.2 14.3 %collective-permute-start.4 = (f32[128,512]{1,0:T(8,128)S(1)}, f32[128,512]{1,0:T(8,128)S(1)}, u32[]{:S(2)}, u32[]{:S(2)}) collective-permute-start(f32[128,512]{1,0:T(8,128)S(1)} %dynamic-slice_bitcast_fusion), channel_id=1, source_target_pairs={{0,1},{1,0},{2,3},{3,2},{4,5},{5,4},{6,7},{7,6},{8,9},{9,8},{10,11... | collective-permute-start | bytes 786440 | tf_op jit(solution)/shard_map/ppermute | solution.py:19
  74.5 33.9 %collective-permute-start.5 = (bf16[1024,512]{1,0:T(8,128)(2,1)}, bf16[1024,512]{1,0:T(8,128)(2,1)}, u32[]{:S(2)}, u32[]{:S(2)}) collective-permute-start(bf16[1024,512]{1,0:T(8,128)(2,1)} %pad_maximum_fusion.1), channel_id=1, source_target_pairs={{0,1},{1,0},{2,3},{3,2},{4,5},{5,4},{6,7},{7,6},{8,9},{9,8},{10,11... | collective-permute-start | bytes 3145736 | tf_op jit(solution)/shard_map/ppermute | solution.py:19
  77.0 31.1 %copy-start.10 = (f32[128]{0:T(128)S(1)}, f32[128]{0:T(128)}, u32[]{:S(2)}) copy-start(f32[128]{0:T(128)} %param.21) | copy-start | bytes 1540
  78.1 22.0 %all-to-all-start.1 = ((bf16[128,2,640]{2,1,0:T(2,128)(2,1)}), bf16[128,2,640]{2,1,0:T(2,128)(2,1)S(1)}, u32[]{:S(2)}, u32[]{:S(2)}) async-start(bf16[128,2,640]{2,1,0:T(2,128)(2,1)} %reshape.181), calls=%async_computation.1 | async-start | bytes 655360 | tf_op jit(solution)/shard_map/all_to_all | solution.py:227
  102.6 20.8 %all-to-all-start.2 = ((bf16[128,8,128]{2,1,0:T(8,128)(2,1)}), bf16[128,8,128]{2,1,0:T(8,128)(2,1)S(1)}, u32[]{:S(2)}, u32[]{:S(2)}) async-start(bf16[128,8,128]{2,1,0:T(8,128)(2,1)} %bitcast.18), calls=%async_computation.2 | async-start | bytes 524288 | tf_op jit(solution)/shard_map/all_to_all | solution.py:28
  123.4 1.6 copy-start.1
  127.1 12.0 %all-to-all-start.3 = ((bf16[8,144,128]{2,1,0:T(8,128)(2,1)}), bf16[8,144,128]{2,1,0:T(8,128)(2,1)S(1)}, u32[]{:S(2)}, u32[]{:S(2)}) async-start(bf16[8,144,128]{2,1,0:T(8,128)(2,1)} %get-tuple-element.25), calls=%async_computation.3 | async-start | bytes 589824 | tf_op jit(solution)/shard_map/all_to_all | solution.py:28
  139.2 1.6 copy-start.2
  142.3 20.1 %all-to-all-start.4 = ((bf16[64,24,128]{2,1,0:T(8,128)(2,1)}), bf16[64,24,128]{2,1,0:T(8,128)(2,1)}, u32[]{:S(2)}, u32[]{:S(2)}) async-start(bf16[64,24,128]{2,1,0:T(8,128)(2,1)} %pad_maximum_fusion.4), calls=%async_computation.4 | async-start | bytes 786432 | tf_op jit(solution)/shard_map/all_to_all | solution.py:28
  164.1 11.8 %all-to-all-start.5 = ((f32[8,20,128]{2,1,0:T(8,128)}), f32[8,20,128]{2,1,0:T(8,128)S(1)}, u32[]{:S(2)}, u32[]{:S(2)}) async-start(f32[8,20,128]{2,1,0:T(8,128)} %broadcast_in_dim.113), calls=%async_computation.5 | async-start | bytes 196608 | tf_op jit(solution)/shard_map/all_to_all | solution.py:28
Sparse Core Ops, SparseCore 0:
  34.5 41.0 all-gather.2

commit v4 on v3

--- a/solution.py
+++ b/solution.py
@@ -26,15 +26,6 @@
 
 def exchange(pieces, axis):
     return lax.all_to_all(pieces, axis, split_axis=0, concat_axis=0, tiled=True)
-
-
-def gather(value, axis):
-    size = lax.axis_size(axis)
-    return exchange(jnp.broadcast_to(value[None], (size,) + value.shape), axis)
-
-
-def side_by_side(blocks):
-    return jnp.concatenate([blocks[i] for i in range(blocks.shape[0])], axis=1)
 
 
 def owner_tables(captions, owner_table, size_table, index_table, me):
@@ -54,12 +45,81 @@
     return ordered, used
 
 
-def call(kernel, out_shape, *operands):
+def by_rows(left, right):
+    return lax.dot_general(left, right, (((0,), (0,)), ((), ())), preferred_element_type=f32)
+
+
+vmem = pl.BlockSpec(memory_space=pltpu.VMEM)
+smem = pl.BlockSpec(memory_space=pltpu.SMEM)
+anywhere = pl.BlockSpec(memory_space=pl.ANY)
+
+
+def call(kernel, out_shape, *operands, places=None, scratch=(), room=12):
     return pl.pallas_call(
         kernel,
         out_shape=out_shape,
-        compiler_params=pltpu.CompilerParams(vmem_limit_bytes=24 * 2**20),
+        in_specs=places or [vmem] * len(operands),
+        scratch_shapes=scratch,
+        compiler_params=pltpu.CompilerParams(vmem_limit_bytes=room * 2**20),
     )(*operands)
+
+
+def first_kernel(at_ref, weight_ref, out_ref):
+    block = out_ref.shape[2]
+    value = weight_ref[:, pl.ds(pl.multiple_of(at_ref[0] * block, block), block)]
+    out_ref[...] = jnp.broadcast_to(value[None], out_ref.shape)
+
+
+def partial_kernel(parts, at_ref, own_ref, sent_ref, *refs):
+    blocks, (own_out, other_out, weight_out, here, sems) = refs[:parts], refs[parts:]
+    copies = [pltpu.make_async_copy(blocks[i], here.at[i], sems.at[i]) for i in range(parts)]
+    for copy in copies:
+        copy.start()
+    own, sent = own_ref[...], sent_ref[...]
+    for i in range(parts):
+        width = here.shape[2]
+        columns = pl.ds(pl.multiple_of((at_ref[0] ^ i) * width, width), width)
+        copies[i].wait()
+        block = here[i]
+        other_out[:, columns] = by_rows(sent, block)
+        own_out[:, columns] = by_rows(own, block)
+        weight_out[:, columns] = block
+
+
+def payload_kernel(own_ref, sent_ref, slots_ref, labels_ref, unit_ref, norm_ref, out_ref):
+    projected = own_ref[...] + sent_ref[...]
+    norm_len = jnp.sqrt(jnp.sum(projected * projected, axis=1, keepdims=True) + 1e-06)
+    unit = projected / norm_len
+    unit_ref[...] = unit
+    norm_ref[...] = norm_len
+    rows, width = out_ref.shape[0], unit.shape[1]
+    here = lax.broadcasted_iota(jnp.int32, (rows, unit.shape[0]), 0) == slots_ref[...]
+    place = jnp.where(here, 1.0, 0.0).astype(bf16)
+    out_ref[:, :width] = jnp.dot(place, unit.astype(bf16), preferred_element_type=f32).astype(bf16)
+    out_ref[:, width:] = jnp.dot(place, labels_ref[...], preferred_element_type=f32).astype(bf16)
+
+
+def sum_kernel(depth, pieces_ref, out_ref):
+    size = out_ref.shape[1]
+    total = pieces_ref[0].astype(f32)
+    for i in range(1, pieces_ref.shape[0]):
+        total += pieces_ref[i].astype(f32)
+    tail = total[size - 2 * depth :]
+    tail = tail + pltpu.roll(tail, depth, 0)
+    for i in range(out_ref.shape[0]):
+        out_ref[i, : size - 2 * depth, :] = total[: size - 2 * depth]
+        out_ref[i, size - 2 * depth :, :] = tail
+
+
+def last_kernel(depth, at_ref, last_ref, weight_ref, gain_ref, bias_ref):
+    group, _, block = last_ref.shape
+    shard, width = weight_ref.shape
+    cores = group * block // width
+    for i in range(width // block):
+        weight_ref[:, i * block : (i + 1) * block] = last_ref[i * cores + at_ref[1], :shard, :]
+    for i in range(group // 2):
+        gain_ref[i * depth : (i + 1) * depth, :] = last_ref[i, shard : shard + depth, :]
+        bias_ref[i * depth : (i + 1) * depth, :] = last_ref[i + group // 2, shard : shard + depth, :]
 
 
 def owner_kernel(kmax, parts, rows_ref, ordered_ref, used_ref, out_ref):
@@ -90,10 +150,32 @@
 
 
 def gradient_kernel(
-    parts, depth, back_ref, slots_ref, unit_ref, norm_ref, cot_ref, weight_ref, normed_ref, pieces_ref, grad_ref
+    parts,
+    depth,
+    back_ref,
+    slots_ref,
+    unit_ref,
+    norm_ref,
+    cot_ref,
+    weight_ref,
+    normed_ref,
+    pieces_ref,
+    grad_ref,
+    weight_here,
+    normed_here,
+    sems,
 ):
     group, rows, block = pieces_ref.shape
     count = unit_ref.shape[0]
+    steps = sems.shape[1]
+    step = weight_ref.shape[0] // steps
+    copies = []
+    for j in range(steps):
+        some = pl.ds(j * step, step)
+        copies.append(pltpu.make_async_copy(weight_ref.at[some, :], weight_here.at[some, :], sems.at[0, j]))
+        copies.append(pltpu.make_async_copy(normed_ref.at[:, some], normed_here.at[:, some], sems.at[1, j]))
+    for copy in copies:
+        copy.start()
     back, unit, slots = back_ref[...], unit_ref[...], slots_ref[...]
     columns = lax.broadcasted_iota(jnp.int32, (count, back.shape[0]), 1)
     blocks = []
@@ -103,18 +185,24 @@
     unit_grad = cot_ref[...] * jnp.concatenate(blocks, axis=1)
     along = jnp.sum(unit * unit_grad, axis=1, keepdims=True)
     proj = ((unit_grad - unit * along) / norm_ref[...]).astype(bf16)
-    window_grad = lax.dot_general(
-        proj, weight_ref[...], (((1,), (1,)), ((), ())), preferred_element_type=f32
-    )
-    grad_ref[...] = window_grad
-    gain = jnp.sum(window_grad * normed_ref[...], axis=0, keepdims=True)
-    bias = jnp.sum(window_grad, axis=0, keepdims=True)
+    gain, bias = [], []
+    for j in range(steps):
+        some = slice(j * step, (j + 1) * step)
+        copies[2 * j].wait()
+        part = lax.dot_general(
+            proj, weight_here[some, :], (((1,), (1,)), ((), ())), preferred_element_type=f32
+        )
+        grad_ref[:, some] = part
+        copies[2 * j + 1].wait()
+        gain.append(jnp.sum(part * normed_here[:, some], axis=0, keepdims=True))
+        bias.append(jnp.sum(part, axis=0, keepdims=True))
     place = lax.broadcasted_iota(jnp.int32, (rows - count, block), 0)
     for g in range(group):
         tail = jnp.zeros((rows - count, block), f32)
         values, at = (gain, g) if g < group // 2 else (bias, g - group // 2)
         for r in range(depth):
-            line = values[:, (at * depth + r) * block : (at * depth + r + 1) * block]
+            begin = (at * depth + r) * block
+            line = values[begin // step][:, begin % step : begin % step + block]
             high = line.astype(bf16).astype(f32)
             tail = jnp.where(place == r, high, jnp.where(place == depth + r, line - high, tail))
         i = g * parts // group
@@ -122,19 +210,22 @@
         pieces_ref[g, count:, :] = tail.astype(bf16)
 
 
-def term_kernel(windows_ref, pieces_ref, out_ref):
-    groups, height, width = windows_ref.shape
+def term_kernel(windows_ref, pieces_ref, out_ref, here, total, sems):
+    groups, _, width = windows_ref.shape
     count = width // 2
-    step = height // 4
-    proj = [
-        jnp.concatenate([pieces_ref[2 * g, :count, :], pieces_ref[2 * g + 1, :count, :]], axis=0)
-        for g in range(groups)
-    ]
-    for at in range(0, height, step):
-        total = jnp.dot(windows_ref[0, at : at + step, :], proj[0], preferred_element_type=f32)
-        for g in range(1, groups):
-            total += jnp.dot(windows_ref[g, at : at + step, :], proj[g], preferred_element_type=f32)
-        out_ref[at : at + step, :] = total.astype(bf16)
+    copies = [pltpu.make_async_copy(windows_ref.at[g], here.at[g], sems.at[g]) for g in range(groups)]
+    for copy in copies:
+        copy.start()
+    for g in range(groups):
+        proj = jnp.concatenate([pieces_ref[2 * g, :count, :], pieces_ref[2 * g + 1, :count, :]], axis=0)
+        copies[g].wait()
+        product = jnp.dot(here[g], proj, preferred_element_type=f32)
+        if g == 0:
+            total[...] = product
+        elif g < groups - 1:
+            total[...] += product
+        else:
+            out_ref[...] = (total[...] + product).astype(bf16)
 
 
 def body(
@@ -166,14 +257,15 @@
     outer = lax.axis_index("outer")
     n_outer = lax.axis_size("outer")
     block = embed_width // n_outer
-    columns = lax.dynamic_slice_in_dim(head_weight, outer * block, block, 1)
-    columns = gather(columns, ("z", "y")).reshape(half, block)
-    blocks = [columns] + [swap(columns, "outer", i) for i in range(1, n_outer)]
-    for bit in (1, 2):
-        odd = (outer & bit) > 0
-        blocks = [jnp.where(odd, blocks[i ^ bit], blocks[i]) for i in range(n_outer)]
-    weight_own = jnp.concatenate(blocks, axis=1)
-
+    at = jnp.stack([outer, core])
+    columns = call(
+        first_kernel,
+        jax.ShapeDtypeStruct((nz * ny, shard, block), bf16),
+        at,
+        head_weight,
+        places=[smem, vmem],
+    )
+    columns = exchange(columns, ("z", "y")).reshape(half, block)
 
     widened = feats.astype(f32)
     means = jnp.mean(widened, axis=1, keepdims=True)
@@ -185,12 +277,12 @@
     by_feature = window_bf.T.reshape(nz * ny, nc, shard, count)
     window_own = lax.dynamic_index_in_dim(by_feature, core, 1, keepdims=False).reshape(half, count)
     window_other = lax.dynamic_index_in_dim(by_feature, 1 - core, 1, keepdims=False).reshape(half, count)
+    columns, window_other = lax.optimization_barrier((columns, window_other))
+    blocks = [columns] + [swap(columns, "outer", i) for i in range(1, n_outer)]
     window_sent = swap(window_other, "core", 1)
     window_pair = jnp.concatenate(
         [jnp.where(core == 0, window_own, window_sent), jnp.where(core == 0, window_sent, window_own)], axis=1
     )
-    window_all = lax.all_gather(window_pair, "outer", axis=0)
-
     ids = jnp.arange(owner_table.shape[0], dtype=jnp.int32)[None, :]
     owners = jnp.sum(jnp.where(image_cluster[:, None] == ids, owner_table[None, :], 0), axis=1)
     local = jnp.sum(
@@ -201,32 +293,42 @@
         ((owners[:, None] == owners[None, :]) & (images[None, :] < images[:, None])).astype(jnp.int32), axis=1
     )
     slots = owners * capacity + ranks
-    place = (jnp.arange(dp_count * capacity, dtype=jnp.int32)[:, None] == slots[None, :]).astype(bf16)
     labels = jnp.stack([local, image_target], axis=1).astype(bf16)
     labels = jnp.concatenate([labels, jnp.zeros((count, 126), bf16)], axis=1)
     ordered, used = owner_tables(captions, owner_table, cluster_size[0], cap_index[0], me)
-    weight_own, ordered, used, place, labels = lax.optimization_barrier((weight_own, ordered, used, place, labels))
-
-    def by_rows(left, right):
-        return lax.dot_general(left, right, (((0,), (0,)), ((), ())), preferred_element_type=f32)
-
-    partial = by_rows(window_pair, weight_own).reshape(nc, count, embed_width)
-    partial_own = lax.dynamic_index_in_dim(partial, core, 0, keepdims=False)
-    partial_other = lax.dynamic_index_in_dim(partial, 1 - core, 0, keepdims=False)
+
+    partial_own, partial_other, weight_own = call(
+        functools.partial(partial_kernel, n_outer),
+        (
+            jax.ShapeDtypeStruct((count, embed_width), f32),
+            jax.ShapeDtypeStruct((count, embed_width), f32),
+            jax.ShapeDtypeStruct((half, embed_width), bf16),
+        ),
+        at,
+        window_own,
+        window_sent,
+        *blocks,
+        places=[smem] + [vmem] * 2 + [anywhere] * n_outer,
+        scratch=[pltpu.VMEM((n_outer, half, block), bf16), pltpu.SemaphoreType.DMA((n_outer,))],
+    )
     partial_sent = swap(partial_other, "core", 1)
-    projected = partial_own + partial_sent
-    weight_own, projected = lax.optimization_barrier((weight_own, projected))
-    weight_other = swap(weight_own, "core", 1)
-    first = jnp.where(core == 0, weight_own, weight_other).reshape(nz * ny, 1, shard, embed_width)
-    second = jnp.where(core == 0, weight_other, weight_own).reshape(nz * ny, 1, shard, embed_width)
-    full_weight = jnp.concatenate([first, second], axis=1).reshape(window_width, embed_width)
-    norm_len = jnp.sqrt(jnp.sum(projected * projected, axis=1, keepdims=True) + 1e-06)
-    unit = projected / norm_len
-    payload = jnp.concatenate([unit.astype(bf16), labels], axis=1)
-    send_rows = jnp.dot(place, payload, preferred_element_type=f32).astype(bf16)
-    received = lax.all_to_all(
-        send_rows.reshape(dp_count, capacity, -1), DP, split_axis=0, concat_axis=0, tiled=True
-    )
+    unit, norm_len, send_rows = call(
+        payload_kernel,
+        (
+            jax.ShapeDtypeStruct((count, embed_width), f32),
+            jax.ShapeDtypeStruct((count, 1), f32),
+            jax.ShapeDtypeStruct((dp_count * capacity, embed_width + 128), bf16),
+        ),
+        partial_own,
+        partial_sent,
+        slots[None, :],
+        labels,
+    )
+    send_rows = send_rows.reshape(dp_count, capacity, -1)
+
+    send_rows, window_pair = lax.optimization_barrier((send_rows, window_pair))
+    window_all = lax.all_gather(window_pair, "outer", axis=0)
+    received = exchange(send_rows, DP)
     gradient = call(
         functools.partial(owner_kernel, kmax, n_outer),
         jax.ShapeDtypeStruct((dp_count * capacity * n_outer, block), bf16),
@@ -234,7 +336,11 @@
         ordered,
         used.astype(f32),
     )
-    window_all, gradient = lax.optimization_barrier((window_all, gradient))
+    gradient, weight_own = lax.optimization_barrier((gradient, weight_own))
+    weight_other = swap(weight_own, "core", 1)
+    first = jnp.where(core == 0, weight_own, weight_other).reshape(nz * ny, 1, shard, embed_width)
+    second = jnp.where(core == 0, weight_other, weight_own).reshape(nz * ny, 1, shard, embed_width)
+    full_weight = jnp.concatenate([first, second], axis=1).reshape(window_width, embed_width)
     returned = exchange(gradient.reshape(dp_count, capacity * n_outer, block), DP).reshape(-1, block)
 
     group = n_outer * nc
@@ -252,23 +358,52 @@
         cotangent[:, None],
         full_weight,
         normed_head,
+        places=[vmem] * 5 + [anywhere] * 2,
+        scratch=[
+            pltpu.VMEM((window_width, embed_width), bf16),
+            pltpu.VMEM((count, window_width), f32),
+            pltpu.SemaphoreType.DMA((2, 4)),
+        ],
+        room=50,
     )
     pieces = exchange(pieces, ("outer", "core"))
     sums = jnp.sum(pieces[:, count : count + 2 * depth].astype(f32), axis=0)
     sums = sums[:depth] + sums[depth:]
 
-    term = call(term_kernel, jax.ShapeDtypeStruct((half, block), bf16), window_all, pieces)
+    term = call(
+        term_kernel,
+        jax.ShapeDtypeStruct((half, block), bf16),
+        window_all,
+        pieces,
+        places=[anywhere, vmem],
+        scratch=[
+            pltpu.VMEM((n_outer, half, nc * count), bf16),
+            pltpu.VMEM((half, block), f32),
+            pltpu.SemaphoreType.DMA((n_outer,)),
+        ],
+        room=57,
+    )
     sums = split_sum(sums, 0)
     sums = jnp.broadcast_to(sums[None], (nz * ny,) + sums.shape)
     pieces = exchange(jnp.concatenate([term.reshape(nz * ny, shard, block), sums], axis=1), ("z", "y"))
-    pieces = jnp.sum(pieces.astype(f32), axis=0)
-    sums = pieces[shard : shard + depth] + pieces[shard + depth :]
-
-    last = gather(jnp.concatenate([pieces[:shard], sums], axis=0), ("outer", "core"))
-    last = last.reshape(n_outer, nc, shard + depth, block)
-    weight_grad = side_by_side(lax.dynamic_index_in_dim(last[:, :, :shard], core, 1, keepdims=False))
-    sums = last[:, :, shard:].reshape(2, window_width)
-    gain_grad, bias_grad = sums[0], sums[1]
+
+    pieces = call(
+        functools.partial(sum_kernel, depth),
+        jax.ShapeDtypeStruct((group, shard + 2 * depth, block), f32),
+        pieces,
+    )
+    weight_grad, gain_grad, bias_grad = call(
+        functools.partial(last_kernel, depth),
+        (
+            jax.ShapeDtypeStruct((shard, embed_width), f32),
+            jax.ShapeDtypeStruct((window_width // block, block), f32),
+            jax.ShapeDtypeStruct((window_width // block, block), f32),
+        ),
+        at,
+        exchange(pieces, ("outer", "core")),
+        places=[smem, vmem],
+    )
+    gain_grad, bias_grad = gain_grad.reshape(window_width), bias_grad.reshape(window_width)
 
     scaled_grad = window_grad * ln_gain
     first_mean = jnp.sum(scaled_grad, axis=1, keepdims=True) / width

time: 185 us -> 187 us (1.011)
  Pallas kernels: 5.1 us -> 15.9 us
  starting transfers between devices: 72.7 us -> 67.8 us
  waiting for transfers between devices: 64.2 us -> 59.3 us
  matrix products: 2.4 us -> 0.48 us
    all_to_all x1 -> x0, waiting for transfers between devices: 16.7 us -> none  [body(): lax.all_to_all(send_rows.reshape(dp_count, capacity, -1), DP, split_axis=...]
    all_to_all x5 -> x6, waiting for transfers between devices: 39.8 us -> 54.7 us  [exchange(): return lax.all_to_all(pieces, axis, split_axis=0, concat_axis=0, tiled=True)]
    pallas_call x3 -> x8, Pallas kernels: 5.1 us -> 15.9 us  [call(): pl.pallas_call(kernel, out_shape=out_shape, in_specs=places or [vmem] * l...]
    all_to_all x5 -> x6, starting transfers between devices: 40.1 us -> 46.1 us  [exchange(): return lax.all_to_all(pieces, axis, split_axis=0, concat_axis=0, tiled=True)]
    ppermute x6, starting transfers between devices: 27.3 us -> 21.6 us  [swap(): return lax.ppermute(value, axis, [(i, i ^ flip) for i in range(size)])]
    all_to_all x1 -> x0, starting transfers between devices: 5.3 us -> none  [body(): lax.all_to_all(send_rows.reshape(dp_count, capacity, -1), DP, split_axis=...]
    ppermute x6, waiting for transfers between devices: 7.75 us -> 3.86 us  [swap(): return lax.ppermute(value, axis, [(i, i ^ flip) for i in range(size)])]
    unnamed x25 -> x46, local copies, waits for them, and re-layouts: 4.39 us -> 8.1 us
  transfers between devices with their start and end apart: 13 -> 13, of which waited for: 10 -> 9; matrix products, arithmetic and copies ran while one was open for 10% -> 9% of each run, Pallas kernels for 1% -> 3%
where the time goes in v4:
time: 187 us; the launch traced here: 186 us
  starting transfers between devices  67.8 us (36%)
  waiting for transfers between devices  59.3 us (32%)
  Pallas kernels  15.9 us (9%)
  other arithmetic  15.3 us (8%)
  between operations  14.5 us (8%)
  local copies, waits for them, and re-layouts  12.3 us (7%)
    all_to_all x6, waiting for transfers between devices, exchange(): return lax.all_to_all(pieces, axis, split_axis=0, concat_axis=0, tiled=True)  54.7 us
    all_to_all x6, starting transfers between devices, exchange(): return lax.all_to_all(pieces, axis, split_axis=0, concat_axis=0, tiled=True)  46.1 us
    ppermute x6, starting transfers between devices, swap(): return lax.ppermute(value, axis, [(i, i ^ flip) for i in range(size)])  21.6 us
    pallas_call x8, Pallas kernels, call(): pl.pallas_call(kernel, out_shape=out_shape, in_specs=places or [vmem] * l...  15.9 us
    unnamed x46, local copies, waits for them, and re-layouts  8.1 us
    ppermute x6, waiting for transfers between devices, swap(): return lax.ppermute(value, axis, [(i, i ^ flip) for i in range(size)])  3.86 us
  transfers between devices with their start and end apart: 13, of which 9 were waited for; matrix products, arithmetic and copies ran while one was open for 9% of the time, Pallas kernels for 3%

profile of v4, /device:TPU:1, one launch (start us, length us, event | category | flops | bytes accessed | tf_op | source)
XLA Modules:
  0.0 185.5 jit_solution(4115237413875375293)
XLA Ops:
  7.3 0.8 copy-done.13
  8.0 1.3 shard_map.138
  9.3 17.1 %all-to-all-start = ((bf16[64,16,128]{2,1,0:T(8,128)(2,1)}), bf16[64,16,128]{2,1,0:T(8,128)(2,1)S(1)}, u32[]{:S(2)}, u32[]{:S(2)}) async-start(bf16[64,16,128]{2,1,0:T(8,128)(2,1)} %shard_map.138), calls=%async_computation | async-start | bytes 524288 | tf_op jit(solution)/shard_map/all_to_all | solution.py:28
  26.5 1.3 convert_reduce_fusion
  27.9 1.4 multiply_reduce_fusion
  29.9 1.4 fusion
  32.1 7.1 %all-to-all-done = bf16[64,16,128]{2,1,0:T(8,128)(2,1)S(1)} async-done(((bf16[64,16,128]{2,1,0:T(8,128)(2,1)}), bf16[64,16,128]{2,1,0:T(8,128)(2,1)S(1)}, u32[]{:S(2)}, u32[]{:S(2)}) %all-to-all-start) | async-done | bytes 262176 | tf_op jit(solution)/shard_map/all_to_all | solution.py:28
  39.1 3.1 %collective-permute-start.1 = (bf16[1024,128]{1,0:T(8,128)(2,1)S(1)}, bf16[1024,128]{1,0:T(8,128)(2,1)S(1)}, u32[]{:S(2)}, u32[]{:S(2)}) collective-permute-start(bf16[1024,128]{1,0:T(8,128)(2,1)S(1)} %bitcast.44), channel_id=1, source_target_pairs={{0,128},{128,0},{256,384},{384,256},{1,129},{129,1},{257,385},{385... | collective-permute-start | bytes 786440 | tf_op jit(solution)/shard_map/ppermute | solution.py:19
  42.2 4.4 %collective-permute-start.2 = (bf16[1024,128]{1,0:T(8,128)(2,1)S(1)}, bf16[1024,128]{1,0:T(8,128)(2,1)S(1)}, u32[]{:S(2)}, u32[]{:S(2)}) collective-permute-start(bf16[1024,128]{1,0:T(8,128)(2,1)S(1)} %bitcast.45), channel_id=1, source_target_pairs={{0,256},{128,384},{256,0},{384,128},{1,257},{129,385},{257,1},{385... | collective-permute-start | bytes 786440 | tf_op jit(solution)/shard_map/ppermute | solution.py:19
  46.6 2.1 %collective-permute-start.3 = (bf16[1024,128]{1,0:T(8,128)(2,1)S(1)}, bf16[1024,128]{1,0:T(8,128)(2,1)S(1)}, u32[]{:S(2)}, u32[]{:S(2)}) collective-permute-start(bf16[1024,128]{1,0:T(8,128)(2,1)S(1)} %bitcast.46), channel_id=1, source_target_pairs={{0,384},{128,256},{256,128},{384,0},{1,385},{129,257},{257,129},{3... | collective-permute-start | bytes 786440 | tf_op jit(solution)/shard_map/ppermute | solution.py:19
  48.7 6.0 %collective-permute-start = (bf16[1024,128]{1,0:T(8,128)(2,1)S(1)}, bf16[1024,128]{1,0:T(8,128)(2,1)S(1)}, u32[]{:S(2)}, u32[]{:S(2)}) collective-permute-start(bf16[1024,128]{1,0:T(8,128)(2,1)S(1)} %bitcast.56), channel_id=1, source_target_pairs={{0,1},{1,0},{2,3},{3,2},{4,5},{5,4},{6,7},{7,6},{8,9},{9,8},{10,11... | collective-permute-start | bytes 786440 | tf_op jit(solution)/shard_map/ppermute | solution.py:19
  54.9 1.0 collective-permute-done.sent_ref
  55.8 0.7 copy-done.3
  56.5 0.7 copy-done.5
  57.3 2.5 %collective-permute-done.3.refs_3_ = bf16[1024,128]{1,0:T(8,128)(2,1)S(1)} collective-permute-done((bf16[1024,128]{1,0:T(8,128)(2,1)S(1)}, bf16[1024,128]{1,0:T(8,128)(2,1)S(1)}, u32[]{:S(2)}, u32[]{:S(2)}) %collective-permute-start.3) | collective-permute-done | bytes 262176 | tf_op jit(solution)/shard_map/ppermute | solution.py:19
  59.7 0.7 copy-done.7
  60.4 0.9 copy-done.4
  61.4 0.9 copy-done.6
  62.3 0.9 copy-done.8
  63.3 2.6 %shard_map.139 = (f32[128,512]{1,0:T(8,128)S(1)}, f32[128,512]{1,0:T(8,128)}, bf16[1024,512]{1,0:T(8,128)(2,1)S(1)}) custom-call(s32[2]{0:T(128)S(1)} %pad_add_fusion.at_ref, bf16[1024,128]{1,0:T(8,128)(2,1)S(1)} %bitcast.43, bf16[1024,128]{1,0:T(8,128)(2,1)S(1)} %collective-permute-done.sent_ref, bf16[1024,128]{1,0:T(8,128)(2,1)S(1)} %bitcast.47, ...), custom_call_target="tpu_custom_call" | custom-call | tf_op jit(solution)/shard_map/pallas_call | solution.py:58
  65.9 3.9 %collective-permute-start.4 = (f32[128,512]{1,0:T(8,128)}, f32[128,512]{1,0:T(8,128)S(1)}, u32[]{:S(2)}, u32[]{:S(2)}) collective-permute-start(f32[128,512]{1,0:T(8,128)} %get-tuple-element.24), channel_id=1, source_target_pairs={{0,1},{1,0},{2,3},{3,2},{4,5},{5,4},{6,7},{7,6},{8,9},{9,8},{10,11... | collective-permute-start | bytes 786440 | tf_op jit(solution)/shard_map/ppermute | solution.py:19
  69.9 0.9 pad_maximum_fusion.2
  71.2 0.9 copy-done.2
  73.2 0.9 reshape.166
  74.1 8.3 %all-to-all-start.1 = ((bf16[128,2,640]{2,1,0:T(2,128)(2,1)}), bf16[128,2,640]{2,1,0:T(2,128)(2,1)}, u32[]{:S(2)}, u32[]{:S(2)}) async-start(bf16[128,2,640]{2,1,0:T(2,128)(2,1)} %reshape.166), calls=%async_computation.1 | async-start | bytes 655360 | tf_op jit(solution)/shard_map/all_to_all | solution.py:28
  83.2 1.5 gather_fusion
  85.3 13.4 %all-to-all-done.1 = bf16[128,2,640]{2,1,0:T(2,128)(2,1)} async-done(((bf16[128,2,640]{2,1,0:T(2,128)(2,1)}), bf16[128,2,640]{2,1,0:T(2,128)(2,1)}, u32[]{:S(2)}, u32[]{:S(2)}) %all-to-all-start.1) | async-done | bytes 327712 | tf_op jit(solution)/shard_map/all_to_all | solution.py:28
  98.7 1.1 reshape.167.rows_ref
  99.8 2.3 %shard_map.141 = bf16[1024,128]{1,0:T(8,128)(2,1)} custom-call(bf16[256,640]{1,0:T(8,128)(2,1)S(1)} %reshape.167.rows_ref, bf16[512,512]{1,0:T(8,128)(2,1)S(1)} %convolution_convert_fusion.ordered_ref, f32[1,512]{1,0:T(1,128)S(1)} %bitcast.49), custom_call_target="tpu_custom_call" | custom-call | tf_op jit(solution)/shard_map/pallas_call | solution.py:58
  102.2 2.2 %collective-permute-start.5 = (bf16[1024,512]{1,0:T(8,128)(2,1)S(1)}, bf16[1024,512]{1,0:T(8,128)(2,1)}, u32[]{:S(2)}, u32[]{:S(2)}) collective-permute-start(bf16[1024,512]{1,0:T(8,128)(2,1)S(1)} %get-tuple-element.31), channel_id=1, source_target_pairs={{0,1},{1,0},{2,3},{3,2},{4,5},{5,4},{6,7},{7,6},{8,9},{9,8},{10,11... | collective-permute-start | bytes 3145736 | tf_op jit(solution)/shard_map/ppermute | solution.py:19
  104.4 5.5 %all-to-all-start.2 = ((bf16[128,8,128]{2,1,0:T(8,128)(2,1)}), bf16[128,8,128]{2,1,0:T(8,128)(2,1)S(1)}, u32[]{:S(2)}, u32[]{:S(2)}) async-start(bf16[128,8,128]{2,1,0:T(8,128)(2,1)} %bitcast.18), calls=%async_computation.2 | async-start | bytes 524288 | tf_op jit(solution)/shard_map/all_to_all | solution.py:28
  110.1 1.4 broadcast_select_fusion.1
  111.5 1.5 pad_maximum_fusion
  113.0 12.2 %all-to-all-done.2 = bf16[128,8,128]{2,1,0:T(8,128)(2,1)S(1)} async-done(((bf16[128,8,128]{2,1,0:T(8,128)(2,1)}), bf16[128,8,128]{2,1,0:T(8,128)(2,1)S(1)}, u32[]{:S(2)}, u32[]{:S(2)}) %all-to-all-start.2) | async-done | bytes 262176 | tf_op jit(solution)/shard_map/all_to_all | solution.py:28
  125.1 3.3 %shard_map.142 = (bf16[8,144,128]{2,1,0:T(8,128)(2,1)}, f32[128,2048]{1,0:T(8,128)S(1)}) custom-call(bf16[1024,128]{1,0:T(8,128)(2,1)S(1)} %bitcast.48, s32[128,1]{1,0:T(8,128)S(1)} %copy.40.slots_ref, f32[128,512]{1,0:T(8,128)S(1)} %copy-done.10, f32[128,1]{1,0:T(8,128)S(1)} %copy-done.12, f32[128,1]{1,0:T(8,128)S(1)} %copy.41.cot_ref, ...), custom_call_target="tpu_custom_call" | custom-call | tf_op jit(solution)/shard_map/pallas_call | solution.py:58
  128.4 3.7 %all-to-all-start.3 = ((bf16[8,144,128]{2,1,0:T(8,128)(2,1)}), bf16[8,144,128]{2,1,0:T(8,128)(2,1)S(1)}, u32[]{:S(2)}, u32[]{:S(2)}) async-start(bf16[8,144,128]{2,1,0:T(8,128)(2,1)} %get-tuple-element.34), calls=%async_computation.3 | async-start | bytes 589824 | tf_op jit(solution)/shard_map/all_to_all | solution.py:28
  132.3 6.6 %all-to-all-done.3.pieces_ref = bf16[8,144,128]{2,1,0:T(8,128)(2,1)S(1)} async-done(((bf16[8,144,128]{2,1,0:T(8,128)(2,1)}), bf16[8,144,128]{2,1,0:T(8,128)(2,1)S(1)}, u32[]{:S(2)}, u32[]{:S(2)}) %all-to-all-start.3) | async-done | bytes 294944 | tf_op jit(solution)/shard_map/all_to_all | solution.py:28
  139.7 4.2 %shard_map.143 = bf16[1024,128]{1,0:T(8,128)(2,1)} custom-call(bf16[4,1024,256]{2,1,0:T(8,128)(2,1)} %bitcast.54, bf16[8,144,128]{2,1,0:T(8,128)(2,1)} %copy-done.15), custom_call_target="tpu_custom_call" | custom-call | tf_op jit(solution)/shard_map/pallas_call | solution.py:58
  143.9 1.7 pad_maximum_fusion.3
  145.6 4.6 %all-to-all-start.4 = ((bf16[64,24,128]{2,1,0:T(8,128)(2,1)}), bf16[64,24,128]{2,1,0:T(8,128)(2,1)S(1)}, u32[]{:S(2)}, u32[]{:S(2)}) async-start(bf16[64,24,128]{2,1,0:T(8,128)(2,1)} %pad_maximum_fusion.3), calls=%async_computation.4 | async-start | bytes 786432 | tf_op jit(solution)/shard_map/all_to_all | solution.py:28
  150.3 1.2 fusion.4
  151.5 1.1 multiply_convert_fusion
  152.5 12.4 %all-to-all-done.4.pieces_ref = bf16[64,24,128]{2,1,0:T(8,128)(2,1)S(1)} async-done(((bf16[64,24,128]{2,1,0:T(8,128)(2,1)}), bf16[64,24,128]{2,1,0:T(8,128)(2,1)S(1)}, u32[]{:S(2)}, u32[]{:S(2)}) %all-to-all-start.4) | async-done | bytes 393248 | tf_op jit(solution)/shard_map/all_to_all | solution.py:28
  165.0 0.7 shard_map.144
  165.7 6.8 %all-to-all-start.5 = ((f32[8,24,128]{2,1,0:T(8,128)}), f32[8,24,128]{2,1,0:T(8,128)S(1)}, u32[]{:S(2)}, u32[]{:S(2)}) async-start(f32[8,24,128]{2,1,0:T(8,128)} %shard_map.144), calls=%async_computation.5 | async-start | bytes 196608 | tf_op jit(solution)/shard_map/all_to_all | solution.py:28
  172.5 2.0 %pad_maximum_fusion.1 = bf16[128,3072]{1,0:T(8,128)(2,1)} fusion(bf16[128,1024]{1,0:T(8,128)(2,1)S(1)} %fusion.4, bf16[128,2048]{1,0:T(8,128)(2,1)} %multiply_convert_fusion), kind=kLoop, calls=%fused_computation.16 | loop fusion | flops 1572864 | bytes 1572864 | tf_op jit(solution)/shard_map/concatenate | solution.py:413
  174.5 3.0 %all-to-all-done.5.last_ref = f32[8,24,128]{2,1,0:T(8,128)S(1)} async-done(((f32[8,24,128]{2,1,0:T(8,128)}), f32[8,24,128]{2,1,0:T(8,128)S(1)}, u32[]{:S(2)}, u32[]{:S(2)}) %all-to-all-start.5) | async-done | bytes 98336 | tf_op jit(solution)/shard_map/all_to_all | solution.py:28
  177.5 1.2 shard_map.145
  (76 shorter events, 5.5 us)
Async XLA Ops:
  7.2 77.6 %copy-start = (bf16[512,512]{1,0:T(8,128)(2,1)S(1)}, bf16[512,512]{1,0:T(8,128)(2,1)}, u32[]{:S(2)}) copy-start(bf16[512,512]{1,0:T(8,128)(2,1)} %param.15) | copy-start | bytes 1572868
  7.3 0.8 copy-start.13
  8.0 19.8 %copy-start.14 = (bf16[128,3072]{1,0:T(8,128)(2,1)S(1)}, bf16[128,3072]{1,0:T(8,128)(2,1)}, u32[]{:S(2)}) copy-start(bf16[128,3072]{1,0:T(8,128)(2,1)} %param.11) | copy-start | bytes 2359300
  9.3 29.8 %all-to-all-start = ((bf16[64,16,128]{2,1,0:T(8,128)(2,1)}), bf16[64,16,128]{2,1,0:T(8,128)(2,1)S(1)}, u32[]{:S(2)}, u32[]{:S(2)}) async-start(bf16[64,16,128]{2,1,0:T(8,128)(2,1)} %shard_map.138), calls=%async_computation | async-start | bytes 524288 | tf_op jit(solution)/shard_map/all_to_all | solution.py:28
  26.5 2.9 %copy-start.17 = (s32[1,512]{1,0:T(1,128)S(1)}, s32[1,512]{1,0:T(1,128)}, u32[]{:S(2)}) copy-start(s32[1,512]{1,0:T(1,128)} %param.18) | copy-start | bytes 6148
  26.5 2.9 %copy-start.19 = (s32[128]{0:T(128)S(1)}, s32[128]{0:T(128)}, u32[]{:S(2)}) copy-start(s32[128]{0:T(128)} %param.16) | copy-start | bytes 1540
  26.5 3.4 %copy-start.16 = (f32[2048]{0:T(1024)S(1)}, f32[2048]{0:T(1024)}, u32[]{:S(2)}) copy-start(f32[2048]{0:T(1024)} %param.12) | copy-start | bytes 24580
  26.5 3.4 %copy-start.18 = (f32[2048]{0:T(1024)S(1)}, f32[2048]{0:T(1024)}, u32[]{:S(2)}) copy-start(f32[2048]{0:T(1024)} %param.13) | copy-start | bytes 24580
  29.3 2.0 %copy-start.20 = (s32[1,512]{1,0:T(1,128)S(1)}, s32[1,512]{1,0:T(1,128)}, u32[]{:S(2)}) copy-start(s32[1,512]{1,0:T(1,128)} %param.19) | copy-start | bytes 6148
  31.3 0.7 copy-start.22
  39.1 16.7 %collective-permute-start.1 = (bf16[1024,128]{1,0:T(8,128)(2,1)S(1)}, bf16[1024,128]{1,0:T(8,128)(2,1)S(1)}, u32[]{:S(2)}, u32[]{:S(2)}) collective-permute-start(bf16[1024,128]{1,0:T(8,128)(2,1)S(1)} %bitcast.44), channel_id=1, source_target_pairs={{0,128},{128,0},{256,384},{384,256},{1,129},{129,1},{257,385},{385... | collective-permute-start | bytes 786440 | tf_op jit(solution)/shard_map/ppermute | solution.py:19
  42.2 14.3 %collective-permute-start.2 = (bf16[1024,128]{1,0:T(8,128)(2,1)S(1)}, bf16[1024,128]{1,0:T(8,128)(2,1)S(1)}, u32[]{:S(2)}, u32[]{:S(2)}) collective-permute-start(bf16[1024,128]{1,0:T(8,128)(2,1)S(1)} %bitcast.45), channel_id=1, source_target_pairs={{0,256},{128,384},{256,0},{384,128},{1,257},{129,385},{257,1},{385... | collective-permute-start | bytes 786440 | tf_op jit(solution)/shard_map/ppermute | solution.py:19
  46.6 13.1 %collective-permute-start.3 = (bf16[1024,128]{1,0:T(8,128)(2,1)S(1)}, bf16[1024,128]{1,0:T(8,128)(2,1)S(1)}, u32[]{:S(2)}, u32[]{:S(2)}) collective-permute-start(bf16[1024,128]{1,0:T(8,128)(2,1)S(1)} %bitcast.46), channel_id=1, source_target_pairs={{0,384},{128,256},{256,128},{384,0},{1,385},{129,257},{257,129},{3... | collective-permute-start | bytes 786440 | tf_op jit(solution)/shard_map/ppermute | solution.py:19
  48.7 7.1 %collective-permute-start = (bf16[1024,128]{1,0:T(8,128)(2,1)S(1)}, bf16[1024,128]{1,0:T(8,128)(2,1)S(1)}, u32[]{:S(2)}, u32[]{:S(2)}) collective-permute-start(bf16[1024,128]{1,0:T(8,128)(2,1)S(1)} %bitcast.56), channel_id=1, source_target_pairs={{0,1},{1,0},{2,3},{3,2},{4,5},{5,4},{6,7},{7,6},{8,9},{9,8},{10,11... | collective-permute-start | bytes 786440 | tf_op jit(solution)/shard_map/ppermute | solution.py:19
  55.8 0.7 copy-start.3
  56.5 0.7 copy-start.5
  59.7 0.7 copy-start.7
  60.4 0.9 copy-start.4
  61.4 0.9 copy-start.6
  62.3 0.9 copy-start.8
  65.9 4.0 %copy-start.1 = (f32[128,512]{1,0:T(8,128)}, f32[128,512]{1,0:T(8,128)S(1)}, u32[]{:S(2)}) copy-start(f32[128,512]{1,0:T(8,128)S(1)} %get-tuple-element.23.own_ref) | copy-start | bytes 786436
  65.9 5.3 %collective-permute-start.4 = (f32[128,512]{1,0:T(8,128)}, f32[128,512]{1,0:T(8,128)S(1)}, u32[]{:S(2)}, u32[]{:S(2)}) collective-permute-start(f32[128,512]{1,0:T(8,128)} %get-tuple-element.24), channel_id=1, source_target_pairs={{0,1},{1,0},{2,3},{3,2},{4,5},{5,4},{6,7},{7,6},{8,9},{9,8},{10,11... | collective-permute-start | bytes 786440 | tf_op jit(solution)/shard_map/ppermute | solution.py:19
  71.2 0.9 copy-start.2
  72.5 0.7 copy-start.9
  73.2 11.6 %copy-start.11 = (f32[128,1]{1,0:T(8,128)}, f32[128,1]{1,0:T(8,128)S(1)}, u32[]{:S(2)}) copy-start(f32[128,1]{1,0:T(8,128)S(1)} %get-tuple-element.30.norm_ref) | copy-start | bytes 1540
  74.1 24.6 %all-to-all-start.1 = ((bf16[128,2,640]{2,1,0:T(2,128)(2,1)}), bf16[128,2,640]{2,1,0:T(2,128)(2,1)}, u32[]{:S(2)}, u32[]{:S(2)}) async-start(bf16[128,2,640]{2,1,0:T(2,128)(2,1)} %reshape.166), calls=%async_computation.1 | async-start | bytes 655360 | tf_op jit(solution)/shard_map/all_to_all | solution.py:28
  82.4 56.6 %all-gather.3.cloned.1.call-start = ((), (), s32[]{:S(2)}) async-start(), calls=%async_computation.6 | async-start | bytes 2621440 | tf_op jit(solution)/shard_map/all_gather | solution.py:330
  84.8 25.2 %copy-start.21 = (f32[128]{0:T(128)S(1)}, f32[128]{0:T(128)}, u32[]{:S(2)}) copy-start(f32[128]{0:T(128)} %param.21) | copy-start | bytes 1540
  102.2 7.9 %collective-permute-start.5 = (bf16[1024,512]{1,0:T(8,128)(2,1)S(1)}, bf16[1024,512]{1,0:T(8,128)(2,1)}, u32[]{:S(2)}, u32[]{:S(2)}) collective-permute-start(bf16[1024,512]{1,0:T(8,128)(2,1)S(1)} %get-tuple-element.31), channel_id=1, source_target_pairs={{0,1},{1,0},{2,3},{3,2},{4,5},{5,4},{6,7},{7,6},{8,9},{9,8},{10,11... | collective-permute-start | bytes 3145736 | tf_op jit(solution)/shard_map/ppermute | solution.py:19
  104.4 20.8 %all-to-all-start.2 = ((bf16[128,8,128]{2,1,0:T(8,128)(2,1)}), bf16[128,8,128]{2,1,0:T(8,128)(2,1)S(1)}, u32[]{:S(2)}, u32[]{:S(2)}) async-start(bf16[128,8,128]{2,1,0:T(8,128)(2,1)} %bitcast.18), calls=%async_computation.2 | async-start | bytes 524288 | tf_op jit(solution)/shard_map/all_to_all | solution.py:28
  111.4 13.7 %copy-start.10 = (f32[128,512]{1,0:T(8,128)S(1)}, f32[128,512]{1,0:T(8,128)}, u32[]{:S(2)}) copy-start(f32[128,512]{1,0:T(8,128)} %copy-done.9) | copy-start | bytes 786436
  111.5 13.7 %copy-start.12 = (f32[128,1]{1,0:T(8,128)S(1)}, f32[128,1]{1,0:T(8,128)}, u32[]{:S(2)}) copy-start(f32[128,1]{1,0:T(8,128)} %copy-done.11) | copy-start | bytes 1540
  128.4 10.5 %all-to-all-start.3 = ((bf16[8,144,128]{2,1,0:T(8,128)(2,1)}), bf16[8,144,128]{2,1,0:T(8,128)(2,1)S(1)}, u32[]{:S(2)}, u32[]{:S(2)}) async-start(bf16[8,144,128]{2,1,0:T(8,128)(2,1)} %get-tuple-element.34), calls=%async_computation.3 | async-start | bytes 589824 | tf_op jit(solution)/shard_map/all_to_all | solution.py:28
  138.9 0.7 copy-start.15
  145.6 19.4 %all-to-all-start.4 = ((bf16[64,24,128]{2,1,0:T(8,128)(2,1)}), bf16[64,24,128]{2,1,0:T(8,128)(2,1)S(1)}, u32[]{:S(2)}, u32[]{:S(2)}) async-start(bf16[64,24,128]{2,1,0:T(8,128)(2,1)} %pad_maximum_fusion.3), calls=%async_computation.4 | async-start | bytes 786432 | tf_op jit(solution)/shard_map/all_to_all | solution.py:28
  165.7 11.8 %all-to-all-start.5 = ((f32[8,24,128]{2,1,0:T(8,128)}), f32[8,24,128]{2,1,0:T(8,128)S(1)}, u32[]{:S(2)}, u32[]{:S(2)}) async-start(f32[8,24,128]{2,1,0:T(8,128)} %shard_map.144), calls=%async_computation.5 | async-start | bytes 196608 | tf_op jit(solution)/shard_map/all_to_all | solution.py:28
Sparse Core Ops, SparseCore 0:
  85.9 34.4 all-gather.2

commit v5 on v3

--- a/solution.py
+++ b/solution.py
@@ -54,12 +54,67 @@
     return ordered, used
 
 
-def call(kernel, out_shape, *operands):
+vmem = pl.BlockSpec(memory_space=pltpu.VMEM)
+smem = pl.BlockSpec(memory_space=pltpu.SMEM)
+
+
+def call(kernel, out_shape, *operands, places=None):
     return pl.pallas_call(
         kernel,
         out_shape=out_shape,
-        compiler_params=pltpu.CompilerParams(vmem_limit_bytes=24 * 2**20),
+        in_specs=places or [vmem] * len(operands),
+        compiler_params=pltpu.CompilerParams(vmem_limit_bytes=12 * 2**20),
     )(*operands)
+
+
+def owner_kernel(kmax, parts, rows_ref, ordered_ref, used_ref, out_ref):
+    count, (held, width) = rows_ref.shape[0], ordered_ref.shape
+    block = width // parts
+    ordered = ordered_ref[...]
+    labels = rows_ref[:, width:].astype(f32).astype(jnp.int32)
+    local, target = labels[:, 0:1], labels[:, 1:2]
+    columns = lax.broadcasted_iota(jnp.int32, (count, held), 1)
+    first = local * kmax
+    valid = (used_ref[...] > 0) & (columns >= first) & (columns < first + kmax)
+    scores = logit_scale * lax.dot_general(
+        rows_ref[:, :width], ordered, (((1,), (1,)), ((), ())), preferred_element_type=f32
+    )
+    highest = jnp.max(jnp.where(valid, scores, -jnp.inf), axis=1, keepdims=True)
+    weights = jnp.where(valid, jnp.exp(scores - highest), 0.0)
+    probs = weights / jnp.sum(weights, axis=1, keepdims=True)
+    positive = jnp.where(columns == first + target, 1.0, 0.0)
+    coefficients = (logit_scale * (probs - positive)).astype(bf16)
+    gradient = jnp.dot(coefficients, ordered, preferred_element_type=f32).astype(bf16)
+    size = 16 * parts
+    row = lax.broadcasted_iota(jnp.int32, (size, size), 0)
+    column = lax.broadcasted_iota(jnp.int32, (size, size), 1)
+    order = jnp.where(column == lax.rem(row, parts) * 16 + lax.div(row, parts), 1.0, 0.0).astype(bf16)
+    for at in range(0, count, 16):
+        some = jnp.concatenate([gradient[at : at + 16, i * block : (i + 1) * block] for i in range(parts)], axis=0)
+        out_ref[at * parts : (at + 16) * parts, :] = jnp.dot(order, some, preferred_element_type=f32).astype(bf16)
+
+
+def sum_kernel(depth, pieces_ref, out_ref):
+    size = out_ref.shape[1]
+    total = pieces_ref[0].astype(f32)
+    for i in range(1, pieces_ref.shape[0]):
+        total += pieces_ref[i].astype(f32)
+    tail = total[size - 2 * depth :]
+    tail = tail + pltpu.roll(tail, depth, 0)
+    for i in range(out_ref.shape[0]):
+        out_ref[i, : size - 2 * depth, :] = total[: size - 2 * depth]
+        out_ref[i, size - 2 * depth :, :] = tail
+
+
+def last_kernel(depth, at_ref, last_ref, weight_ref, gain_ref, bias_ref):
+    group, _, block = last_ref.shape
+    shard, width = weight_ref.shape
+    cores = group * block // width
+    for i in range(width // block):
+        weight_ref[:, i * block : (i + 1) * block] = last_ref[i * cores + at_ref[1], :shard, :]
+    for i in range(group // 2):
+        gain_ref[i * depth : (i + 1) * depth, :] = last_ref[i, shard : shard + depth, :]
+        bias_ref[i * depth : (i + 1) * depth, :] = last_ref[i + group // 2, shard : shard + depth, :]
 
 
 def owner_kernel(kmax, parts, rows_ref, ordered_ref, used_ref, out_ref):
@@ -168,12 +223,7 @@
     block = embed_width // n_outer
     columns = lax.dynamic_slice_in_dim(head_weight, outer * block, block, 1)
     columns = gather(columns, ("z", "y")).reshape(half, block)
-    blocks = [columns] + [swap(columns, "outer", i) for i in range(1, n_outer)]
-    for bit in (1, 2):
-        odd = (outer & bit) > 0
-        blocks = [jnp.where(odd, blocks[i ^ bit], blocks[i]) for i in range(n_outer)]
-    weight_own = jnp.concatenate(blocks, axis=1)
-
+    weight_own = side_by_side(gather(columns, "outer"))
 
     widened = feats.astype(f32)
     means = jnp.mean(widened, axis=1, keepdims=True)
@@ -189,7 +239,6 @@
     window_pair = jnp.concatenate(
         [jnp.where(core == 0, window_own, window_sent), jnp.where(core == 0, window_sent, window_own)], axis=1
     )
-    window_all = lax.all_gather(window_pair, "outer", axis=0)
 
     ids = jnp.arange(owner_table.shape[0], dtype=jnp.int32)[None, :]
     owners = jnp.sum(jnp.where(image_cluster[:, None] == ids, owner_table[None, :], 0), axis=1)
@@ -205,17 +254,18 @@
     labels = jnp.stack([local, image_target], axis=1).astype(bf16)
     labels = jnp.concatenate([labels, jnp.zeros((count, 126), bf16)], axis=1)
     ordered, used = owner_tables(captions, owner_table, cluster_size[0], cap_index[0], me)
-    weight_own, ordered, used, place, labels = lax.optimization_barrier((weight_own, ordered, used, place, labels))
 
     def by_rows(left, right):
         return lax.dot_general(left, right, (((0,), (0,)), ((), ())), preferred_element_type=f32)
+
+    weight_own, window_pair = lax.optimization_barrier((weight_own, window_pair))
+    window_all = lax.all_gather(window_pair, "outer", axis=0)
 
     partial = by_rows(window_pair, weight_own).reshape(nc, count, embed_width)
     partial_own = lax.dynamic_index_in_dim(partial, core, 0, keepdims=False)
     partial_other = lax.dynamic_index_in_dim(partial, 1 - core, 0, keepdims=False)
     partial_sent = swap(partial_other, "core", 1)
     projected = partial_own + partial_sent
-    weight_own, projected = lax.optimization_barrier((weight_own, projected))
     weight_other = swap(weight_own, "core", 1)
     first = jnp.where(core == 0, weight_own, weight_other).reshape(nz * ny, 1, shard, embed_width)
     second = jnp.where(core == 0, weight_other, weight_own).reshape(nz * ny, 1, shard, embed_width)
@@ -234,7 +284,6 @@
         ordered,
         used.astype(f32),
     )
-    window_all, gradient = lax.optimization_barrier((window_all, gradient))
     returned = exchange(gradient.reshape(dp_count, capacity * n_outer, block), DP).reshape(-1, block)
 
     group = n_outer * nc
@@ -261,14 +310,24 @@
     sums = split_sum(sums, 0)
     sums = jnp.broadcast_to(sums[None], (nz * ny,) + sums.shape)
     pieces = exchange(jnp.concatenate([term.reshape(nz * ny, shard, block), sums], axis=1), ("z", "y"))
-    pieces = jnp.sum(pieces.astype(f32), axis=0)
-    sums = pieces[shard : shard + depth] + pieces[shard + depth :]
-
-    last = gather(jnp.concatenate([pieces[:shard], sums], axis=0), ("outer", "core"))
-    last = last.reshape(n_outer, nc, shard + depth, block)
-    weight_grad = side_by_side(lax.dynamic_index_in_dim(last[:, :, :shard], core, 1, keepdims=False))
-    sums = last[:, :, shard:].reshape(2, window_width)
-    gain_grad, bias_grad = sums[0], sums[1]
+
+    pieces = call(
+        functools.partial(sum_kernel, depth),
+        jax.ShapeDtypeStruct((group, shard + 2 * depth, block), f32),
+        pieces,
+    )
+    weight_grad, gain_grad, bias_grad = call(
+        functools.partial(last_kernel, depth),
+        (
+            jax.ShapeDtypeStruct((shard, embed_width), f32),
+            jax.ShapeDtypeStruct((window_width // block, block), f32),
+            jax.ShapeDtypeStruct((window_width // block, block), f32),
+        ),
+        jnp.stack([outer, core]),
+        exchange(pieces, ("outer", "core")),
+        places=[smem, vmem],
+    )
+    gain_grad, bias_grad = gain_grad.reshape(window_width), bias_grad.reshape(window_width)
 
     scaled_grad = window_grad * ln_gain
     first_mean = jnp.sum(scaled_grad, axis=1, keepdims=True) / width

time: 185 us -> 174 us (0.941)
  starting transfers between devices: 72.7 us -> 60.7 us
  Pallas kernels: 5.1 us -> 7.01 us
    ppermute x6 -> x3, starting transfers between devices: 27.3 us -> 11.4 us  [swap(): return lax.ppermute(value, axis, [(i, i ^ flip) for i in range(size)])]
    all_to_all x5 -> x6, waiting for transfers between devices: 39.8 us -> 48.8 us  [exchange(): return lax.all_to_all(pieces, axis, split_axis=0, concat_axis=0, tiled=True)]
    ppermute x6 -> x3, waiting for transfers between devices: 7.75 us -> 0.01 us  [swap(): return lax.ppermute(value, axis, [(i, i ^ flip) for i in range(size)])]
    all_to_all x1, starting transfers between devices: 5.3 us -> 7.61 us  [body(): lax.all_to_all(send_rows.reshape(dp_count, capacity, -1), DP, split_axis=...]
    all_to_all x1, waiting for transfers between devices: 16.7 us -> 14.5 us  [body(): lax.all_to_all(send_rows.reshape(dp_count, capacity, -1), DP, split_axis=...]
    pallas_call x3 -> x5, Pallas kernels: 5.1 us -> 7.01 us  [call(): pl.pallas_call(kernel, out_shape=out_shape, in_specs=places or [vmem] * l...]
    all_to_all x5 -> x6, starting transfers between devices: 40.1 us -> 41.7 us  [exchange(): return lax.all_to_all(pieces, axis, split_axis=0, concat_axis=0, tiled=True)]
    unnamed x25 -> x26, local copies, waits for them, and re-layouts: 4.39 us -> 4.4 us
  transfers between devices with their start and end apart: 13 -> 11, of which waited for: 10 -> 7; matrix products, arithmetic and copies ran while one was open for 10% -> 11% of each run, Pallas kernels for 1% -> 3%
where the time goes in v5:
time: 174 us; the launch traced here: 173 us
  waiting for transfers between devices  63.3 us (36%)
  starting transfers between devices  60.7 us (35%)
  other arithmetic  14.6 us (8%)
  between operations  14.4 us (8%)
  local copies, waits for them, and re-layouts  10.6 us (6%)
  Pallas kernels  7.01 us (4%)
  matrix products  2.41 us (1%)
    all_to_all x6, waiting for transfers between devices, exchange(): return lax.all_to_all(pieces, axis, split_axis=0, concat_axis=0, tiled=True)  48.8 us
    all_to_all x6, starting transfers between devices, exchange(): return lax.all_to_all(pieces, axis, split_axis=0, concat_axis=0, tiled=True)  41.7 us
    all_to_all x1, waiting for transfers between devices, body(): lax.all_to_all(send_rows.reshape(dp_count, capacity, -1), DP, split_axis=...  14.5 us
    ppermute x3, starting transfers between devices, swap(): return lax.ppermute(value, axis, [(i, i ^ flip) for i in range(size)])  11.4 us
    all_to_all x1, starting transfers between devices, body(): lax.all_to_all(send_rows.reshape(dp_count, capacity, -1), DP, split_axis=...  7.61 us
    pallas_call x5, Pallas kernels, call(): pl.pallas_call(kernel, out_shape=out_shape, in_specs=places or [vmem] * l...  7.01 us
    unnamed x26, local copies, waits for them, and re-layouts  4.4 us
  transfers between devices with their start and end apart: 11, of which 7 were waited for; matrix products, arithmetic and copies ran while one was open for 11% of the time, Pallas kernels for 3%

profile of v5, /device:TPU:1, one launch (start us, length us, event | category | flops | bytes accessed | tf_op | source)
XLA Modules:
  0.0 173.1 jit_solution(8037606644622256313)
XLA Ops:
  7.2 0.8 constant_dynamic-slice_fusion.2
  8.0 0.7 broadcast_in_dim.63
  8.7 17.1 %all-to-all-start = ((bf16[64,16,128]{2,1,0:T(8,128)(2,1)}), bf16[64,16,128]{2,1,0:T(8,128)(2,1)S(1)}, u32[]{:S(2)}, u32[]{:S(2)}) async-start(bf16[64,16,128]{2,1,0:T(8,128)(2,1)} %broadcast_in_dim.63), calls=%async_computation | async-start | bytes 524288 | tf_op jit(solution)/shard_map/all_to_all | solution.py:28
  25.9 1.3 convert_reduce_fusion
  27.2 0.4 multiply_reduce_fusion
  27.6 1.2 copy-done.3
  28.8 0.2 fusion
  29.0 0.3 copy.28
  29.3 2.9 %collective-permute-start = (bf16[1024,128]{1,0:T(8,128)(2,1)S(1)}, bf16[1024,128]{1,0:T(8,128)(2,1)}, u32[]{:S(2)}, u32[]{:S(2)}) collective-permute-start(bf16[1024,128]{1,0:T(8,128)(2,1)S(1)} %bitcast.70), channel_id=1, source_target_pairs={{0,1},{1,0},{2,3},{3,2},{4,5},{5,4},{6,7},{7,6},{8,9},{9,8},{10,11... | collective-permute-start | bytes 786440 | tf_op jit(solution)/shard_map/ppermute | solution.py:19
  32.6 5.9 %all-to-all-done = bf16[64,16,128]{2,1,0:T(8,128)(2,1)S(1)} async-done(((bf16[64,16,128]{2,1,0:T(8,128)(2,1)}), bf16[64,16,128]{2,1,0:T(8,128)(2,1)S(1)}, u32[]{:S(2)}, u32[]{:S(2)}) %all-to-all-start) | async-done | bytes 262176 | tf_op jit(solution)/shard_map/all_to_all | solution.py:28
  38.5 1.1 broadcast_in_dim.65
  39.6 4.0 %all-to-all-start.1 = ((bf16[4,1024,128]{2,1,0:T(8,128)(2,1)}), bf16[4,1024,128]{2,1,0:T(8,128)(2,1)S(1)}, u32[]{:S(2)}, u32[]{:S(2)}) async-start(bf16[4,1024,128]{2,1,0:T(8,128)(2,1)} %broadcast_in_dim.65), calls=%async_computation.1 | async-start | bytes 2097152 | tf_op jit(solution)/shard_map/all_to_all | solution.py:28
  43.7 0.2 convert_reduce_fusion.1
  44.1 1.0 bitcast_select_fusion.1
  45.0 0.9 pad_maximum_fusion.3
  45.9 9.1 %all-to-all-done.1 = bf16[4,1024,128]{2,1,0:T(8,128)(2,1)S(1)} async-done(((bf16[4,1024,128]{2,1,0:T(8,128)(2,1)}), bf16[4,1024,128]{2,1,0:T(8,128)(2,1)S(1)}, u32[]{:S(2)}, u32[]{:S(2)}) %all-to-all-start.1) | async-done | bytes 1048608 | tf_op jit(solution)/shard_map/all_to_all | solution.py:28
  55.1 1.1 pad_maximum_fusion.1
  56.2 1.7 fusion.23
  57.9 6.6 %collective-permute-start.1 = (f32[128,512]{1,0:T(8,128)S(1)}, f32[128,512]{1,0:T(8,128)S(1)}, u32[]{:S(2)}, u32[]{:S(2)}) collective-permute-start(f32[128,512]{1,0:T(8,128)S(1)} %dynamic-slice_bitcast_fusion), channel_id=1, source_target_pairs={{0,1},{1,0},{2,3},{3,2},{4,5},{5,4},{6,7},{7,6},{8,9},{9,8},{10,11... | collective-permute-start | bytes 786440 | tf_op jit(solution)/shard_map/ppermute | solution.py:19
  65.1 1.9 %collective-permute-start.2 = (bf16[1024,512]{1,0:T(8,128)(2,1)}, bf16[1024,512]{1,0:T(8,128)(2,1)}, u32[]{:S(2)}, u32[]{:S(2)}) collective-permute-start(bf16[1024,512]{1,0:T(8,128)(2,1)} %pad_maximum_fusion.1), channel_id=1, source_target_pairs={{0,1},{1,0},{2,3},{3,2},{4,5},{5,4},{6,7},{7,6},{8,9},{9,8},{10,11... | collective-permute-start | bytes 3145736 | tf_op jit(solution)/shard_map/ppermute | solution.py:19
  67.3 0.3 convolution_convert_fusion.1
  67.5 0.9 reshape.172
  68.4 7.6 %all-to-all-start.2 = ((bf16[128,2,640]{2,1,0:T(2,128)(2,1)}), bf16[128,2,640]{2,1,0:T(2,128)(2,1)S(1)}, u32[]{:S(2)}, u32[]{:S(2)}) async-start(bf16[128,2,640]{2,1,0:T(2,128)(2,1)} %reshape.172), calls=%async_computation.2 | async-start | bytes 655360 | tf_op jit(solution)/shard_map/all_to_all | solution.py:277
  76.0 1.5 gather_fusion
  77.6 0.5 convolution_convert_fusion.ordered_ref
  78.1 14.5 %all-to-all-done.2 = bf16[128,2,640]{2,1,0:T(2,128)(2,1)S(1)} async-done(((bf16[128,2,640]{2,1,0:T(2,128)(2,1)}), bf16[128,2,640]{2,1,0:T(2,128)(2,1)S(1)}, u32[]{:S(2)}, u32[]{:S(2)}) %all-to-all-start.2) | async-done | bytes 327712 | tf_op jit(solution)/shard_map/all_to_all | solution.py:277
  92.7 2.4 %shard_map.138 = bf16[1024,128]{1,0:T(8,128)(2,1)} custom-call(bf16[256,640]{1,0:T(8,128)(2,1)S(1)} %reshape.173.rows_ref, bf16[512,512]{1,0:T(8,128)(2,1)S(1)} %convolution_convert_fusion.ordered_ref, f32[1,512]{1,0:T(1,128)S(1)} %bitcast.62), custom_call_target="tpu_custom_call" | custom-call | tf_op jit(solution)/shard_map/pallas_call | solution.py:62
  95.1 5.4 %all-to-all-start.3 = ((bf16[128,8,128]{2,1,0:T(8,128)(2,1)}), bf16[128,8,128]{2,1,0:T(8,128)(2,1)S(1)}, u32[]{:S(2)}, u32[]{:S(2)}) async-start(bf16[128,8,128]{2,1,0:T(8,128)(2,1)} %bitcast.22), calls=%async_computation.3 | async-start | bytes 524288 | tf_op jit(solution)/shard_map/all_to_all | solution.py:28
  100.9 1.7 broadcast_select_fusion.1
  102.5 1.5 pad_maximum_fusion
  104.1 11.8 %all-to-all-done.3 = bf16[128,8,128]{2,1,0:T(8,128)(2,1)S(1)} async-done(((bf16[128,8,128]{2,1,0:T(8,128)(2,1)}), bf16[128,8,128]{2,1,0:T(8,128)(2,1)S(1)}, u32[]{:S(2)}, u32[]{:S(2)}) %all-to-all-start.3) | async-done | bytes 262176 | tf_op jit(solution)/shard_map/all_to_all | solution.py:28
  115.9 1.6 copy-done.1
  117.5 2.1 %shard_map.139 = (bf16[8,144,128]{2,1,0:T(8,128)(2,1)}, f32[128,2048]{1,0:T(8,128)S(1)}) custom-call(bf16[1024,128]{1,0:T(8,128)(2,1)S(1)} %bitcast.61, s32[128,1]{1,0:T(8,128)S(1)} %copy.31.slots_ref, f32[128,512]{1,0:T(8,128)S(1)} %get-tuple-element.25.unit_ref, f32[128,1]{1,0:T(8,128)S(1)} %copy.32.norm_ref, f32[128,1]{1,0:T(8,128)S(1)} %copy.33.cot_ref, ...), custom_call_target="tpu_custom_call" | custom-call | tf_op jit(solution)/shard_map/pallas_call | solution.py:62
  119.5 3.7 %all-to-all-start.4 = ((bf16[8,144,128]{2,1,0:T(8,128)(2,1)}), bf16[8,144,128]{2,1,0:T(8,128)(2,1)S(1)}, u32[]{:S(2)}, u32[]{:S(2)}) async-start(bf16[8,144,128]{2,1,0:T(8,128)(2,1)} %get-tuple-element.14), calls=%async_computation.4 | async-start | bytes 589824 | tf_op jit(solution)/shard_map/all_to_all | solution.py:28
  123.3 0.2 multiply_reduce_fusion.2
  123.5 6.5 %all-to-all-done.4.pieces_ref = bf16[8,144,128]{2,1,0:T(8,128)(2,1)S(1)} async-done(((bf16[8,144,128]{2,1,0:T(8,128)(2,1)}), bf16[8,144,128]{2,1,0:T(8,128)(2,1)S(1)}, u32[]{:S(2)}, u32[]{:S(2)}) %all-to-all-start.4) | async-done | bytes 294944 | tf_op jit(solution)/shard_map/all_to_all | solution.py:28
  130.1 1.6 copy-done.2
  131.7 0.7 shard_map.140
  132.5 0.8 pad_maximum_fusion.4
  133.2 4.6 %all-to-all-start.5 = ((bf16[64,24,128]{2,1,0:T(8,128)(2,1)}), bf16[64,24,128]{2,1,0:T(8,128)(2,1)S(1)}, u32[]{:S(2)}, u32[]{:S(2)}) async-start(bf16[64,24,128]{2,1,0:T(8,128)(2,1)} %pad_maximum_fusion.4), calls=%async_computation.5 | async-start | bytes 786432 | tf_op jit(solution)/shard_map/all_to_all | solution.py:28
  137.9 1.2 fusion.4
  139.1 1.1 multiply_convert_fusion
  140.1 12.5 %all-to-all-done.5.pieces_ref = bf16[64,24,128]{2,1,0:T(8,128)(2,1)S(1)} async-done(((bf16[64,24,128]{2,1,0:T(8,128)(2,1)}), bf16[64,24,128]{2,1,0:T(8,128)(2,1)S(1)}, u32[]{:S(2)}, u32[]{:S(2)}) %all-to-all-start.5) | async-done | bytes 393248 | tf_op jit(solution)/shard_map/all_to_all | solution.py:28
  152.6 0.7 shard_map.141
  153.3 6.8 %all-to-all-start.6 = ((f32[8,24,128]{2,1,0:T(8,128)}), f32[8,24,128]{2,1,0:T(8,128)S(1)}, u32[]{:S(2)}, u32[]{:S(2)}) async-start(f32[8,24,128]{2,1,0:T(8,128)} %shard_map.141), calls=%async_computation.6 | async-start | bytes 196608 | tf_op jit(solution)/shard_map/all_to_all | solution.py:28
  160.1 2.0 %pad_maximum_fusion.2 = bf16[128,3072]{1,0:T(8,128)(2,1)} fusion(bf16[128,1024]{1,0:T(8,128)(2,1)S(1)} %fusion.4, bf16[128,2048]{1,0:T(8,128)(2,1)} %multiply_convert_fusion), kind=kLoop, calls=%fused_computation.18 | loop fusion | flops 1572864 | bytes 1572864 | tf_op jit(solution)/shard_map/concatenate | solution.py:337
  162.1 3.0 %all-to-all-done.6.last_ref = f32[8,24,128]{2,1,0:T(8,128)S(1)} async-done(((f32[8,24,128]{2,1,0:T(8,128)}), f32[8,24,128]{2,1,0:T(8,128)S(1)}, u32[]{:S(2)}, u32[]{:S(2)}) %all-to-all-start.6) | async-done | bytes 98336 | tf_op jit(solution)/shard_map/all_to_all | solution.py:28
  165.1 1.2 shard_map.142
  (62 shorter events, 2.2 us)
Async XLA Ops:
  7.2 70.5 %copy-start = (bf16[512,512]{1,0:T(8,128)(2,1)S(1)}, bf16[512,512]{1,0:T(8,128)(2,1)}, u32[]{:S(2)}) copy-start(bf16[512,512]{1,0:T(8,128)(2,1)} %param.15) | copy-start | bytes 1572868
  7.2 20.0 %copy-start.5 = (bf16[128,3072]{1,0:T(8,128)(2,1)S(1)}, bf16[128,3072]{1,0:T(8,128)(2,1)}, u32[]{:S(2)}) copy-start(bf16[128,3072]{1,0:T(8,128)(2,1)} %param.11) | copy-start | bytes 2359300
  7.2 21.6 %copy-start.8 = (f32[2048]{0:T(1024)S(1)}, f32[2048]{0:T(1024)}, u32[]{:S(2)}) copy-start(f32[2048]{0:T(1024)} %param.13) | copy-start | bytes 24580
  7.2 21.6 %copy-start.6 = (f32[2048]{0:T(1024)S(1)}, f32[2048]{0:T(1024)}, u32[]{:S(2)}) copy-start(f32[2048]{0:T(1024)} %param.12) | copy-start | bytes 24580
  8.7 29.8 %all-to-all-start = ((bf16[64,16,128]{2,1,0:T(8,128)(2,1)}), bf16[64,16,128]{2,1,0:T(8,128)(2,1)S(1)}, u32[]{:S(2)}, u32[]{:S(2)}) async-start(bf16[64,16,128]{2,1,0:T(8,128)(2,1)} %broadcast_in_dim.63), calls=%async_computation | async-start | bytes 524288 | tf_op jit(solution)/shard_map/all_to_all | solution.py:28
  27.6 1.2 copy-start.3
  28.8 3.5 %copy-start.7 = (s32[1,512]{1,0:T(1,128)S(1)}, s32[1,512]{1,0:T(1,128)}, u32[]{:S(2)}) copy-start(s32[1,512]{1,0:T(1,128)} %param.18) | copy-start | bytes 6148
  28.8 3.5 %copy-start.9 = (s32[128]{0:T(128)S(1)}, s32[128]{0:T(128)}, u32[]{:S(2)}) copy-start(s32[128]{0:T(128)} %param.16) | copy-start | bytes 1540
  28.8 3.8 %copy-start.12 = (s32[128]{0:T(128)S(1)}, s32[128]{0:T(128)}, u32[]{:S(2)}) copy-start(s32[128]{0:T(128)} %param.17) | copy-start | bytes 1540
  29.3 14.7 %collective-permute-start = (bf16[1024,128]{1,0:T(8,128)(2,1)S(1)}, bf16[1024,128]{1,0:T(8,128)(2,1)}, u32[]{:S(2)}, u32[]{:S(2)}) collective-permute-start(bf16[1024,128]{1,0:T(8,128)(2,1)S(1)} %bitcast.70), channel_id=1, source_target_pairs={{0,1},{1,0},{2,3},{3,2},{4,5},{5,4},{6,7},{7,6},{8,9},{9,8},{10,11... | collective-permute-start | bytes 786440 | tf_op jit(solution)/shard_map/ppermute | solution.py:19
  39.6 15.3 %all-to-all-start.1 = ((bf16[4,1024,128]{2,1,0:T(8,128)(2,1)}), bf16[4,1024,128]{2,1,0:T(8,128)(2,1)S(1)}, u32[]{:S(2)}, u32[]{:S(2)}) async-start(bf16[4,1024,128]{2,1,0:T(8,128)(2,1)} %broadcast_in_dim.65), calls=%async_computation.1 | async-start | bytes 2097152 | tf_op jit(solution)/shard_map/all_to_all | solution.py:28
  43.7 86.5 %all-gather.3.cloned.1.call-start = ((), (), s32[]{:S(2)}) async-start(), calls=%async_computation.7 | async-start | bytes 2621440 | tf_op jit(solution)/shard_map/all_gather | solution.py:262
  45.9 10.3 %copy-start.4 = (bf16[1024,256]{1,0:T(8,128)(2,1)S(1)}, bf16[1024,256]{1,0:T(8,128)(2,1)}, u32[]{:S(2)}) copy-start(bf16[1024,256]{1,0:T(8,128)(2,1)} %pad_maximum_fusion.3) | copy-start | bytes 1572868
  56.1 8.4 %copy-start.10 = (s32[1,512]{1,0:T(1,128)S(1)}, s32[1,512]{1,0:T(1,128)}, u32[]{:S(2)}) copy-start(s32[1,512]{1,0:T(1,128)} %param.19) | copy-start | bytes 6148
  57.9 9.1 %collective-permute-start.1 = (f32[128,512]{1,0:T(8,128)S(1)}, f32[128,512]{1,0:T(8,128)S(1)}, u32[]{:S(2)}, u32[]{:S(2)}) collective-permute-start(f32[128,512]{1,0:T(8,128)S(1)} %dynamic-slice_bitcast_fusion), channel_id=1, source_target_pairs={{0,1},{1,0},{2,3},{3,2},{4,5},{5,4},{6,7},{7,6},{8,9},{9,8},{10,11... | collective-permute-start | bytes 786440 | tf_op jit(solution)/shard_map/ppermute | solution.py:19
  65.1 35.8 %collective-permute-start.2 = (bf16[1024,512]{1,0:T(8,128)(2,1)}, bf16[1024,512]{1,0:T(8,128)(2,1)}, u32[]{:S(2)}, u32[]{:S(2)}) collective-permute-start(bf16[1024,512]{1,0:T(8,128)(2,1)} %pad_maximum_fusion.1), channel_id=1, source_target_pairs={{0,1},{1,0},{2,3},{3,2},{4,5},{5,4},{6,7},{7,6},{8,9},{9,8},{10,11... | collective-permute-start | bytes 3145736 | tf_op jit(solution)/shard_map/ppermute | solution.py:19
  68.4 24.2 %all-to-all-start.2 = ((bf16[128,2,640]{2,1,0:T(2,128)(2,1)}), bf16[128,2,640]{2,1,0:T(2,128)(2,1)S(1)}, u32[]{:S(2)}, u32[]{:S(2)}) async-start(bf16[128,2,640]{2,1,0:T(2,128)(2,1)} %reshape.172), calls=%async_computation.2 | async-start | bytes 655360 | tf_op jit(solution)/shard_map/all_to_all | solution.py:277
  76.0 24.6 %copy-start.11 = (f32[128]{0:T(128)S(1)}, f32[128]{0:T(128)}, u32[]{:S(2)}) copy-start(f32[128]{0:T(128)} %param.21) | copy-start | bytes 1540
  95.1 20.8 %all-to-all-start.3 = ((bf16[128,8,128]{2,1,0:T(8,128)(2,1)}), bf16[128,8,128]{2,1,0:T(8,128)(2,1)S(1)}, u32[]{:S(2)}, u32[]{:S(2)}) async-start(bf16[128,8,128]{2,1,0:T(8,128)(2,1)} %bitcast.22), calls=%async_computation.3 | async-start | bytes 524288 | tf_op jit(solution)/shard_map/all_to_all | solution.py:28
  115.9 1.6 copy-start.1
  119.5 10.5 %all-to-all-start.4 = ((bf16[8,144,128]{2,1,0:T(8,128)(2,1)}), bf16[8,144,128]{2,1,0:T(8,128)(2,1)S(1)}, u32[]{:S(2)}, u32[]{:S(2)}) async-start(bf16[8,144,128]{2,1,0:T(8,128)(2,1)} %get-tuple-element.14), calls=%async_computation.4 | async-start | bytes 589824 | tf_op jit(solution)/shard_map/all_to_all | solution.py:28
  130.1 1.6 copy-start.2
  133.2 19.4 %all-to-all-start.5 = ((bf16[64,24,128]{2,1,0:T(8,128)(2,1)}), bf16[64,24,128]{2,1,0:T(8,128)(2,1)S(1)}, u32[]{:S(2)}, u32[]{:S(2)}) async-start(bf16[64,24,128]{2,1,0:T(8,128)(2,1)} %pad_maximum_fusion.4), calls=%async_computation.5 | async-start | bytes 786432 | tf_op jit(solution)/shard_map/all_to_all | solution.py:28
  153.3 11.8 %all-to-all-start.6 = ((f32[8,24,128]{2,1,0:T(8,128)}), f32[8,24,128]{2,1,0:T(8,128)S(1)}, u32[]{:S(2)}, u32[]{:S(2)}) async-start(f32[8,24,128]{2,1,0:T(8,128)} %shard_map.141), calls=%async_computation.6 | async-start | bytes 196608 | tf_op jit(solution)/shard_map/all_to_all | solution.py:28
Sparse Core Ops, SparseCore 0:
  56.3 33.1 all-gather.2

commit v6 on v5

--- a/solution.py
+++ b/solution.py
@@ -223,7 +223,7 @@
     block = embed_width // n_outer
     columns = lax.dynamic_slice_in_dim(head_weight, outer * block, block, 1)
     columns = gather(columns, ("z", "y")).reshape(half, block)
-    weight_own = side_by_side(gather(columns, "outer"))
+    blocks = gather(columns, "outer")
 
     widened = feats.astype(f32)
     means = jnp.mean(widened, axis=1, keepdims=True)
@@ -250,7 +250,6 @@
         ((owners[:, None] == owners[None, :]) & (images[None, :] < images[:, None])).astype(jnp.int32), axis=1
     )
     slots = owners * capacity + ranks
-    place = (jnp.arange(dp_count * capacity, dtype=jnp.int32)[:, None] == slots[None, :]).astype(bf16)
     labels = jnp.stack([local, image_target], axis=1).astype(bf16)
     labels = jnp.concatenate([labels, jnp.zeros((count, 126), bf16)], axis=1)
     ordered, used = owner_tables(captions, owner_table, cluster_size[0], cap_index[0], me)
@@ -258,18 +257,17 @@
     def by_rows(left, right):
         return lax.dot_general(left, right, (((0,), (0,)), ((), ())), preferred_element_type=f32)
 
-    weight_own, window_pair = lax.optimization_barrier((weight_own, window_pair))
-    window_all = lax.all_gather(window_pair, "outer", axis=0)
-
-    partial = by_rows(window_pair, weight_own).reshape(nc, count, embed_width)
+    blocks, window_pair, slots, labels = lax.optimization_barrier((blocks, window_pair, slots, labels))
+    place = (jnp.arange(dp_count * capacity, dtype=jnp.int32)[:, None] == slots[None, :]).astype(bf16)
+
+    partial = by_rows(window_pair, side_by_side(blocks)).reshape(nc, count, embed_width)
     partial_own = lax.dynamic_index_in_dim(partial, core, 0, keepdims=False)
     partial_other = lax.dynamic_index_in_dim(partial, 1 - core, 0, keepdims=False)
     partial_sent = swap(partial_other, "core", 1)
     projected = partial_own + partial_sent
-    weight_other = swap(weight_own, "core", 1)
-    first = jnp.where(core == 0, weight_own, weight_other).reshape(nz * ny, 1, shard, embed_width)
-    second = jnp.where(core == 0, weight_other, weight_own).reshape(nz * ny, 1, shard, embed_width)
-    full_weight = jnp.concatenate([first, second], axis=1).reshape(window_width, embed_width)
+    blocks, window_pair, projected = lax.optimization_barrier((blocks, window_pair, projected))
+    weight_all = lax.all_gather(blocks, "core", axis=0)
+    window_all = lax.all_gather(window_pair, "outer", axis=0)
     norm_len = jnp.sqrt(jnp.sum(projected * projected, axis=1, keepdims=True) + 1e-06)
     unit = projected / norm_len
     payload = jnp.concatenate([unit.astype(bf16), labels], axis=1)
@@ -284,6 +282,8 @@
         ordered,
         used.astype(f32),
     )
+    weight_all = [side_by_side(weight_all[i]).reshape(nz * ny, 1, shard, embed_width) for i in range(nc)]
+    full_weight = jnp.concatenate(weight_all, axis=1).reshape(window_width, embed_width)
     returned = exchange(gradient.reshape(dp_count, capacity * n_outer, block), DP).reshape(-1, block)
 
     group = n_outer * nc

time: 174 us -> 172 us (0.989)
  other arithmetic: 14.6 us -> 11.1 us
  waiting for transfers between devices: 63.3 us -> 65.8 us
  starting transfers between devices: 60.7 us -> 58.8 us
  local copies, waits for them, and re-layouts: 10.6 us -> 12.5 us
    ppermute x3 -> x2, starting transfers between devices: 11.4 us -> 9.5 us  [swap(): return lax.ppermute(value, axis, [(i, i ^ flip) for i in range(size)])]
    unnamed x26 -> x28, local copies, waits for them, and re-layouts: 4.4 us -> 4.84 us
  transfers between devices with their start and end apart: 11 -> 11, of which waited for: 7 -> 8; matrix products, arithmetic and copies ran while one was open for 11% -> 10% of each run, Pallas kernels for 3% -> 3%
where the time goes in v6:
time: 172 us; the launch traced here: 171 us
  waiting for transfers between devices  65.8 us (38%)
  starting transfers between devices  58.8 us (34%)
  between operations  14.5 us (8%)
  local copies, waits for them, and re-layouts  12.5 us (7%)
  other arithmetic  11.1 us (6%)
  Pallas kernels  7.01 us (4%)
    all_to_all x6, waiting for transfers between devices, exchange(): return lax.all_to_all(pieces, axis, split_axis=0, concat_axis=0, tiled=True)  50 us
    all_to_all x6, starting transfers between devices, exchange(): return lax.all_to_all(pieces, axis, split_axis=0, concat_axis=0, tiled=True)  41.7 us
    all_to_all x1, waiting for transfers between devices, body(): lax.all_to_all(send_rows.reshape(dp_count, capacity, -1), DP, split_axis=...  14.2 us
    ppermute x2, starting transfers between devices, swap(): return lax.ppermute(value, axis, [(i, i ^ flip) for i in range(size)])  9.5 us
    all_to_all x1, starting transfers between devices, body(): lax.all_to_all(send_rows.reshape(dp_count, capacity, -1), DP, split_axis=...  7.5 us
    pallas_call x5, Pallas kernels, call(): pl.pallas_call(kernel, out_shape=out_shape, in_specs=places or [vmem] * l...  7.01 us
    unnamed x28, local copies, waits for them, and re-layouts  4.84 us
  transfers between devices with their start and end apart: 11, of which 8 were waited for; matrix products, arithmetic and copies ran while one was open for 10% of the time, Pallas kernels for 3%

profile of v6, /device:TPU:1, one launch (start us, length us, event | category | flops | bytes accessed | tf_op | source)
XLA Modules:
  0.0 170.7 jit_solution(15052725479761590623)
XLA Ops:
  7.2 0.8 constant_dynamic-slice_fusion.2
  8.0 0.7 broadcast_in_dim.60
  8.7 17.1 %all-to-all-start = ((bf16[64,16,128]{2,1,0:T(8,128)(2,1)}), bf16[64,16,128]{2,1,0:T(8,128)(2,1)S(1)}, u32[]{:S(2)}, u32[]{:S(2)}) async-start(bf16[64,16,128]{2,1,0:T(8,128)(2,1)} %broadcast_in_dim.60), calls=%async_computation | async-start | bytes 524288 | tf_op jit(solution)/shard_map/all_to_all | solution.py:28
  25.9 1.3 convert_reduce_fusion
  27.2 0.4 multiply_reduce_fusion
  27.6 1.2 copy-done.4
  28.8 0.2 fusion.8
  29.0 0.3 copy.33
  29.3 2.9 %collective-permute-start = (bf16[1024,128]{1,0:T(8,128)(2,1)S(1)}, bf16[1024,128]{1,0:T(8,128)(2,1)}, u32[]{:S(2)}, u32[]{:S(2)}) collective-permute-start(bf16[1024,128]{1,0:T(8,128)(2,1)S(1)} %bitcast.77), channel_id=1, source_target_pairs={{0,1},{1,0},{2,3},{3,2},{4,5},{5,4},{6,7},{7,6},{8,9},{9,8},{10,11... | collective-permute-start | bytes 786440 | tf_op jit(solution)/shard_map/ppermute | solution.py:19
  32.4 0.2 convert_reduce_fusion.1
  32.6 5.9 %all-to-all-done = bf16[64,16,128]{2,1,0:T(8,128)(2,1)S(1)} async-done(((bf16[64,16,128]{2,1,0:T(8,128)(2,1)}), bf16[64,16,128]{2,1,0:T(8,128)(2,1)S(1)}, u32[]{:S(2)}, u32[]{:S(2)}) %all-to-all-start) | async-done | bytes 262176 | tf_op jit(solution)/shard_map/all_to_all | solution.py:28
  38.5 1.1 broadcast_in_dim.62
  39.6 4.0 %all-to-all-start.1 = ((bf16[4,1024,128]{2,1,0:T(8,128)(2,1)}), bf16[4,1024,128]{2,1,0:T(8,128)(2,1)S(1)}, u32[]{:S(2)}, u32[]{:S(2)}) async-start(bf16[4,1024,128]{2,1,0:T(8,128)(2,1)} %broadcast_in_dim.62), calls=%async_computation.1 | async-start | bytes 2097152 | tf_op jit(solution)/shard_map/all_to_all | solution.py:28
  44.0 1.0 bitcast_select_fusion.1
  45.1 9.9 %all-to-all-done.1 = bf16[4,1024,128]{2,1,0:T(8,128)(2,1)S(1)} async-done(((bf16[4,1024,128]{2,1,0:T(8,128)(2,1)}), bf16[4,1024,128]{2,1,0:T(8,128)(2,1)S(1)}, u32[]{:S(2)}, u32[]{:S(2)}) %all-to-all-start.1) | async-done | bytes 1048608 | tf_op jit(solution)/shard_map/all_to_all | solution.py:28
  55.1 0.5 fusion
  55.5 0.4 copy-done.3
  56.0 6.6 %collective-permute-start.1 = (f32[128,512]{1,0:T(8,128)S(1)}, f32[128,512]{1,0:T(8,128)S(1)}, u32[]{:S(2)}, u32[]{:S(2)}) collective-permute-start(f32[128,512]{1,0:T(8,128)S(1)} %dynamic-slice_bitcast_fusion), channel_id=1, source_target_pairs={{0,1},{1,0},{2,3},{3,2},{4,5},{5,4},{6,7},{7,6},{8,9},{9,8},{10,11... | collective-permute-start | bytes 786440 | tf_op jit(solution)/shard_map/ppermute | solution.py:19
  62.6 1.1 collective-permute-done.1
  64.2 0.4 all-gather.7.cloned.1.call-update
  65.0 0.2 convolution_convert_fusion.1
  65.2 0.9 reshape.178
  66.1 7.5 %all-to-all-start.2 = ((bf16[128,2,640]{2,1,0:T(2,128)(2,1)}), bf16[128,2,640]{2,1,0:T(2,128)(2,1)S(1)}, u32[]{:S(2)}, u32[]{:S(2)}) async-start(bf16[128,2,640]{2,1,0:T(2,128)(2,1)} %reshape.178), calls=%async_computation.2 | async-start | bytes 655360 | tf_op jit(solution)/shard_map/all_to_all | solution.py:275
  73.6 1.5 gather_fusion
  75.3 0.5 convolution_convert_fusion.ordered_ref
  76.0 14.2 %all-to-all-done.2 = bf16[128,2,640]{2,1,0:T(2,128)(2,1)S(1)} async-done(((bf16[128,2,640]{2,1,0:T(2,128)(2,1)}), bf16[128,2,640]{2,1,0:T(2,128)(2,1)S(1)}, u32[]{:S(2)}, u32[]{:S(2)}) %all-to-all-start.2) | async-done | bytes 327712 | tf_op jit(solution)/shard_map/all_to_all | solution.py:275
  90.3 2.3 %shard_map.138 = bf16[1024,128]{1,0:T(8,128)(2,1)} custom-call(bf16[256,640]{1,0:T(8,128)(2,1)S(1)} %reshape.179.rows_ref, bf16[512,512]{1,0:T(8,128)(2,1)S(1)} %convolution_convert_fusion.ordered_ref, f32[1,512]{1,0:T(1,128)S(1)} %bitcast.63), custom_call_target="tpu_custom_call" | custom-call | tf_op jit(solution)/shard_map/pallas_call | solution.py:62
  92.6 5.5 %all-to-all-start.3 = ((bf16[128,8,128]{2,1,0:T(8,128)(2,1)}), bf16[128,8,128]{2,1,0:T(8,128)(2,1)S(1)}, u32[]{:S(2)}, u32[]{:S(2)}) async-start(bf16[128,8,128]{2,1,0:T(8,128)(2,1)} %bitcast.22), calls=%async_computation.3 | async-start | bytes 524288 | tf_op jit(solution)/shard_map/all_to_all | solution.py:28
  98.1 1.7 fusion.28
  99.8 1.5 maximum_maximum_fusion
  101.3 12.2 %all-to-all-done.3 = bf16[128,8,128]{2,1,0:T(8,128)(2,1)S(1)} async-done(((bf16[128,8,128]{2,1,0:T(8,128)(2,1)}), bf16[128,8,128]{2,1,0:T(8,128)(2,1)S(1)}, u32[]{:S(2)}, u32[]{:S(2)}) %all-to-all-start.3) | async-done | bytes 262176 | tf_op jit(solution)/shard_map/all_to_all | solution.py:28
  113.5 1.6 copy-done.1
  115.1 2.1 %shard_map.139 = (bf16[8,144,128]{2,1,0:T(8,128)(2,1)}, f32[128,2048]{1,0:T(8,128)S(1)}) custom-call(bf16[1024,128]{1,0:T(8,128)(2,1)S(1)} %bitcast.62, s32[128,1]{1,0:T(8,128)S(1)} %copy.35.slots_ref, f32[128,512]{1,0:T(8,128)S(1)} %get-tuple-element.35.unit_ref, f32[128,1]{1,0:T(8,128)S(1)} %copy.36.norm_ref, f32[128,1]{1,0:T(8,128)S(1)} %copy.37.cot_ref, ...), custom_call_target="tpu_custom_call" | custom-call | tf_op jit(solution)/shard_map/pallas_call | solution.py:62
  117.2 3.7 %all-to-all-start.4 = ((bf16[8,144,128]{2,1,0:T(8,128)(2,1)}), bf16[8,144,128]{2,1,0:T(8,128)(2,1)S(1)}, u32[]{:S(2)}, u32[]{:S(2)}) async-start(bf16[8,144,128]{2,1,0:T(8,128)(2,1)} %get-tuple-element.24), calls=%async_computation.4 | async-start | bytes 589824 | tf_op jit(solution)/shard_map/all_to_all | solution.py:28
  120.9 0.2 multiply_reduce_fusion.2
  121.1 6.6 %all-to-all-done.4.pieces_ref = bf16[8,144,128]{2,1,0:T(8,128)(2,1)S(1)} async-done(((bf16[8,144,128]{2,1,0:T(8,128)(2,1)}), bf16[8,144,128]{2,1,0:T(8,128)(2,1)S(1)}, u32[]{:S(2)}, u32[]{:S(2)}) %all-to-all-start.4) | async-done | bytes 294944 | tf_op jit(solution)/shard_map/all_to_all | solution.py:28
  127.8 1.6 copy-done.2
  129.3 0.7 shard_map.140
  130.1 0.8 pad_maximum_fusion.2
  130.8 4.6 %all-to-all-start.5 = ((bf16[64,24,128]{2,1,0:T(8,128)(2,1)}), bf16[64,24,128]{2,1,0:T(8,128)(2,1)S(1)}, u32[]{:S(2)}, u32[]{:S(2)}) async-start(bf16[64,24,128]{2,1,0:T(8,128)(2,1)} %pad_maximum_fusion.2), calls=%async_computation.5 | async-start | bytes 786432 | tf_op jit(solution)/shard_map/all_to_all | solution.py:28
  135.5 1.2 fusion.12
  136.7 1.1 multiply_convert_fusion
  137.8 12.5 %all-to-all-done.5.pieces_ref = bf16[64,24,128]{2,1,0:T(8,128)(2,1)S(1)} async-done(((bf16[64,24,128]{2,1,0:T(8,128)(2,1)}), bf16[64,24,128]{2,1,0:T(8,128)(2,1)S(1)}, u32[]{:S(2)}, u32[]{:S(2)}) %all-to-all-start.5) | async-done | bytes 393248 | tf_op jit(solution)/shard_map/all_to_all | solution.py:28
  150.2 0.7 shard_map.141
  150.9 6.8 %all-to-all-start.6 = ((f32[8,24,128]{2,1,0:T(8,128)}), f32[8,24,128]{2,1,0:T(8,128)S(1)}, u32[]{:S(2)}, u32[]{:S(2)}) async-start(f32[8,24,128]{2,1,0:T(8,128)} %shard_map.141), calls=%async_computation.6 | async-start | bytes 196608 | tf_op jit(solution)/shard_map/all_to_all | solution.py:28
  157.7 2.0 %pad_maximum_fusion = bf16[128,3072]{1,0:T(8,128)(2,1)} fusion(bf16[128,1024]{1,0:T(8,128)(2,1)S(1)} %fusion.12, bf16[128,2048]{1,0:T(8,128)(2,1)} %multiply_convert_fusion), kind=kLoop, calls=%fused_computation.23 | loop fusion | flops 1572864 | bytes 1572864 | tf_op jit(solution)/shard_map/concatenate | solution.py:337
  159.7 3.0 %all-to-all-done.6.last_ref = f32[8,24,128]{2,1,0:T(8,128)S(1)} async-done(((f32[8,24,128]{2,1,0:T(8,128)}), f32[8,24,128]{2,1,0:T(8,128)S(1)}, u32[]{:S(2)}, u32[]{:S(2)}) %all-to-all-start.6) | async-done | bytes 98336 | tf_op jit(solution)/shard_map/all_to_all | solution.py:28
  162.7 1.2 shard_map.142
  (64 shorter events, 2.1 us)
Async XLA Ops:
  7.2 68.1 %copy-start = (bf16[512,512]{1,0:T(8,128)(2,1)S(1)}, bf16[512,512]{1,0:T(8,128)(2,1)}, u32[]{:S(2)}) copy-start(bf16[512,512]{1,0:T(8,128)(2,1)} %param.15) | copy-start | bytes 1572868
  7.2 20.0 %copy-start.5 = (bf16[128,3072]{1,0:T(8,128)(2,1)S(1)}, bf16[128,3072]{1,0:T(8,128)(2,1)}, u32[]{:S(2)}) copy-start(bf16[128,3072]{1,0:T(8,128)(2,1)} %param.11) | copy-start | bytes 2359300
  7.2 21.6 %copy-start.7 = (f32[2048]{0:T(1024)S(1)}, f32[2048]{0:T(1024)}, u32[]{:S(2)}) copy-start(f32[2048]{0:T(1024)} %param.12) | copy-start | bytes 24580
  7.2 21.6 %copy-start.9 = (f32[2048]{0:T(1024)S(1)}, f32[2048]{0:T(1024)}, u32[]{:S(2)}) copy-start(f32[2048]{0:T(1024)} %param.13) | copy-start | bytes 24580
  8.7 29.8 %all-to-all-start = ((bf16[64,16,128]{2,1,0:T(8,128)(2,1)}), bf16[64,16,128]{2,1,0:T(8,128)(2,1)S(1)}, u32[]{:S(2)}, u32[]{:S(2)}) async-start(bf16[64,16,128]{2,1,0:T(8,128)(2,1)} %broadcast_in_dim.60), calls=%async_computation | async-start | bytes 524288 | tf_op jit(solution)/shard_map/all_to_all | solution.py:28
  27.6 1.2 copy-start.4
  28.8 3.4 %copy-start.8 = (s32[1,512]{1,0:T(1,128)S(1)}, s32[1,512]{1,0:T(1,128)}, u32[]{:S(2)}) copy-start(s32[1,512]{1,0:T(1,128)} %param.18) | copy-start | bytes 6148
  28.8 3.4 %copy-start.10 = (s32[128]{0:T(128)S(1)}, s32[128]{0:T(128)}, u32[]{:S(2)}) copy-start(s32[128]{0:T(128)} %param.16) | copy-start | bytes 1540
  28.8 3.8 %copy-start.13 = (s32[128]{0:T(128)S(1)}, s32[128]{0:T(128)}, u32[]{:S(2)}) copy-start(s32[128]{0:T(128)} %param.17) | copy-start | bytes 1540
  29.3 14.7 %collective-permute-start = (bf16[1024,128]{1,0:T(8,128)(2,1)S(1)}, bf16[1024,128]{1,0:T(8,128)(2,1)}, u32[]{:S(2)}, u32[]{:S(2)}) collective-permute-start(bf16[1024,128]{1,0:T(8,128)(2,1)S(1)} %bitcast.77), channel_id=1, source_target_pairs={{0,1},{1,0},{2,3},{3,2},{4,5},{5,4},{6,7},{7,6},{8,9},{9,8},{10,11... | collective-permute-start | bytes 786440 | tf_op jit(solution)/shard_map/ppermute | solution.py:19
  39.6 15.3 %all-to-all-start.1 = ((bf16[4,1024,128]{2,1,0:T(8,128)(2,1)}), bf16[4,1024,128]{2,1,0:T(8,128)(2,1)S(1)}, u32[]{:S(2)}, u32[]{:S(2)}) async-start(bf16[4,1024,128]{2,1,0:T(8,128)(2,1)} %broadcast_in_dim.62), calls=%async_computation.1 | async-start | bytes 2097152 | tf_op jit(solution)/shard_map/all_to_all | solution.py:28
  43.7 54.5 %all-gather.5.cloned.1.call-start = ((), (), s32[]{:S(2)}) async-start(), calls=%async_computation.7 | async-start | bytes 3145728 | tf_op jit(solution)/shard_map/all_gather | solution.py:269
  45.1 10.4 %copy-start.6 = (bf16[1024,256]{1,0:T(8,128)(2,1)}, bf16[1024,256]{1,0:T(8,128)(2,1)S(1)}, u32[]{:S(2)}) copy-start(bf16[1024,256]{1,0:T(8,128)(2,1)S(1)} %pad_maximum_fusion.1) | copy-start | bytes 1572868
  55.0 1.0 copy-start.3
  56.0 8.1 %copy-start.11 = (s32[1,512]{1,0:T(1,128)S(1)}, s32[1,512]{1,0:T(1,128)}, u32[]{:S(2)}) copy-start(s32[1,512]{1,0:T(1,128)} %param.19) | copy-start | bytes 6148
  56.0 8.6 %copy-start.12 = (f32[128]{0:T(128)S(1)}, f32[128]{0:T(128)}, u32[]{:S(2)}) copy-start(f32[128]{0:T(128)} %param.21) | copy-start | bytes 1540
  56.0 7.8 %collective-permute-start.1 = (f32[128,512]{1,0:T(8,128)S(1)}, f32[128,512]{1,0:T(8,128)S(1)}, u32[]{:S(2)}, u32[]{:S(2)}) collective-permute-start(f32[128,512]{1,0:T(8,128)S(1)} %dynamic-slice_bitcast_fusion), channel_id=1, source_target_pairs={{0,1},{1,0},{2,3},{3,2},{4,5},{5,4},{6,7},{7,6},{8,9},{9,8},{10,11... | collective-permute-start | bytes 786440 | tf_op jit(solution)/shard_map/ppermute | solution.py:19
  63.8 63.9 %all-gather.7.cloned.1.call-start = ((), (), s32[]{:S(2)}) async-start(), calls=%async_computation.8 | async-start | bytes 2621440 | tf_op jit(solution)/shard_map/all_gather | solution.py:270
  66.1 24.1 %all-to-all-start.2 = ((bf16[128,2,640]{2,1,0:T(2,128)(2,1)}), bf16[128,2,640]{2,1,0:T(2,128)(2,1)S(1)}, u32[]{:S(2)}, u32[]{:S(2)}) async-start(bf16[128,2,640]{2,1,0:T(2,128)(2,1)} %reshape.178), calls=%async_computation.2 | async-start | bytes 655360 | tf_op jit(solution)/shard_map/all_to_all | solution.py:275
  92.6 20.8 %all-to-all-start.3 = ((bf16[128,8,128]{2,1,0:T(8,128)(2,1)}), bf16[128,8,128]{2,1,0:T(8,128)(2,1)S(1)}, u32[]{:S(2)}, u32[]{:S(2)}) async-start(bf16[128,8,128]{2,1,0:T(8,128)(2,1)} %bitcast.22), calls=%async_computation.3 | async-start | bytes 524288 | tf_op jit(solution)/shard_map/all_to_all | solution.py:28
  113.5 1.6 copy-start.1
  117.2 10.5 %all-to-all-start.4 = ((bf16[8,144,128]{2,1,0:T(8,128)(2,1)}), bf16[8,144,128]{2,1,0:T(8,128)(2,1)S(1)}, u32[]{:S(2)}, u32[]{:S(2)}) async-start(bf16[8,144,128]{2,1,0:T(8,128)(2,1)} %get-tuple-element.24), calls=%async_computation.4 | async-start | bytes 589824 | tf_op jit(solution)/shard_map/all_to_all | solution.py:28
  127.7 1.6 copy-start.2
  130.8 19.4 %all-to-all-start.5 = ((bf16[64,24,128]{2,1,0:T(8,128)(2,1)}), bf16[64,24,128]{2,1,0:T(8,128)(2,1)S(1)}, u32[]{:S(2)}, u32[]{:S(2)}) async-start(bf16[64,24,128]{2,1,0:T(8,128)(2,1)} %pad_maximum_fusion.2), calls=%async_computation.5 | async-start | bytes 786432 | tf_op jit(solution)/shard_map/all_to_all | solution.py:28
  150.9 11.8 %all-to-all-start.6 = ((f32[8,24,128]{2,1,0:T(8,128)}), f32[8,24,128]{2,1,0:T(8,128)S(1)}, u32[]{:S(2)}, u32[]{:S(2)}) async-start(f32[8,24,128]{2,1,0:T(8,128)} %shard_map.141), calls=%async_computation.6 | async-start | bytes 196608 | tf_op jit(solution)/shard_map/all_to_all | solution.py:28
Sparse Core Ops, SparseCore 0:
  64.0 12.8 all-gather.4
  79.6 36.0 all-gather.6

commit v7 on v6

--- a/solution.py
+++ b/solution.py
@@ -58,16 +58,17 @@
 smem = pl.BlockSpec(memory_space=pltpu.SMEM)
 
 
-def call(kernel, out_shape, *operands, places=None):
+def call(kernel, out_shape, *operands, places=None, scratch=()):
     return pl.pallas_call(
         kernel,
         out_shape=out_shape,
         in_specs=places or [vmem] * len(operands),
+        scratch_shapes=scratch,
         compiler_params=pltpu.CompilerParams(vmem_limit_bytes=12 * 2**20),
     )(*operands)
 
 
-def owner_kernel(kmax, parts, rows_ref, ordered_ref, used_ref, out_ref):
+def owner_kernel(kmax, parts, rows_ref, ordered_ref, used_ref, out_ref, lines):
     count, (held, width) = rows_ref.shape[0], ordered_ref.shape
     block = width // parts
     ordered = ordered_ref[...]
@@ -84,14 +85,10 @@
     probs = weights / jnp.sum(weights, axis=1, keepdims=True)
     positive = jnp.where(columns == first + target, 1.0, 0.0)
     coefficients = (logit_scale * (probs - positive)).astype(bf16)
-    gradient = jnp.dot(coefficients, ordered, preferred_element_type=f32).astype(bf16)
-    size = 16 * parts
-    row = lax.broadcasted_iota(jnp.int32, (size, size), 0)
-    column = lax.broadcasted_iota(jnp.int32, (size, size), 1)
-    order = jnp.where(column == lax.rem(row, parts) * 16 + lax.div(row, parts), 1.0, 0.0).astype(bf16)
-    for at in range(0, count, 16):
-        some = jnp.concatenate([gradient[at : at + 16, i * block : (i + 1) * block] for i in range(parts)], axis=0)
-        out_ref[at * parts : (at + 16) * parts, :] = jnp.dot(order, some, preferred_element_type=f32).astype(bf16)
+    gradient = jnp.dot(coefficients, ordered, preferred_element_type=f32)
+    for i in range(parts):
+        lines[pl.ds(i, count, stride=parts), :] = gradient[:, i * block : (i + 1) * block]
+    out_ref[...] = lines[...].astype(bf16)
 
 
 def sum_kernel(depth, pieces_ref, out_ref):
@@ -117,7 +114,7 @@
         bias_ref[i * depth : (i + 1) * depth, :] = last_ref[i + group // 2, shard : shard + depth, :]
 
 
-def owner_kernel(kmax, parts, rows_ref, ordered_ref, used_ref, out_ref):
+def owner_kernel(kmax, parts, rows_ref, ordered_ref, used_ref, out_ref, lines):
     count, (held, width) = rows_ref.shape[0], ordered_ref.shape
     block = width // parts
     ordered = ordered_ref[...]
@@ -281,6 +278,7 @@
         received.reshape(dp_count * capacity, -1),
         ordered,
         used.astype(f32),
+        scratch=[pltpu.VMEM((dp_count * capacity * n_outer, block), f32)],
     )
     weight_all = [side_by_side(weight_all[i]).reshape(nz * ny, 1, shard, embed_width) for i in range(nc)]
     full_weight = jnp.concatenate(weight_all, axis=1).reshape(window_width, embed_width)

time: 172 us -> 172 us (level)
  no operation moved by 1% of the time
where the time goes in v7:
time: 172 us; the launch traced here: 171 us
  waiting for transfers between devices  65.8 us (38%)
  starting transfers between devices  58.8 us (34%)
  between operations  14.5 us (8%)
  local copies, waits for them, and re-layouts  12.5 us (7%)
  other arithmetic  11.1 us (6%)
  Pallas kernels  7.01 us (4%)
    all_to_all x6, waiting for transfers between devices, exchange(): return lax.all_to_all(pieces, axis, split_axis=0, concat_axis=0, tiled=True)  50 us
    all_to_all x6, starting transfers between devices, exchange(): return lax.all_to_all(pieces, axis, split_axis=0, concat_axis=0, tiled=True)  41.7 us
    all_to_all x1, waiting for transfers between devices, body(): lax.all_to_all(send_rows.reshape(dp_count, capacity, -1), DP, split_axis=...  14.2 us
    ppermute x2, starting transfers between devices, swap(): return lax.ppermute(value, axis, [(i, i ^ flip) for i in range(size)])  9.5 us
    all_to_all x1, starting transfers between devices, body(): lax.all_to_all(send_rows.reshape(dp_count, capacity, -1), DP, split_axis=...  7.5 us
    pallas_call x5, Pallas kernels, call(): pl.pallas_call(kernel, out_shape=out_shape, in_specs=places or [vmem] * l...  7.01 us
    unnamed x28, local copies, waits for them, and re-layouts  4.84 us
  transfers between devices with their start and end apart: 11, of which 8 were waited for; matrix products, arithmetic and copies ran while one was open for 10% of the time, Pallas kernels for 3%

profile of v7, /device:TPU:1, one launch (start us, length us, event | category | flops | bytes accessed | tf_op | source)
XLA Modules:
  0.0 170.7 jit_solution(15052725479761590623)
XLA Ops:
  7.2 0.8 constant_dynamic-slice_fusion.2
  8.0 0.7 broadcast_in_dim.60
  8.7 17.1 %all-to-all-start = ((bf16[64,16,128]{2,1,0:T(8,128)(2,1)}), bf16[64,16,128]{2,1,0:T(8,128)(2,1)S(1)}, u32[]{:S(2)}, u32[]{:S(2)}) async-start(bf16[64,16,128]{2,1,0:T(8,128)(2,1)} %broadcast_in_dim.60), calls=%async_computation | async-start | bytes 524288 | tf_op jit(solution)/shard_map/all_to_all | solution.py:28
  25.9 1.3 convert_reduce_fusion
  27.2 0.4 multiply_reduce_fusion
  27.6 1.2 copy-done.4
  28.8 0.2 fusion.8
  29.0 0.3 copy.33
  29.3 2.9 %collective-permute-start = (bf16[1024,128]{1,0:T(8,128)(2,1)S(1)}, bf16[1024,128]{1,0:T(8,128)(2,1)}, u32[]{:S(2)}, u32[]{:S(2)}) collective-permute-start(bf16[1024,128]{1,0:T(8,128)(2,1)S(1)} %bitcast.77), channel_id=1, source_target_pairs={{0,1},{1,0},{2,3},{3,2},{4,5},{5,4},{6,7},{7,6},{8,9},{9,8},{10,11... | collective-permute-start | bytes 786440 | tf_op jit(solution)/shard_map/ppermute | solution.py:19
  32.4 0.2 convert_reduce_fusion.1
  32.6 5.9 %all-to-all-done = bf16[64,16,128]{2,1,0:T(8,128)(2,1)S(1)} async-done(((bf16[64,16,128]{2,1,0:T(8,128)(2,1)}), bf16[64,16,128]{2,1,0:T(8,128)(2,1)S(1)}, u32[]{:S(2)}, u32[]{:S(2)}) %all-to-all-start) | async-done | bytes 262176 | tf_op jit(solution)/shard_map/all_to_all | solution.py:28
  38.5 1.1 broadcast_in_dim.62
  39.6 4.0 %all-to-all-start.1 = ((bf16[4,1024,128]{2,1,0:T(8,128)(2,1)}), bf16[4,1024,128]{2,1,0:T(8,128)(2,1)S(1)}, u32[]{:S(2)}, u32[]{:S(2)}) async-start(bf16[4,1024,128]{2,1,0:T(8,128)(2,1)} %broadcast_in_dim.62), calls=%async_computation.1 | async-start | bytes 2097152 | tf_op jit(solution)/shard_map/all_to_all | solution.py:28
  44.0 1.0 bitcast_select_fusion.1
  45.1 9.9 %all-to-all-done.1 = bf16[4,1024,128]{2,1,0:T(8,128)(2,1)S(1)} async-done(((bf16[4,1024,128]{2,1,0:T(8,128)(2,1)}), bf16[4,1024,128]{2,1,0:T(8,128)(2,1)S(1)}, u32[]{:S(2)}, u32[]{:S(2)}) %all-to-all-start.1) | async-done | bytes 1048608 | tf_op jit(solution)/shard_map/all_to_all | solution.py:28
  55.1 0.5 fusion
  55.5 0.4 copy-done.3
  56.0 6.6 %collective-permute-start.1 = (f32[128,512]{1,0:T(8,128)S(1)}, f32[128,512]{1,0:T(8,128)S(1)}, u32[]{:S(2)}, u32[]{:S(2)}) collective-permute-start(f32[128,512]{1,0:T(8,128)S(1)} %dynamic-slice_bitcast_fusion), channel_id=1, source_target_pairs={{0,1},{1,0},{2,3},{3,2},{4,5},{5,4},{6,7},{7,6},{8,9},{9,8},{10,11... | collective-permute-start | bytes 786440 | tf_op jit(solution)/shard_map/ppermute | solution.py:19
  62.6 1.1 collective-permute-done.1
  64.2 0.4 all-gather.7.cloned.1.call-update
  65.0 0.2 convolution_convert_fusion.1
  65.2 0.9 reshape.178
  66.1 7.5 %all-to-all-start.2 = ((bf16[128,2,640]{2,1,0:T(2,128)(2,1)}), bf16[128,2,640]{2,1,0:T(2,128)(2,1)S(1)}, u32[]{:S(2)}, u32[]{:S(2)}) async-start(bf16[128,2,640]{2,1,0:T(2,128)(2,1)} %reshape.178), calls=%async_computation.2 | async-start | bytes 655360 | tf_op jit(solution)/shard_map/all_to_all | solution.py:272
  73.6 1.5 gather_fusion
  75.3 0.5 convolution_convert_fusion.ordered_ref
  76.0 14.2 %all-to-all-done.2 = bf16[128,2,640]{2,1,0:T(2,128)(2,1)S(1)} async-done(((bf16[128,2,640]{2,1,0:T(2,128)(2,1)}), bf16[128,2,640]{2,1,0:T(2,128)(2,1)S(1)}, u32[]{:S(2)}, u32[]{:S(2)}) %all-to-all-start.2) | async-done | bytes 327712 | tf_op jit(solution)/shard_map/all_to_all | solution.py:272
  90.3 2.3 %shard_map.138 = bf16[1024,128]{1,0:T(8,128)(2,1)} custom-call(bf16[256,640]{1,0:T(8,128)(2,1)S(1)} %reshape.179.rows_ref, bf16[512,512]{1,0:T(8,128)(2,1)S(1)} %convolution_convert_fusion.ordered_ref, f32[1,512]{1,0:T(1,128)S(1)} %bitcast.63), custom_call_target="tpu_custom_call" | custom-call | tf_op jit(solution)/shard_map/pallas_call | solution.py:62
  92.6 5.5 %all-to-all-start.3 = ((bf16[128,8,128]{2,1,0:T(8,128)(2,1)}), bf16[128,8,128]{2,1,0:T(8,128)(2,1)S(1)}, u32[]{:S(2)}, u32[]{:S(2)}) async-start(bf16[128,8,128]{2,1,0:T(8,128)(2,1)} %bitcast.22), calls=%async_computation.3 | async-start | bytes 524288 | tf_op jit(solution)/shard_map/all_to_all | solution.py:28
  98.1 1.7 fusion.28
  99.8 1.5 maximum_maximum_fusion
  101.3 12.2 %all-to-all-done.3 = bf16[128,8,128]{2,1,0:T(8,128)(2,1)S(1)} async-done(((bf16[128,8,128]{2,1,0:T(8,128)(2,1)}), bf16[128,8,128]{2,1,0:T(8,128)(2,1)S(1)}, u32[]{:S(2)}, u32[]{:S(2)}) %all-to-all-start.3) | async-done | bytes 262176 | tf_op jit(solution)/shard_map/all_to_all | solution.py:28
  113.5 1.6 copy-done.1
  115.1 2.1 %shard_map.139 = (bf16[8,144,128]{2,1,0:T(8,128)(2,1)}, f32[128,2048]{1,0:T(8,128)S(1)}) custom-call(bf16[1024,128]{1,0:T(8,128)(2,1)S(1)} %bitcast.62, s32[128,1]{1,0:T(8,128)S(1)} %copy.35.slots_ref, f32[128,512]{1,0:T(8,128)S(1)} %get-tuple-element.35.unit_ref, f32[128,1]{1,0:T(8,128)S(1)} %copy.36.norm_ref, f32[128,1]{1,0:T(8,128)S(1)} %copy.37.cot_ref, ...), custom_call_target="tpu_custom_call" | custom-call | tf_op jit(solution)/shard_map/pallas_call | solution.py:62
  117.2 3.7 %all-to-all-start.4 = ((bf16[8,144,128]{2,1,0:T(8,128)(2,1)}), bf16[8,144,128]{2,1,0:T(8,128)(2,1)S(1)}, u32[]{:S(2)}, u32[]{:S(2)}) async-start(bf16[8,144,128]{2,1,0:T(8,128)(2,1)} %get-tuple-element.24), calls=%async_computation.4 | async-start | bytes 589824 | tf_op jit(solution)/shard_map/all_to_all | solution.py:28
  120.9 0.2 multiply_reduce_fusion.2
  121.1 6.6 %all-to-all-done.4.pieces_ref = bf16[8,144,128]{2,1,0:T(8,128)(2,1)S(1)} async-done(((bf16[8,144,128]{2,1,0:T(8,128)(2,1)}), bf16[8,144,128]{2,1,0:T(8,128)(2,1)S(1)}, u32[]{:S(2)}, u32[]{:S(2)}) %all-to-all-start.4) | async-done | bytes 294944 | tf_op jit(solution)/shard_map/all_to_all | solution.py:28
  127.8 1.6 copy-done.2
  129.3 0.7 shard_map.140
  130.1 0.8 pad_maximum_fusion.2
  130.8 4.6 %all-to-all-start.5 = ((bf16[64,24,128]{2,1,0:T(8,128)(2,1)}), bf16[64,24,128]{2,1,0:T(8,128)(2,1)S(1)}, u32[]{:S(2)}, u32[]{:S(2)}) async-start(bf16[64,24,128]{2,1,0:T(8,128)(2,1)} %pad_maximum_fusion.2), calls=%async_computation.5 | async-start | bytes 786432 | tf_op jit(solution)/shard_map/all_to_all | solution.py:28
  135.5 1.2 fusion.12
  136.7 1.1 multiply_convert_fusion
  137.8 12.5 %all-to-all-done.5.pieces_ref = bf16[64,24,128]{2,1,0:T(8,128)(2,1)S(1)} async-done(((bf16[64,24,128]{2,1,0:T(8,128)(2,1)}), bf16[64,24,128]{2,1,0:T(8,128)(2,1)S(1)}, u32[]{:S(2)}, u32[]{:S(2)}) %all-to-all-start.5) | async-done | bytes 393248 | tf_op jit(solution)/shard_map/all_to_all | solution.py:28
  150.2 0.7 shard_map.141
  150.9 6.8 %all-to-all-start.6 = ((f32[8,24,128]{2,1,0:T(8,128)}), f32[8,24,128]{2,1,0:T(8,128)S(1)}, u32[]{:S(2)}, u32[]{:S(2)}) async-start(f32[8,24,128]{2,1,0:T(8,128)} %shard_map.141), calls=%async_computation.6 | async-start | bytes 196608 | tf_op jit(solution)/shard_map/all_to_all | solution.py:28
  157.7 2.0 %pad_maximum_fusion = bf16[128,3072]{1,0:T(8,128)(2,1)} fusion(bf16[128,1024]{1,0:T(8,128)(2,1)S(1)} %fusion.12, bf16[128,2048]{1,0:T(8,128)(2,1)} %multiply_convert_fusion), kind=kLoop, calls=%fused_computation.23 | loop fusion | flops 1572864 | bytes 1572864 | tf_op jit(solution)/shard_map/concatenate | solution.py:335
  159.7 3.0 %all-to-all-done.6.last_ref = f32[8,24,128]{2,1,0:T(8,128)S(1)} async-done(((f32[8,24,128]{2,1,0:T(8,128)}), f32[8,24,128]{2,1,0:T(8,128)S(1)}, u32[]{:S(2)}, u32[]{:S(2)}) %all-to-all-start.6) | async-done | bytes 98336 | tf_op jit(solution)/shard_map/all_to_all | solution.py:28
  162.7 1.2 shard_map.142
  (64 shorter events, 2.1 us)
Async XLA Ops:
  7.2 68.1 %copy-start = (bf16[512,512]{1,0:T(8,128)(2,1)S(1)}, bf16[512,512]{1,0:T(8,128)(2,1)}, u32[]{:S(2)}) copy-start(bf16[512,512]{1,0:T(8,128)(2,1)} %param.15) | copy-start | bytes 1572868
  7.2 20.0 %copy-start.5 = (bf16[128,3072]{1,0:T(8,128)(2,1)S(1)}, bf16[128,3072]{1,0:T(8,128)(2,1)}, u32[]{:S(2)}) copy-start(bf16[128,3072]{1,0:T(8,128)(2,1)} %param.11) | copy-start | bytes 2359300
  7.2 21.6 %copy-start.7 = (f32[2048]{0:T(1024)S(1)}, f32[2048]{0:T(1024)}, u32[]{:S(2)}) copy-start(f32[2048]{0:T(1024)} %param.12) | copy-start | bytes 24580
  7.2 21.6 %copy-start.9 = (f32[2048]{0:T(1024)S(1)}, f32[2048]{0:T(1024)}, u32[]{:S(2)}) copy-start(f32[2048]{0:T(1024)} %param.13) | copy-start | bytes 24580
  8.7 29.8 %all-to-all-start = ((bf16[64,16,128]{2,1,0:T(8,128)(2,1)}), bf16[64,16,128]{2,1,0:T(8,128)(2,1)S(1)}, u32[]{:S(2)}, u32[]{:S(2)}) async-start(bf16[64,16,128]{2,1,0:T(8,128)(2,1)} %broadcast_in_dim.60), calls=%async_computation | async-start | bytes 524288 | tf_op jit(solution)/shard_map/all_to_all | solution.py:28
  27.6 1.2 copy-start.4
  28.8 3.4 %copy-start.8 = (s32[1,512]{1,0:T(1,128)S(1)}, s32[1,512]{1,0:T(1,128)}, u32[]{:S(2)}) copy-start(s32[1,512]{1,0:T(1,128)} %param.18) | copy-start | bytes 6148
  28.8 3.4 %copy-start.10 = (s32[128]{0:T(128)S(1)}, s32[128]{0:T(128)}, u32[]{:S(2)}) copy-start(s32[128]{0:T(128)} %param.16) | copy-start | bytes 1540
  28.8 3.8 %copy-start.13 = (s32[128]{0:T(128)S(1)}, s32[128]{0:T(128)}, u32[]{:S(2)}) copy-start(s32[128]{0:T(128)} %param.17) | copy-start | bytes 1540
  29.3 14.7 %collective-permute-start = (bf16[1024,128]{1,0:T(8,128)(2,1)S(1)}, bf16[1024,128]{1,0:T(8,128)(2,1)}, u32[]{:S(2)}, u32[]{:S(2)}) collective-permute-start(bf16[1024,128]{1,0:T(8,128)(2,1)S(1)} %bitcast.77), channel_id=1, source_target_pairs={{0,1},{1,0},{2,3},{3,2},{4,5},{5,4},{6,7},{7,6},{8,9},{9,8},{10,11... | collective-permute-start | bytes 786440 | tf_op jit(solution)/shard_map/ppermute | solution.py:19
  39.6 15.3 %all-to-all-start.1 = ((bf16[4,1024,128]{2,1,0:T(8,128)(2,1)}), bf16[4,1024,128]{2,1,0:T(8,128)(2,1)S(1)}, u32[]{:S(2)}, u32[]{:S(2)}) async-start(bf16[4,1024,128]{2,1,0:T(8,128)(2,1)} %broadcast_in_dim.62), calls=%async_computation.1 | async-start | bytes 2097152 | tf_op jit(solution)/shard_map/all_to_all | solution.py:28
  43.7 54.5 %all-gather.5.cloned.1.call-start = ((), (), s32[]{:S(2)}) async-start(), calls=%async_computation.7 | async-start | bytes 3145728 | tf_op jit(solution)/shard_map/all_gather | solution.py:266
  45.1 10.4 %copy-start.6 = (bf16[1024,256]{1,0:T(8,128)(2,1)}, bf16[1024,256]{1,0:T(8,128)(2,1)S(1)}, u32[]{:S(2)}) copy-start(bf16[1024,256]{1,0:T(8,128)(2,1)S(1)} %pad_maximum_fusion.1) | copy-start | bytes 1572868
  55.0 1.0 copy-start.3
  56.0 8.1 %copy-start.11 = (s32[1,512]{1,0:T(1,128)S(1)}, s32[1,512]{1,0:T(1,128)}, u32[]{:S(2)}) copy-start(s32[1,512]{1,0:T(1,128)} %param.19) | copy-start | bytes 6148
  56.0 8.6 %copy-start.12 = (f32[128]{0:T(128)S(1)}, f32[128]{0:T(128)}, u32[]{:S(2)}) copy-start(f32[128]{0:T(128)} %param.21) | copy-start | bytes 1540
  56.0 7.8 %collective-permute-start.1 = (f32[128,512]{1,0:T(8,128)S(1)}, f32[128,512]{1,0:T(8,128)S(1)}, u32[]{:S(2)}, u32[]{:S(2)}) collective-permute-start(f32[128,512]{1,0:T(8,128)S(1)} %dynamic-slice_bitcast_fusion), channel_id=1, source_target_pairs={{0,1},{1,0},{2,3},{3,2},{4,5},{5,4},{6,7},{7,6},{8,9},{9,8},{10,11... | collective-permute-start | bytes 786440 | tf_op jit(solution)/shard_map/ppermute | solution.py:19
  63.8 63.9 %all-gather.7.cloned.1.call-start = ((), (), s32[]{:S(2)}) async-start(), calls=%async_computation.8 | async-start | bytes 2621440 | tf_op jit(solution)/shard_map/all_gather | solution.py:267
  66.1 24.1 %all-to-all-start.2 = ((bf16[128,2,640]{2,1,0:T(2,128)(2,1)}), bf16[128,2,640]{2,1,0:T(2,128)(2,1)S(1)}, u32[]{:S(2)}, u32[]{:S(2)}) async-start(bf16[128,2,640]{2,1,0:T(2,128)(2,1)} %reshape.178), calls=%async_computation.2 | async-start | bytes 655360 | tf_op jit(solution)/shard_map/all_to_all | solution.py:272
  92.6 20.8 %all-to-all-start.3 = ((bf16[128,8,128]{2,1,0:T(8,128)(2,1)}), bf16[128,8,128]{2,1,0:T(8,128)(2,1)S(1)}, u32[]{:S(2)}, u32[]{:S(2)}) async-start(bf16[128,8,128]{2,1,0:T(8,128)(2,1)} %bitcast.22), calls=%async_computation.3 | async-start | bytes 524288 | tf_op jit(solution)/shard_map/all_to_all | solution.py:28
  113.5 1.6 copy-start.1
  117.2 10.5 %all-to-all-start.4 = ((bf16[8,144,128]{2,1,0:T(8,128)(2,1)}), bf16[8,144,128]{2,1,0:T(8,128)(2,1)S(1)}, u32[]{:S(2)}, u32[]{:S(2)}) async-start(bf16[8,144,128]{2,1,0:T(8,128)(2,1)} %get-tuple-element.24), calls=%async_computation.4 | async-start | bytes 589824 | tf_op jit(solution)/shard_map/all_to_all | solution.py:28
  127.7 1.6 copy-start.2
  130.8 19.4 %all-to-all-start.5 = ((bf16[64,24,128]{2,1,0:T(8,128)(2,1)}), bf16[64,24,128]{2,1,0:T(8,128)(2,1)S(1)}, u32[]{:S(2)}, u32[]{:S(2)}) async-start(bf16[64,24,128]{2,1,0:T(8,128)(2,1)} %pad_maximum_fusion.2), calls=%async_computation.5 | async-start | bytes 786432 | tf_op jit(solution)/shard_map/all_to_all | solution.py:28
  150.9 11.8 %all-to-all-start.6 = ((f32[8,24,128]{2,1,0:T(8,128)}), f32[8,24,128]{2,1,0:T(8,128)S(1)}, u32[]{:S(2)}, u32[]{:S(2)}) async-start(f32[8,24,128]{2,1,0:T(8,128)} %shard_map.141), calls=%async_computation.6 | async-start | bytes 196608 | tf_op jit(solution)/shard_map/all_to_all | solution.py:28
Sparse Core Ops, SparseCore 0:
  64.0 12.8 all-gather.4
  79.6 36.0 all-gather.6

commit v8 on v7

--- a/solution.py
+++ b/solution.py
@@ -220,7 +220,9 @@
     block = embed_width // n_outer
     columns = lax.dynamic_slice_in_dim(head_weight, outer * block, block, 1)
     columns = gather(columns, ("z", "y")).reshape(half, block)
-    blocks = gather(columns, "outer")
+    cut = half * 5 // 8
+    upper = lax.all_gather(columns[cut:], "outer", axis=0)
+    blocks = jnp.concatenate([gather(columns[:cut], "outer"), upper], axis=1)
 
     widened = feats.astype(f32)
     means = jnp.mean(widened, axis=1, keepdims=True)

time: 172 us -> 184 us (1.070)
  blocking collectives: 0 us -> 14.7 us
  waiting for transfers between devices: 65.8 us -> 62.8 us
  other arithmetic: 11.1 us -> 13.2 us
  starting transfers between devices: 58.8 us -> 56.7 us
    all_gather x0 -> x1, blocking collectives: none -> 14.7 us  [body(): upper = lax.all_gather(columns[cut:], 'outer', axis=0)]
    all_to_all x6, starting transfers between devices: 41.7 us -> 35.5 us  [exchange(): return lax.all_to_all(pieces, axis, split_axis=0, concat_axis=0, tiled=True)]
    ppermute x2, starting transfers between devices: 9.5 us -> 15.1 us  [swap(): return lax.ppermute(value, axis, [(i, i ^ flip) for i in range(size)])]
    all_to_all x6, waiting for transfers between devices: 50 us -> 47.2 us  [exchange(): return lax.all_to_all(pieces, axis, split_axis=0, concat_axis=0, tiled=True)]
    unnamed x28 -> x24, local copies, waits for them, and re-layouts: 4.84 us -> 4.39 us
  transfers between devices with their start and end apart: 11 -> 11, of which waited for: 8 -> 7; matrix products, arithmetic and copies ran while one was open for 10% -> 9% of each run, Pallas kernels for 3% -> 2%
where the time goes in v8:
time: 184 us; the launch traced here: 183 us
  waiting for transfers between devices  62.8 us (34%)
  starting transfers between devices  56.7 us (31%)
  blocking collectives  14.7 us (8%)
  between operations  14.5 us (8%)
  other arithmetic  13.2 us (7%)
  local copies, waits for them, and re-layouts  11.9 us (6%)
  Pallas kernels  7.01 us (4%)
  matrix products  2.51 us (1%)
    all_to_all x6, waiting for transfers between devices, exchange(): return lax.all_to_all(pieces, axis, split_axis=0, concat_axis=0, tiled=True)  47.2 us
    all_to_all x6, starting transfers between devices, exchange(): return lax.all_to_all(pieces, axis, split_axis=0, concat_axis=0, tiled=True)  35.5 us
    ppermute x2, starting transfers between devices, swap(): return lax.ppermute(value, axis, [(i, i ^ flip) for i in range(size)])  15.1 us
    all_gather x1, blocking collectives, body(): upper = lax.all_gather(columns[cut:], 'outer', axis=0)  14.7 us
    all_to_all x1, waiting for transfers between devices, body(): lax.all_to_all(send_rows.reshape(dp_count, capacity, -1), DP, split_axis=...  14.1 us
    pallas_call x5, Pallas kernels, call(): pl.pallas_call(kernel, out_shape=out_shape, in_specs=places or [vmem] * l...  7.01 us
    all_to_all x1, starting transfers between devices, body(): lax.all_to_all(send_rows.reshape(dp_count, capacity, -1), DP, split_axis=...  6.07 us
    unnamed x24, local copies, waits for them, and re-layouts  4.39 us
  transfers between devices with their start and end apart: 11, of which 7 were waited for; matrix products, arithmetic and copies ran while one was open for 9% of the time, Pallas kernels for 2%

profile of v8, /device:TPU:1, one launch (start us, length us, event | category | flops | bytes accessed | tf_op | source)
XLA Modules:
  0.0 183.3 jit_solution(2571194635036613164)
XLA Ops:
  7.2 1.4 convert_reduce_fusion
  8.6 1.5 multiply_reduce_fusion
  10.1 1.2 copy-done.4
  11.3 0.2 fusion.8
  11.5 0.3 copy.33
  11.8 8.8 %collective-permute-start = (bf16[1024,128]{1,0:T(8,128)(2,1)S(1)}, bf16[1024,128]{1,0:T(8,128)(2,1)S(1)}, u32[]{:S(2)}, u32[]{:S(2)}) collective-permute-start(bf16[1024,128]{1,0:T(8,128)(2,1)S(1)} %bitcast.79), channel_id=1, source_target_pairs={{0,1},{1,0},{2,3},{3,2},{4,5},{5,4},{6,7},{7,6},{8,9},{9,8},{10,11... | collective-permute-start | bytes 786440 | tf_op jit(solution)/shard_map/ppermute | solution.py:19
  20.6 0.7 constant_dynamic-slice_fusion.2
  21.3 0.7 broadcast_in_dim.60
  22.1 10.9 %all-to-all-start = ((bf16[64,16,128]{2,1,0:T(8,128)(2,1)}), bf16[64,16,128]{2,1,0:T(8,128)(2,1)S(1)}, u32[]{:S(2)}, u32[]{:S(2)}) async-start(bf16[64,16,128]{2,1,0:T(8,128)(2,1)} %broadcast_in_dim.60), calls=%async_computation | async-start | bytes 524288 | tf_op jit(solution)/shard_map/all_to_all | solution.py:28
  33.2 0.2 convert_reduce_fusion.1
  33.8 12.9 %all-to-all-done = bf16[64,16,128]{2,1,0:T(8,128)(2,1)S(1)} async-done(((bf16[64,16,128]{2,1,0:T(8,128)(2,1)}), bf16[64,16,128]{2,1,0:T(8,128)(2,1)S(1)}, u32[]{:S(2)}, u32[]{:S(2)}) %all-to-all-start) | async-done | bytes 262176 | tf_op jit(solution)/shard_map/all_to_all | solution.py:28
  46.7 0.9 broadcast_in_dim.62
  47.6 4.0 %all-to-all-start.1 = ((bf16[4,640,128]{2,1,0:T(8,128)(2,1)}), bf16[4,640,128]{2,1,0:T(8,128)(2,1)S(1)}, u32[]{:S(2)}, u32[]{:S(2)}) async-start(bf16[4,640,128]{2,1,0:T(8,128)(2,1)} %broadcast_in_dim.62), calls=%async_computation.1 | async-start | bytes 1310720 | tf_op jit(solution)/shard_map/all_to_all | solution.py:28
  51.7 0.9 pad_maximum_fusion.2
  52.6 14.7 %all_gather.19 = bf16[4,384,128]{2,1,0:T(8,128)(2,1)} all-gather(bf16[1,384,128]{2,1,0:T(8,128)(2,1)S(1)} %bitcast.78), channel_id=1, replica_groups=mesh['outer'=4,'z'=8,'y'=8,'core'=2] {'outer'}, dimensions={0}, use_global_device_ids=true | all-gather | bytes 491520 | tf_op jit(solution)/shard_map/all_gather | solution.py:224
  67.3 1.1 pad_maximum_fusion
  68.4 1.8 fusion
  70.3 6.3 %collective-permute-start.1 = (f32[128,512]{1,0:T(8,128)S(1)}, f32[128,512]{1,0:T(8,128)S(1)}, u32[]{:S(2)}, u32[]{:S(2)}) collective-permute-start(f32[128,512]{1,0:T(8,128)S(1)} %dynamic-slice_bitcast_fusion), channel_id=1, source_target_pairs={{0,1},{1,0},{2,3},{3,2},{4,5},{5,4},{6,7},{7,6},{8,9},{9,8},{10,11... | collective-permute-start | bytes 786440 | tf_op jit(solution)/shard_map/ppermute | solution.py:19
  76.6 1.1 collective-permute-done.1
  78.2 0.4 all-gather.7.cloned.1.call-update
  79.0 0.2 convolution_convert_fusion.1
  79.2 0.8 reshape.183
  80.1 6.1 %all-to-all-start.2 = ((bf16[128,2,640]{2,1,0:T(2,128)(2,1)}), bf16[128,2,640]{2,1,0:T(2,128)(2,1)S(1)}, u32[]{:S(2)}, u32[]{:S(2)}) async-start(bf16[128,2,640]{2,1,0:T(2,128)(2,1)} %reshape.183), calls=%async_computation.2 | async-start | bytes 655360 | tf_op jit(solution)/shard_map/all_to_all | solution.py:274
  86.2 1.6 gather_fusion
  87.9 0.5 convolution_convert_fusion.ordered_ref
  88.6 14.1 %all-to-all-done.2 = bf16[128,2,640]{2,1,0:T(2,128)(2,1)S(1)} async-done(((bf16[128,2,640]{2,1,0:T(2,128)(2,1)}), bf16[128,2,640]{2,1,0:T(2,128)(2,1)S(1)}, u32[]{:S(2)}, u32[]{:S(2)}) %all-to-all-start.2) | async-done | bytes 327712 | tf_op jit(solution)/shard_map/all_to_all | solution.py:274
  102.9 2.3 %shard_map.138 = bf16[1024,128]{1,0:T(8,128)(2,1)} custom-call(bf16[256,640]{1,0:T(8,128)(2,1)S(1)} %reshape.184.rows_ref, bf16[512,512]{1,0:T(8,128)(2,1)S(1)} %convolution_convert_fusion.ordered_ref, f32[1,512]{1,0:T(1,128)S(1)} %bitcast.64), custom_call_target="tpu_custom_call" | custom-call | tf_op jit(solution)/shard_map/pallas_call | solution.py:62
  105.2 5.5 %all-to-all-start.3 = ((bf16[128,8,128]{2,1,0:T(8,128)(2,1)}), bf16[128,8,128]{2,1,0:T(8,128)(2,1)S(1)}, u32[]{:S(2)}, u32[]{:S(2)}) async-start(bf16[128,8,128]{2,1,0:T(8,128)(2,1)} %bitcast.23), calls=%async_computation.3 | async-start | bytes 524288 | tf_op jit(solution)/shard_map/all_to_all | solution.py:28
  110.7 1.7 fusion.28
  112.4 1.5 maximum_maximum_fusion
  113.9 12.2 %all-to-all-done.3 = bf16[128,8,128]{2,1,0:T(8,128)(2,1)S(1)} async-done(((bf16[128,8,128]{2,1,0:T(8,128)(2,1)}), bf16[128,8,128]{2,1,0:T(8,128)(2,1)S(1)}, u32[]{:S(2)}, u32[]{:S(2)}) %all-to-all-start.3) | async-done | bytes 262176 | tf_op jit(solution)/shard_map/all_to_all | solution.py:28
  126.0 1.6 copy-done.1
  127.6 2.1 %shard_map.139 = (bf16[8,144,128]{2,1,0:T(8,128)(2,1)}, f32[128,2048]{1,0:T(8,128)S(1)}) custom-call(bf16[1024,128]{1,0:T(8,128)(2,1)S(1)} %bitcast.63, s32[128,1]{1,0:T(8,128)S(1)} %copy.35.slots_ref, f32[128,512]{1,0:T(8,128)S(1)} %get-tuple-element.35.unit_ref, f32[128,1]{1,0:T(8,128)S(1)} %copy.36.norm_ref, f32[128,1]{1,0:T(8,128)S(1)} %copy.37.cot_ref, ...), custom_call_target="tpu_custom_call" | custom-call | tf_op jit(solution)/shard_map/pallas_call | solution.py:62
  129.7 3.7 %all-to-all-start.4 = ((bf16[8,144,128]{2,1,0:T(8,128)(2,1)}), bf16[8,144,128]{2,1,0:T(8,128)(2,1)S(1)}, u32[]{:S(2)}, u32[]{:S(2)}) async-start(bf16[8,144,128]{2,1,0:T(8,128)(2,1)} %get-tuple-element.24), calls=%async_computation.4 | async-start | bytes 589824 | tf_op jit(solution)/shard_map/all_to_all | solution.py:28
  133.4 0.2 multiply_reduce_fusion.2
  133.7 6.6 %all-to-all-done.4.pieces_ref = bf16[8,144,128]{2,1,0:T(8,128)(2,1)S(1)} async-done(((bf16[8,144,128]{2,1,0:T(8,128)(2,1)}), bf16[8,144,128]{2,1,0:T(8,128)(2,1)S(1)}, u32[]{:S(2)}, u32[]{:S(2)}) %all-to-all-start.4) | async-done | bytes 294944 | tf_op jit(solution)/shard_map/all_to_all | solution.py:28
  140.3 1.6 copy-done.2
  141.9 0.7 shard_map.140
  142.6 0.8 pad_maximum_fusion.3
  143.4 4.6 %all-to-all-start.5 = ((bf16[64,24,128]{2,1,0:T(8,128)(2,1)}), bf16[64,24,128]{2,1,0:T(8,128)(2,1)S(1)}, u32[]{:S(2)}, u32[]{:S(2)}) async-start(bf16[64,24,128]{2,1,0:T(8,128)(2,1)} %pad_maximum_fusion.3), calls=%async_computation.5 | async-start | bytes 786432 | tf_op jit(solution)/shard_map/all_to_all | solution.py:28
  148.1 1.2 fusion.12
  149.3 1.1 multiply_convert_fusion
  150.3 12.5 %all-to-all-done.5.pieces_ref = bf16[64,24,128]{2,1,0:T(8,128)(2,1)S(1)} async-done(((bf16[64,24,128]{2,1,0:T(8,128)(2,1)}), bf16[64,24,128]{2,1,0:T(8,128)(2,1)S(1)}, u32[]{:S(2)}, u32[]{:S(2)}) %all-to-all-start.5) | async-done | bytes 393248 | tf_op jit(solution)/shard_map/all_to_all | solution.py:28
  162.8 0.7 shard_map.141
  163.6 6.7 %all-to-all-start.6 = ((f32[8,24,128]{2,1,0:T(8,128)}), f32[8,24,128]{2,1,0:T(8,128)S(1)}, u32[]{:S(2)}, u32[]{:S(2)}) async-start(f32[8,24,128]{2,1,0:T(8,128)} %shard_map.141), calls=%async_computation.6 | async-start | bytes 196608 | tf_op jit(solution)/shard_map/all_to_all | solution.py:28
  170.3 2.0 %pad_maximum_fusion.1 = bf16[128,3072]{1,0:T(8,128)(2,1)} fusion(bf16[128,1024]{1,0:T(8,128)(2,1)S(1)} %fusion.12, bf16[128,2048]{1,0:T(8,128)(2,1)} %multiply_convert_fusion), kind=kLoop, calls=%fused_computation.24 | loop fusion | flops 1572864 | bytes 1572864 | tf_op jit(solution)/shard_map/concatenate | solution.py:337
  172.3 3.0 %all-to-all-done.6.last_ref = f32[8,24,128]{2,1,0:T(8,128)S(1)} async-done(((f32[8,24,128]{2,1,0:T(8,128)}), f32[8,24,128]{2,1,0:T(8,128)S(1)}, u32[]{:S(2)}, u32[]{:S(2)}) %all-to-all-start.6) | async-done | bytes 98336 | tf_op jit(solution)/shard_map/all_to_all | solution.py:28
  175.3 1.2 shard_map.142
  (64 shorter events, 2.2 us)
Async XLA Ops:
  7.2 80.7 %copy-start = (bf16[512,512]{1,0:T(8,128)(2,1)S(1)}, bf16[512,512]{1,0:T(8,128)(2,1)}, u32[]{:S(2)}) copy-start(bf16[512,512]{1,0:T(8,128)(2,1)} %param.15) | copy-start | bytes 1572868
  7.2 4.1 %copy-start.5 = (f32[2048]{0:T(1024)S(1)}, f32[2048]{0:T(1024)}, u32[]{:S(2)}) copy-start(f32[2048]{0:T(1024)} %param.12) | copy-start | bytes 24580
  7.2 4.1 %copy-start.7 = (f32[2048]{0:T(1024)S(1)}, f32[2048]{0:T(1024)}, u32[]{:S(2)}) copy-start(f32[2048]{0:T(1024)} %param.13) | copy-start | bytes 24580
  10.1 1.2 copy-start.4
  11.5 21.5 %copy-start.6 = (s32[1,512]{1,0:T(1,128)S(1)}, s32[1,512]{1,0:T(1,128)}, u32[]{:S(2)}) copy-start(s32[1,512]{1,0:T(1,128)} %param.18) | copy-start | bytes 6148
  11.5 21.5 %copy-start.8 = (s32[128]{0:T(128)S(1)}, s32[128]{0:T(128)}, u32[]{:S(2)}) copy-start(s32[128]{0:T(128)} %param.16) | copy-start | bytes 1540
  11.5 22.1 %copy-start.11 = (s32[128]{0:T(128)S(1)}, s32[128]{0:T(128)}, u32[]{:S(2)}) copy-start(s32[128]{0:T(128)} %param.17) | copy-start | bytes 1540
  11.8 39.8 %collective-permute-start = (bf16[1024,128]{1,0:T(8,128)(2,1)S(1)}, bf16[1024,128]{1,0:T(8,128)(2,1)S(1)}, u32[]{:S(2)}, u32[]{:S(2)}) collective-permute-start(bf16[1024,128]{1,0:T(8,128)(2,1)S(1)} %bitcast.79), channel_id=1, source_target_pairs={{0,1},{1,0},{2,3},{3,2},{4,5},{5,4},{6,7},{7,6},{8,9},{9,8},{10,11... | collective-permute-start | bytes 786440 | tf_op jit(solution)/shard_map/ppermute | solution.py:19
  22.1 24.6 %all-to-all-start = ((bf16[64,16,128]{2,1,0:T(8,128)(2,1)}), bf16[64,16,128]{2,1,0:T(8,128)(2,1)S(1)}, u32[]{:S(2)}, u32[]{:S(2)}) async-start(bf16[64,16,128]{2,1,0:T(8,128)(2,1)} %broadcast_in_dim.60), calls=%async_computation | async-start | bytes 524288 | tf_op jit(solution)/shard_map/all_to_all | solution.py:28
  47.6 19.7 %all-to-all-start.1 = ((bf16[4,640,128]{2,1,0:T(8,128)(2,1)}), bf16[4,640,128]{2,1,0:T(8,128)(2,1)S(1)}, u32[]{:S(2)}, u32[]{:S(2)}) async-start(bf16[4,640,128]{2,1,0:T(8,128)(2,1)} %broadcast_in_dim.62), calls=%async_computation.1 | async-start | bytes 1310720 | tf_op jit(solution)/shard_map/all_to_all | solution.py:28
  51.6 59.1 %all-gather.5.cloned.1.call-start = ((), (), s32[]{:S(2)}) async-start(), calls=%async_computation.7 | async-start | bytes 3145728 | tf_op jit(solution)/shard_map/all_gather | solution.py:268
  68.3 1.9 %copy-start.3 = (bf16[4,1024,128]{2,1,0:T(8,128)(2,1)}, bf16[4,1024,128]{2,1,0:T(8,128)(2,1)S(1)}, u32[]{:S(2)}) copy-start(bf16[4,1024,128]{2,1,0:T(8,128)(2,1)S(1)} %pad_maximum_fusion) | copy-start | bytes 3145732
  70.2 7.8 %copy-start.9 = (s32[1,512]{1,0:T(1,128)S(1)}, s32[1,512]{1,0:T(1,128)}, u32[]{:S(2)}) copy-start(s32[1,512]{1,0:T(1,128)} %param.19) | copy-start | bytes 6148
  70.2 8.4 %copy-start.10 = (f32[128]{0:T(128)S(1)}, f32[128]{0:T(128)}, u32[]{:S(2)}) copy-start(f32[128]{0:T(128)} %param.21) | copy-start | bytes 1540
  70.3 7.5 %collective-permute-start.1 = (f32[128,512]{1,0:T(8,128)S(1)}, f32[128,512]{1,0:T(8,128)S(1)}, u32[]{:S(2)}, u32[]{:S(2)}) collective-permute-start(f32[128,512]{1,0:T(8,128)S(1)} %dynamic-slice_bitcast_fusion), channel_id=1, source_target_pairs={{0,1},{1,0},{2,3},{3,2},{4,5},{5,4},{6,7},{7,6},{8,9},{9,8},{10,11... | collective-permute-start | bytes 786440 | tf_op jit(solution)/shard_map/ppermute | solution.py:19
  77.8 62.5 %all-gather.7.cloned.1.call-start = ((), (), s32[]{:S(2)}) async-start(), calls=%async_computation.8 | async-start | bytes 2621440 | tf_op jit(solution)/shard_map/all_gather | solution.py:269
  80.1 22.7 %all-to-all-start.2 = ((bf16[128,2,640]{2,1,0:T(2,128)(2,1)}), bf16[128,2,640]{2,1,0:T(2,128)(2,1)S(1)}, u32[]{:S(2)}, u32[]{:S(2)}) async-start(bf16[128,2,640]{2,1,0:T(2,128)(2,1)} %reshape.183), calls=%async_computation.2 | async-start | bytes 655360 | tf_op jit(solution)/shard_map/all_to_all | solution.py:274
  105.2 20.8 %all-to-all-start.3 = ((bf16[128,8,128]{2,1,0:T(8,128)(2,1)}), bf16[128,8,128]{2,1,0:T(8,128)(2,1)S(1)}, u32[]{:S(2)}, u32[]{:S(2)}) async-start(bf16[128,8,128]{2,1,0:T(8,128)(2,1)} %bitcast.23), calls=%async_computation.3 | async-start | bytes 524288 | tf_op jit(solution)/shard_map/all_to_all | solution.py:28
  126.0 1.6 copy-start.1
  129.7 10.5 %all-to-all-start.4 = ((bf16[8,144,128]{2,1,0:T(8,128)(2,1)}), bf16[8,144,128]{2,1,0:T(8,128)(2,1)S(1)}, u32[]{:S(2)}, u32[]{:S(2)}) async-start(bf16[8,144,128]{2,1,0:T(8,128)(2,1)} %get-tuple-element.24), calls=%async_computation.4 | async-start | bytes 589824 | tf_op jit(solution)/shard_map/all_to_all | solution.py:28
  140.3 1.6 copy-start.2
  143.4 19.4 %all-to-all-start.5 = ((bf16[64,24,128]{2,1,0:T(8,128)(2,1)}), bf16[64,24,128]{2,1,0:T(8,128)(2,1)S(1)}, u32[]{:S(2)}, u32[]{:S(2)}) async-start(bf16[64,24,128]{2,1,0:T(8,128)(2,1)} %pad_maximum_fusion.3), calls=%async_computation.5 | async-start | bytes 786432 | tf_op jit(solution)/shard_map/all_to_all | solution.py:28
  163.6 11.8 %all-to-all-start.6 = ((f32[8,24,128]{2,1,0:T(8,128)}), f32[8,24,128]{2,1,0:T(8,128)S(1)}, u32[]{:S(2)}, u32[]{:S(2)}) async-start(f32[8,24,128]{2,1,0:T(8,128)} %shard_map.141), calls=%async_computation.6 | async-start | bytes 196608 | tf_op jit(solution)/shard_map/all_to_all | solution.py:28
Sparse Core Ops, SparseCore 0:
  78.0 11.7 all-gather.4
  91.9 36.0 all-gather.6
